TPU v7x, 32 devices: a whole 2x2x4 slice. The times are simulated.
32 devices in a mesh: dp: 8 (over z, x), tensor: 4 (over y, core).
Axes of the slice: x: 2, y: 2, z: 4, core: 2. Of those that a mesh axis runs over, the one named last changes fastest.
Arguments:
- tokens: bfloat16 [8192, 768], P('dp'), may hold values from -6 to 6
- cotangent: bfloat16 [8192, 768], P('dp'), may hold values from -6 to 6
- clip_lengths: int32 [16, 8], P('dp'), may hold values from 0 to 496, as said below
- key_mask: int32 [8192], P('dp'), may hold values 0 or 1
- rel_buckets: int32 [1023], replicated, may hold values from 0 to 319
- attention_weights: float32 [4, 768, 768], P(None, 'dp', 'tensor'), may hold values from -0.8660254 to 0.8660254
- attention_first: float32 [4, 768, 768], P(None, 'dp', 'tensor'), may hold values from -7.6293945e-05 to 7.6293945e-05
- attention_second: float32 [4, 768, 768], P(None, 'dp', 'tensor'), may hold values from 2.8822156e-11 to 1.15288626e-10
- feedforward_weights: float32 [2, 768, 3072], P(None, 'dp', 'tensor'), may hold values from -0.21875 to 0.21875
- feedforward_first: float32 [2, 768, 3072], P(None, 'dp', 'tensor'), may hold values from -7.6293945e-05 to 7.6293945e-05
- feedforward_second: float32 [2, 768, 3072], P(None, 'dp', 'tensor'), may hold values from 2.8822156e-11 to 1.15288626e-10
- small_params: float32 [13198], replicated, may hold values from -2.8 to 2.8, as said below
- small_first: float32 [13198], replicated, may hold values from -9.1552734e-05 to 9.1552734e-05
- small_second: float32 [13198], replicated, may hold values from 6.499114e-11 to 2.5996455e-10
Outputs:
- global_norm: float32 [], replicated
- attention_moment: float32 [4, 768, 768], P(None, 'dp', 'tensor')
- attention_square: float32 [4, 768, 768], P(None, 'dp', 'tensor')
- attention_master: float32 [4, 768, 768], P(None, 'dp', 'tensor')
- attention_copy: bfloat16 [4, 768, 768], P(None, 'dp', 'tensor')
- feedforward_moment: float32 [2, 768, 3072], P(None, 'dp', 'tensor')
- feedforward_square: float32 [2, 768, 3072], P(None, 'dp', 'tensor')
- feedforward_master: float32 [2, 768, 3072], P(None, 'dp', 'tensor')
- feedforward_copy: bfloat16 [2, 768, 3072], P(None, 'dp', 'tensor')
- small_moment: float32 [13198], replicated
- small_square: float32 [13198], replicated
- small_master: float32 [13198], replicated
- block_output: bfloat16 [8192, 768], P('dp')
- tokens_grad: bfloat16 [8192, 768], P('dp')
Inputs may be any that keep to these rules, and one draw needn't show every extreme that they name: `clip_lengths`: each row sums to at most 512; a row holds either one clip of 496 patches with one short remainder or up to five clips of at most 96; every draw has a clip of 496. `small_params`: norm gains are positive.
All inputs are finite; a program needn't handle non-finite values. No bound on the sum of `key_mask` on one device may be relied on, other than what follows from the above.
Results may differ from a plain program's by a relative error of at most 0.011.
Values may be sent and summed in bfloat16 or wider, within the bound.
A program may use at most 128 MiB of HBM per device.

v0:
```python
from functools import partial

import jax
import jax.numpy as jnp
from jax import lax
from jax.sharding import PartitionSpec as P

MODEL_WIDTH = 768
H = 12
HD = 64
FF = 3072
NB = 320
BUCKET_SLOTS = 512
CLIPS = 8
STEP = 5


FULL_PRECISION = lax.Precision.HIGHEST
DEEP_ALPHA = 24.0**0.25
NORM_EPSILON = 1e-05
MASK_VALUE = -1e30
BETA_FIRST = 0.9
BETA_SECOND = 0.98
RATE_MATRIX = 0.03
RATE_SMALL = 0.5
WEIGHT_DECAY = 0.01
ADAM_EPSILON = 1e-08
CLIP_LIMIT = 0.1


def layer_norm(values, norm_gain, norm_shift):
    row_mean = jnp.mean(values, axis=-1, keepdims=True)
    centred = values - row_mean
    variance = jnp.mean(centred * centred, axis=-1, keepdims=True)
    return centred * lax.rsqrt(variance + NORM_EPSILON) * norm_gain + norm_shift


def gelu_exact(values):
    return jax.nn.gelu(values, approximate=False)


def split_small(vector):
    widths = [MODEL_WIDTH] * 8 + [FF, NB * H, HD * 2, 2, H]
    pieces = []
    offset = 0
    for extent in widths:
        pieces.append(vector[offset : offset + extent])
        offset += extent
    return pieces


def allowed_mask(lengths_row, keep_row):
    positions = jnp.arange(BUCKET_SLOTS, dtype=jnp.int32)
    clip_ends = jnp.cumsum(lengths_row)
    segment = jnp.sum((positions[:, None] >= clip_ends[None, :]).astype(jnp.int32), axis=1)
    live_keys = (keep_row == 1) & (segment < CLIPS)
    same_clip = segment[:, None] == segment[None, :]
    return same_clip & (live_keys[None, :] | (positions[:, None] == positions[None, :]))


def band_matrix(diagonals):
    head_count = diagonals.shape[0]
    length = (diagonals.shape[1] + 1) // 2
    padded = jnp.concatenate([diagonals, jnp.zeros((head_count, 1), diagonals.dtype)], axis=1)
    repeated = jnp.tile(padded, (1, length))
    folded = repeated[:, : length * (2 * length - 1)].reshape(head_count, length, 2 * length - 1)
    return folded[:, :, length - 1 :]


def position_terms(head_inputs, gate_matrix, gate_offset, scale_local, table_local, rel_buckets):
    linear = (
        jnp.einsum(
            "blhd,dk->bhlk", head_inputs, gate_matrix.reshape(HD, 2), precision=FULL_PRECISION
        )
        + gate_offset
    )
    sigmoid = jax.nn.sigmoid(linear)
    gate = sigmoid[..., 0] * (sigmoid[..., 1] * scale_local[None, :, None] - 1.0) + 2.0
    onehot = (rel_buckets[:, None] == jnp.arange(NB, dtype=jnp.int32)[None, :]).astype(jnp.float32)
    per_offset = jnp.dot(
        onehot, table_local, precision=FULL_PRECISION, preferred_element_type=jnp.float32
    )
    toeplitz = band_matrix(per_offset.T)
    return gate[..., None] * toeplitz[None]


def adam_step(weights, moment, second, gradient, step_rate, decay_rate):
    moment_new = BETA_FIRST * moment + (1.0 - BETA_FIRST) * gradient
    second_new = BETA_SECOND * second + (1.0 - BETA_SECOND) * gradient * gradient
    moment_hat = moment_new / (1.0 - BETA_FIRST**STEP)
    second_hat = second_new / (1.0 - BETA_SECOND**STEP)
    master = weights - step_rate * (
        moment_hat / (jnp.sqrt(second_hat) + ADAM_EPSILON) + decay_rate * weights
    )
    return (moment_new, second_new, master)


def placed(total_length, piece, start):
    return lax.dynamic_update_slice_in_dim(jnp.zeros((total_length,), jnp.float32), piece, start, 0)


def column_sum(values):
    return jnp.sum(values.astype(jnp.float32), axis=0)


def body(
    tokens,
    cotangent,
    clip_lengths,
    key_mask,
    rel_buckets,
    attention_weights,
    attention_first,
    attention_second,
    feedforward_weights,
    feedforward_first,
    feedforward_second,
    small_params,
    small_first,
    small_second,
):
    gathered_attention, gathered_forward = (
        lax.all_gather(attention_weights.astype(jnp.bfloat16), "dp", axis=1, tiled=True),
        lax.all_gather(feedforward_weights.astype(jnp.bfloat16), "dp", axis=1, tiled=True),
    )
    query_weight = gathered_attention[0]
    key_weight = gathered_attention[1]
    value_weight = gathered_attention[2]
    output_weight = gathered_attention[3]
    up_weight = gathered_forward[0]
    down_weight = gathered_forward[1]
    head_cols = query_weight.shape[1]
    heads_local = head_cols // HD
    hidden_local = up_weight.shape[1]
    tensor_rank = lax.axis_index("tensor")
    col_start = tensor_rank * head_cols
    head_start = tensor_rank * heads_local
    hidden_start = tensor_rank * hidden_local
    row_count = tokens.shape[0]
    bucket_count = row_count // BUCKET_SLOTS
    (
        gain_one,
        shift_one,
        gain_two,
        shift_two,
        bias_query,
        bias_value,
        bias_output,
        bias_down,
        bias_up,
        rel_table,
        gate_matrix,
        gate_offset,
        gate_scale,
    ) = split_small(small_params)
    local_bias_query = lax.dynamic_slice_in_dim(bias_query, col_start, head_cols)
    local_bias_value = lax.dynamic_slice_in_dim(bias_value, col_start, head_cols)
    local_bias_up = lax.dynamic_slice_in_dim(bias_up, hidden_start, hidden_local)
    scale_local = lax.dynamic_slice_in_dim(gate_scale, head_start, heads_local)
    table_local = lax.dynamic_slice_in_dim(rel_table.reshape(NB, H), head_start, heads_local, 1)
    allowed = jax.vmap(allowed_mask)(clip_lengths, key_mask.reshape(bucket_count, BUCKET_SLOTS))[
        :, None
    ]
    leading = (tensor_rank == 0).astype(jnp.float32)
    inputs = tokens.astype(jnp.float32)
    upstream = cotangent.astype(jnp.float32)
    query_bf = (
        jnp.dot(tokens, query_weight, preferred_element_type=jnp.float32) + local_bias_query
    ).astype(jnp.bfloat16)
    key_bf = jnp.dot(tokens, key_weight, preferred_element_type=jnp.float32).astype(jnp.bfloat16)
    value_bf = (
        jnp.dot(tokens, value_weight, preferred_element_type=jnp.float32) + local_bias_value
    ).astype(jnp.bfloat16)
    head_shape = (bucket_count, BUCKET_SLOTS, heads_local, HD)
    heads_of_query = query_bf.reshape(head_shape)
    heads_of_key = key_bf.reshape(head_shape)
    heads_of_value = value_bf.reshape(head_shape)
    head_inputs = lax.dynamic_slice_in_dim(inputs, col_start, head_cols, 1).reshape(head_shape)
    extra, pull_position = jax.vjp(
        partial(position_terms, rel_buckets=rel_buckets),
        head_inputs,
        gate_matrix,
        gate_offset,
        scale_local,
        table_local,
    )
    attention_logits = (
        jnp.einsum(
            "blhd,bmhd->bhlm", heads_of_query, heads_of_key, preferred_element_type=jnp.float32
        )
        * 0.125
    )
    scores = jnp.where(allowed, attention_logits + extra, MASK_VALUE)
    row_max = jnp.max(scores, axis=-1, keepdims=True)
    exponent = jnp.exp(scores - row_max)
    denominator = jnp.sum(exponent, axis=-1, keepdims=True)
    log_total = row_max + jnp.log(denominator)
    probs_bf = (exponent / denominator).astype(jnp.bfloat16)
    context_bf = (
        jnp.einsum("bhlm,bmhd->blhd", probs_bf, heads_of_value, preferred_element_type=jnp.float32)
        .reshape(row_count, head_cols)
        .astype(jnp.bfloat16)
    )
    attention_part = jnp.einsum(
        "nw,dw->nd", context_bf, output_weight, preferred_element_type=jnp.float32
    )
    attention = lax.psum(attention_part, "tensor") + bias_output
    normed, pull_norm_one = jax.vjp(
        layer_norm, DEEP_ALPHA * inputs + attention, gain_one, shift_one
    )
    normed_bf = normed.astype(jnp.bfloat16)
    up_pre = jnp.dot(normed_bf, up_weight, preferred_element_type=jnp.float32) + local_bias_up
    activated, pull_gelu = jax.vjp(gelu_exact, up_pre)
    activated_bf = activated.astype(jnp.bfloat16)
    down_part = jnp.einsum(
        "nf,df->nd", activated_bf, down_weight, preferred_element_type=jnp.float32
    )
    feedforward = lax.psum(down_part, "tensor") + bias_down
    output_values, pull_norm_two = jax.vjp(
        layer_norm, DEEP_ALPHA * normed + feedforward, gain_two, shift_two
    )
    block_output = output_values.astype(jnp.bfloat16)
    grad_res_two, grad_gain_two, grad_shift_two = pull_norm_two(upstream)
    grad_ffn_share = grad_res_two.astype(jnp.bfloat16)
    grad_bias_down = column_sum(grad_ffn_share)
    down_grad = jnp.einsum(
        "nd,nf->df", grad_ffn_share, activated_bf, preferred_element_type=jnp.float32
    )
    grad_activated = jnp.einsum(
        "nd,df->nf", grad_ffn_share, down_weight, preferred_element_type=jnp.float32
    )
    (grad_up_pre,) = pull_gelu(grad_activated)
    grad_up_bf = grad_up_pre.astype(jnp.bfloat16)
    grad_bias_up = column_sum(grad_up_bf)
    up_grad = jnp.einsum("nd,nf->df", normed_bf, grad_up_bf, preferred_element_type=jnp.float32)
    normed_part = jnp.einsum("nf,df->nd", grad_up_bf, up_weight, preferred_element_type=jnp.float32)
    normed_sum = lax.psum(normed_part, "tensor")
    grad_normed = normed_sum + DEEP_ALPHA * grad_res_two
    grad_res_one, grad_gain_one, grad_shift_one = pull_norm_one(grad_normed)
    grad_attention_share = grad_res_one.astype(jnp.bfloat16)
    grad_bias_output = column_sum(grad_attention_share)
    output_grad = jnp.einsum(
        "nd,nw->dw", grad_attention_share, context_bf, preferred_element_type=jnp.float32
    )
    grad_context_bf = jnp.einsum(
        "nd,dw->nw", grad_attention_share, output_weight, preferred_element_type=jnp.float32
    ).astype(jnp.bfloat16)
    grad_heads = grad_context_bf.reshape(head_shape)
    attention_probabilities = jnp.exp(scores - log_total)
    recomputed_bf = attention_probabilities.astype(jnp.bfloat16)
    grad_probs = jnp.einsum(
        "blhd,bmhd->bhlm", grad_heads, heads_of_value, preferred_element_type=jnp.float32
    )
    inner = jnp.sum(grad_probs * attention_probabilities, axis=-1, keepdims=True)
    grad_scores_bf = (attention_probabilities * (grad_probs - inner)).astype(jnp.bfloat16)
    grad_query = (
        (
            jnp.einsum(
                "bhlm,bmhd->blhd", grad_scores_bf, heads_of_key, preferred_element_type=jnp.float32
            )
            * 0.125
        )
        .astype(jnp.bfloat16)
        .reshape(row_count, head_cols)
    )
    grad_key = (
        (
            jnp.einsum(
                "bhlm,blhd->bmhd",
                grad_scores_bf,
                heads_of_query,
                preferred_element_type=jnp.float32,
            )
            * 0.125
        )
        .astype(jnp.bfloat16)
        .reshape(row_count, head_cols)
    )
    grad_value = (
        jnp.einsum("bhlm,blhd->bmhd", recomputed_bf, grad_heads, preferred_element_type=jnp.float32)
        .astype(jnp.bfloat16)
        .reshape(row_count, head_cols)
    )
    grad_head_inputs, grad_gate_matrix, grad_gate_offset, grad_scale_local, grad_table_local = (
        pull_position(grad_scores_bf.astype(jnp.float32))
    )
    query_grad = jnp.einsum("nd,nw->dw", tokens, grad_query, preferred_element_type=jnp.float32)
    key_grad = jnp.einsum("nd,nw->dw", tokens, grad_key, preferred_element_type=jnp.float32)
    value_grad = jnp.einsum("nd,nw->dw", tokens, grad_value, preferred_element_type=jnp.float32)
    input_part = (
        jnp.einsum("nw,dw->nd", grad_query, query_weight, preferred_element_type=jnp.float32)
        + jnp.einsum("nw,dw->nd", grad_key, key_weight, preferred_element_type=jnp.float32)
        + jnp.einsum("nw,dw->nd", grad_value, value_weight, preferred_element_type=jnp.float32)
    )
    own_columns = lax.dynamic_slice_in_dim(input_part, col_start, head_cols, 1)
    input_part = lax.dynamic_update_slice_in_dim(
        input_part, own_columns + grad_head_inputs.reshape(row_count, head_cols), col_start, 1
    )
    grad_inputs = lax.psum(input_part, "tensor") + DEEP_ALPHA * grad_res_one
    tokens_grad = grad_inputs.astype(jnp.bfloat16)
    table_grad = lax.dynamic_update_slice_in_dim(
        jnp.zeros((NB, H), jnp.float32), grad_table_local, head_start, 1
    ).reshape(-1)
    local_small = jnp.concatenate(
        [
            grad_gain_one * leading,
            grad_shift_one * leading,
            grad_gain_two * leading,
            grad_shift_two * leading,
            placed(MODEL_WIDTH, column_sum(grad_query), col_start),
            placed(MODEL_WIDTH, column_sum(grad_value), col_start),
            grad_bias_output * leading,
            grad_bias_down * leading,
            placed(FF, grad_bias_up, hidden_start),
            table_grad,
            grad_gate_matrix,
            grad_gate_offset,
            placed(H, grad_scale_local, head_start),
        ]
    )
    small_grad = lax.psum(local_small, ("dp", "tensor"))
    local_attention = jnp.stack([query_grad, key_grad, value_grad, output_grad])
    local_forward = jnp.stack([up_grad, down_grad])
    summed_attention, summed_forward = lax.psum((local_attention, local_forward), "dp")
    owner_rank = lax.axis_index("dp")
    owned_rows = attention_weights.shape[1]
    share_attention = lax.dynamic_slice_in_dim(
        summed_attention, owner_rank * owned_rows, owned_rows, 1
    )
    share_forward = lax.dynamic_slice_in_dim(summed_forward, owner_rank * owned_rows, owned_rows, 1)
    share_squares = jnp.sum(share_attention * share_attention) + jnp.sum(
        share_forward * share_forward
    )
    big_squares = lax.psum(share_squares, ("dp", "tensor"))
    global_norm = jnp.sqrt(big_squares + jnp.sum(small_grad * small_grad))
    factor = CLIP_LIMIT / jnp.maximum(global_norm, CLIP_LIMIT)
    attention_moment, attention_square, attention_master = adam_step(
        attention_weights,
        attention_first,
        attention_second,
        factor * share_attention,
        RATE_MATRIX,
        WEIGHT_DECAY,
    )
    feedforward_moment, feedforward_square, feedforward_master = adam_step(
        feedforward_weights,
        feedforward_first,
        feedforward_second,
        factor * share_forward,
        RATE_MATRIX,
        WEIGHT_DECAY,
    )
    small_moment, small_square, small_master = adam_step(
        small_params, small_first, small_second, factor * small_grad, RATE_SMALL, 0.0
    )
    return (
        global_norm,
        attention_moment,
        attention_square,
        attention_master,
        attention_master.astype(jnp.bfloat16),
        feedforward_moment,
        feedforward_square,
        feedforward_master,
        feedforward_master.astype(jnp.bfloat16),
        small_moment,
        small_square,
        small_master,
        block_output,
        tokens_grad,
    )


def solution(mesh):
    in_specs = (
        P("dp", None),
        P("dp", None),
        P("dp", None),
        P("dp"),
        P(),
        P(None, "dp", "tensor"),
        P(None, "dp", "tensor"),
        P(None, "dp", "tensor"),
        P(None, "dp", "tensor"),
        P(None, "dp", "tensor"),
        P(None, "dp", "tensor"),
        P(),
        P(),
        P(),
    )
    out_specs = (
        P(),
        P(None, "dp", "tensor"),
        P(None, "dp", "tensor"),
        P(None, "dp", "tensor"),
        P(None, "dp", "tensor"),
        P(None, "dp", "tensor"),
        P(None, "dp", "tensor"),
        P(None, "dp", "tensor"),
        P(None, "dp", "tensor"),
        P(),
        P(),
        P(),
        P("dp", None),
        P("dp", None),
    )
    return jax.shard_map(body, mesh=mesh, in_specs=in_specs, out_specs=out_specs, check_vma=False)
```

profile of v0, /device:TPU:0, one launch (start us, length us, event | category | flops | bytes accessed | tf_op | source)
XLA Modules:
  0.0 776.3 jit_solution(9756639017639703549)
XLA Ops:
  20.0 3.4 broadcast_bitcast_fusion
  23.4 7.1 copy.391
  30.5 4.3 slice.104
  34.8 13.2 %reshape.229 = f32[3,512,1023]{2,1,0:T(8,128)} reshape(f32[3,523776]{1,0:T(4,128)} %slice.104) | data formatting | bytes 12570624 | tf_op jit(solution)/shard_map/jvp()/reshape | solution.py:66
  48.0 4.6 slice.105
  52.7 3.7 copy.336
  66.1 4.1 fusion.94
  79.4 68.7 %all-reduce.13.cloned.1.call-done = f32[1024,768]{1,0:T(8,128)} async-done(((f32[1024,768]{1,0:T(8,128)}), f32[1024,768]{1,0:T(8,128)}) %all-reduce.13.cloned.1.call-update) | async-done | bytes 3145744 | tf_op jit(solution)/shard_map/psum | solution.py:207
  153.3 49.6 %all-gather.5.cloned.1.call-done = bf16[2,768,768]{2,1,0:T(8,128)(2,1)} async-done(((bf16[2,96,768]{2,1,0:T(8,128)(2,1)}), bf16[2,768,768]{2,1,0:T(8,128)(2,1)}) %all-gather.5.cloned.1.call-update) | async-done | bytes 2359312 | tf_op jit(solution)/shard_map/all_gather | solution.py:124
  202.9 11.7 %multiply_convert_fusion.1 = (bf16[1024,768]{1,0:T(8,128)(2,1)S(1)}, f32[1024,768]{1,0:T(8,128)}, f32[1024,768]{1,0:T(8,128)}) fusion(f32[768]{0:T(1024)} %dynamic_slice.32, bf16[2,768,768]{2,1,0:T(8,128)(2,1)} %all-gather.5.cloned.1.call-done, f32[1024,768]{1,0:T(8,128)} %copy-done.2, f32[768]{0:T(1024)S(1)} %copy-done.68, f32[768]{0:T(1024)S(1)} %copy-done.48, ...), kind=kOutput, calls=%fused_computation.38 | convolution fusion | flops 1263796224 | bytes 12208128 | tf_op jit(solution)/shard_map/dot_general | solution.py:212
  215.7 3.1 fusion.38
  219.0 67.1 %all-reduce.15.cloned.1.call-done = f32[1024,768]{1,0:T(8,128)} async-done(((f32[1024,768]{1,0:T(8,128)}), f32[1024,768]{1,0:T(8,128)}) %all-reduce.15.cloned.1.call-update) | async-done | bytes 3145744 | tf_op jit(solution)/shard_map/psum | solution.py:218
  286.0 3.9 fusion.90
  291.4 3.3 fusion.7
  299.5 2.9 convert_reduce_fusion.1
  303.5 3.1 fusion.35
  307.6 3.5 convolution_bitcast_fusion
  315.5 59.8 %all-reduce.17.cloned.1.call-done = f32[1024,768]{1,0:T(8,128)} async-done(((f32[1024,768]{1,0:T(8,128)}), f32[1024,768]{1,0:T(8,128)}) %all-reduce.17.cloned.1.call-update) | async-done | bytes 3145744 | tf_op jit(solution)/shard_map/psum | solution.py:237
  375.3 5.4 multiply_reduce_fusion.1
  387.6 4.7 convert_reduce_fusion.4
  392.3 4.3 multiply_reduce_fusion
  396.7 4.6 fusion.1
  418.3 8.5 %dynamic_update_slice.23 = f32[1024,768]{1,0:T(8,128)S(1)} dynamic-update-slice(f32[1024,768]{1,0:T(8,128)S(1)} %add_add_fusion.2, f32[1024,192]{1,0:T(8,128)} %dynamic-slice_add_fusion, s32[]{:T(128)} %constant.60.clone.1, s32[]{:T(128)S(6)} %select_n.12) | dynamic-update-slice | bytes 1572868 | tf_op jit(solution)/shard_map/dynamic_update_slice | solution.py:296
  443.7 4.0 pad.13.clone
  447.8 13.6 %reshape.235 = f32[3,523776]{1,0:T(4,128)} reshape(f32[3,512,1023]{2,1,0:T(8,128)} %pad.13.clone) | data formatting | bytes 12570624 | tf_op jit(solution)/shard_map/transpose(jvp())/reshape | solution.py:66
  461.3 4.9 pad.14
  466.4 3.3 bitcast_reduce_fusion
  475.9 167.9 %all-reduce.21.cloned.1.call-done = (f32[4,768,192]{1,2,0:T(8,128)}, f32[2,768,768]{2,1,0:T(8,128)}) async-done(((f32[4,768,192]{1,2,0:T(8,128)}, f32[2,768,768]{2,1,0:T(8,128)}), (f32[4,768,192]{1,2,0:T(8,128)}, f32[2,768,768]{2,1,0:T(8,128)})) %all-reduce.21.cloned.1.call-update) | async-done | bytes 7077904 | tf_op jit(solution)/shard_map/psum | solution.py:324
  648.8 64.9 %all-reduce.19.cloned.1.call-done = f32[1024,768]{1,0:T(8,128)} async-done(((f32[1024,768]{1,0:T(8,128)}), f32[1024,768]{1,0:T(8,128)}) %all-reduce.19.cloned.1.call-update) | async-done | bytes 3145744 | tf_op jit(solution)/shard_map/psum | solution.py:299
  713.8 3.5 add_convert_fusion
  717.2 40.1 %all-reduce.5 = (f32[]{:T(128)}, f32[13198]{0:T(1024)S(1)}) all-reduce(f32[]{:T(128)S(6)} %add.262, f32[13198]{0:T(1024)} %concatenate.7), channel_id=1, replica_groups=mesh['dp'=8,'tensor'=4] {'dp','tensor'}, use_global_device_ids=true, to_apply=%region_20.21 | all-reduce | flops 13199 | bytes 105592 | tf_op jit(solution)/shard_map/psum | solution.py:334
  764.8 2.7 fusion.82
  (313 shorter events, 107.6 us)
Async XLA Ops:
  7.2 11.8 %copy-start.80 = (s32[1023]{0:T(1024)S(1)}, s32[1023]{0:T(1024)}, u32[]{:S(2)}) copy-start(s32[1023]{0:T(1024)} %param.18) | copy-start | bytes 12280
  7.2 50.9 %all-gather.3.cloned.1.call-start = ((), (), s32[]{:S(2)}) async-start(), calls=%async_computation | async-start | bytes 1769472 | tf_op jit(solution)/shard_map/all_gather | solution.py:123
  9.0 139.1 %all-reduce.13.cloned.1.call-start = ((), (), s32[]{:S(2)}) async-start(), calls=%async_computation.1 | async-start | bytes 6291456 | tf_op jit(solution)/shard_map/psum | solution.py:207
  9.7 10.3 %copy-start.74 = (f32[2]{0:T(128)}, f32[2]{0:T(128)S(1)}, u32[]{:S(2)}) copy-start(f32[2]{0:T(128)S(1)} %slice.81) | copy-start | bytes 28
  19.0 47.1 %copy-start.41 = (f32[2,3,512]{2,1,0:T(4,128)}, f32[2,3,512]{2,1,0:T(4,128)S(1)}, u32[]{:S(2)}) copy-start(f32[2,3,512]{2,1,0:T(4,128)S(1)} %copy.335) | copy-start | bytes 36868
  76.7 71.4 %copy-start.70 = (f32[768]{0:T(1024)S(1)}, f32[768]{0:T(1024)}, u32[]{:S(2)}) copy-start(f32[768]{0:T(1024)} %get-tuple-element.173) | copy-start | bytes 9220
  76.8 126.2 %all-gather.5.cloned.1.call-start = ((), (), s32[]{:S(2)}) async-start(), calls=%async_computation.2 | async-start | bytes 2654208 | tf_op jit(solution)/shard_map/all_gather | solution.py:124
  78.6 207.4 %all-reduce.15.cloned.1.call-start = ((), (), s32[]{:S(2)}) async-start(), calls=%async_computation.3 | async-start | bytes 6291456 | tf_op jit(solution)/shard_map/psum | solution.py:218
  150.6 52.4 %copy-start.48 = (f32[768]{0:T(1024)S(1)}, f32[768]{0:T(1024)}, u32[]{:S(2)}) copy-start(f32[768]{0:T(1024)} %get-tuple-element.172) | copy-start | bytes 9220
  150.6 52.3 %copy-start.68 = (f32[768]{0:T(1024)S(1)}, f32[768]{0:T(1024)}, u32[]{:S(2)}) copy-start(f32[768]{0:T(1024)} %get-tuple-element.171) | copy-start | bytes 9220
  150.6 135.4 %copy-start.44 = (f32[1024]{0:T(1024)}, f32[1024]{0:T(1024)S(1)}, u32[]{:S(2)}) copy-start(f32[1024]{0:T(1024)S(1)} %broadcast_multiply_fusion.7) | copy-start | bytes 12292
  153.3 132.7 %copy-start.51 = (f32[1024]{0:T(1024)}, f32[1024]{0:T(1024)S(1)}, u32[]{:S(2)}) copy-start(f32[1024]{0:T(1024)S(1)} %fusion.76) | copy-start | bytes 12292
  202.9 12.8 %copy-start.78 = (bf16[2,768,768]{2,1,0:T(8,128)(2,1)S(1)}, bf16[2,768,768]{2,1,0:T(8,128)(2,1)}, u32[]{:S(2)}) copy-start(bf16[2,768,768]{2,1,0:T(8,128)(2,1)} %all-gather.5.cloned.1.call-done) | copy-start | bytes 7077892
  218.9 156.4 %all-reduce.17.cloned.1.call-start = ((), (), s32[]{:S(2)}) async-start(), calls=%async_computation.4 | async-start | bytes 6291456 | tf_op jit(solution)/shard_map/psum | solution.py:237
  296.2 6.1 copy-start.62
  306.6 337.2 %all-reduce.21.cloned.1.call-start = ((), (), s32[]{:S(2)}) async-start(), calls=%async_computation.6 | async-start | bytes 14155776 | tf_op jit(solution)/shard_map/psum | solution.py:324
  375.3 5.5 copy-start.50
  375.3 5.5 copy-start.53
  387.6 9.0 %slice-start = ((s8[6291456]{0:T(1024)(128)(4,1)}), s8[4194304]{0:T(1024)(128)(4,1)S(1)}, s32[]{:S(2)}) async-start(s8[6291456]{0:T(1024)(128)(4,1)} %bitcast.148), calls=%async_computation.7 | async-start | bytes 8388608
  409.0 304.8 %all-reduce.19.cloned.1.call-start = ((), (), s32[]{:S(2)}) async-start(), calls=%async_computation.5 | async-start | bytes 6291456 | tf_op jit(solution)/shard_map/psum | solution.py:299
  418.3 10.2 %copy-start.24 = (f32[4,96,192]{2,1,0:T(8,128)S(1)}, f32[4,96,192]{2,1,0:T(8,128)}, u32[]{:S(2)}) copy-start(f32[4,96,192]{2,1,0:T(8,128)} %param.19) | copy-start | bytes 884740
  466.3 7.2 copy-start.59
  466.3 7.1 copy-start.60
  466.3 7.5 copy-start.66
  466.3 7.5 copy-start.67
  466.3 7.5 copy-start.71
  466.3 8.2 %copy-start.58 = (f32[3072]{0:T(1024)S(1)}, f32[3072]{0:T(1024)}, u32[]{:S(2)}) copy-start(f32[3072]{0:T(1024)} %copy-done.57) | copy-start | bytes 36868
  466.3 247.4 %copy-start.7 = (f32[1024,768]{1,0:T(8,128)S(1)}, f32[1024,768]{1,0:T(8,128)}, u32[]{:S(2)}) copy-start(f32[1024,768]{1,0:T(8,128)} %copy-done.6) | copy-start | bytes 9437188
  648.8 110.5 %copy-start.28 = (f32[4,96,192]{1,2,0:T(8,128)S(1)}, f32[4,96,192]{1,2,0:T(8,128)}, u32[]{:S(2)}) copy-start(f32[4,96,192]{1,2,0:T(8,128)} %copy.364) | copy-start | bytes 884740
  717.2 47.5 %copy-start.21 = (f32[2,96,768]{2,1,0:T(8,128)S(1)}, f32[2,96,768]{2,1,0:T(8,128)}, u32[]{:S(2)}) copy-start(f32[2,96,768]{2,1,0:T(8,128)} %param.22) | copy-start | bytes 1769476
  717.2 47.5 %copy-start.29 = (f32[2,96,768]{2,1,0:T(8,128)S(1)}, f32[2,96,768]{2,1,0:T(8,128)}, u32[]{:S(2)}) copy-start(f32[2,96,768]{2,1,0:T(8,128)} %param.24) | copy-start | bytes 1769476
  717.2 47.5 %copy-start.30 = (f32[2,96,768]{2,1,0:T(8,128)S(1)}, f32[2,96,768]{2,1,0:T(8,128)}, u32[]{:S(2)}) copy-start(f32[2,96,768]{2,1,0:T(8,128)} %param.23) | copy-start | bytes 1769476
  (65 other events, 180.4 us)
Sparse Core Ops, SparseCore 0:
  10.8 46.8 all-gather.2
  76.9 71.1 all-reduce.12
  150.8 52.0 all-gather.4
  219.0 66.9 all-reduce.14
  306.7 68.5 all-reduce.16
  409.1 234.6 all-reduce.20
  646.3 67.4 all-reduce.18
where the time goes:
time: 784 us; the launch traced here: 776 us
  waiting for transfers between devices  478 us (61%)
  local copies, waits for them, and re-layouts  117 us (15%)
  matrix products  61.7 us (8%)
  other arithmetic  59.4 us (8%)
  blocking collectives  40.1 us (5%)
  between operations  19.4 us (2%)
    psum x1, waiting for transfers between devices, body(): lax.psum((local_attention, local_forward), 'dp')  168 us
    psum x1, waiting for transfers between devices, body(): attention = lax.psum(attention_part, 'tensor') + bias_output  68.7 us
    psum x1, waiting for transfers between devices, body(): feedforward = lax.psum(down_part, 'tensor') + bias_down  67.1 us
    psum x1, waiting for transfers between devices, body(): grad_inputs = lax.psum(input_part, 'tensor') + DEEP_ALPHA * grad_res_one  64.9 us
    psum x1, waiting for transfers between devices, body(): normed_sum = lax.psum(normed_part, 'tensor')  59.8 us
    all_gather x1, waiting for transfers between devices, body(): lax.all_gather(feedforward_weights.astype(jnp.bfloat16), 'dp', axis=1, ti...  49.6 us
    psum x1, blocking collectives, body(): big_squares = lax.psum(share_squares, ('dp', 'tensor'))  40.1 us
    unnamed x193, local copies, waits for them, and re-layouts  34.1 us
  transfers between devices with their start and end apart: 7, of which 6 were waited for; matrix products, arithmetic and copies ran while one was open for 17% of the time, Pallas kernels for 0%

commit v1 on v0

--- a/solution.py
+++ b/solution.py
@@ -1,8 +1,11 @@
 from functools import partial
+from types import SimpleNamespace
 
 import jax
 import jax.numpy as jnp
 from jax import lax
+from jax.experimental import pallas as pl
+from jax.experimental.pallas import tpu as pltpu
 from jax.sharding import PartitionSpec as P
 
 MODEL_WIDTH = 768
@@ -103,7 +106,7 @@
     return jnp.sum(values.astype(jnp.float32), axis=0)
 
 
-def body(
+def general_body(
     tokens,
     cotangent,
     clip_lengths,
@@ -371,6 +374,1044 @@
     )
 
 
+F32 = jnp.float32
+BF16 = jnp.bfloat16
+MESH_ID = pl.DeviceIdType.MESH
+LANES = 128
+SMALL_ROWS = 104
+TABLE_ROW = 72
+GATE_ROW = 102
+OFFSET_ROW = 103
+INV_SQRT2 = 0.5**0.5
+INV_SQRT_2PI = 0.3989422804014327
+CHUNK = 128
+HALF = 256
+W = MODEL_WIDTH
+NT = (((1,), (1,)), ((), ()))
+TN = (((0,), (0,)), ((), ()))
+
+
+def mm(a, b):
+    return jnp.dot(a, b, preferred_element_type=F32)
+
+
+def mm_nt(a, b):
+    return lax.dot_general(a, b, NT, preferred_element_type=F32)
+
+
+def mm_tn(a, b):
+    return lax.dot_general(a, b, TN, preferred_element_type=F32)
+
+
+def exact_nt(a, b):
+    return lax.dot_general(a, b, NT, precision=FULL_PRECISION, preferred_element_type=F32)
+
+
+def exact_tn(a, b):
+    return lax.dot_general(a, b, TN, precision=FULL_PRECISION, preferred_element_type=F32)
+
+
+def exact_mm(a, b):
+    return jnp.dot(a, b, precision=FULL_PRECISION, preferred_element_type=F32)
+
+
+def iota(shape, axis):
+    return lax.broadcasted_iota(jnp.int32, shape, axis)
+
+
+def layer_scratch(owned, nz, qkv_pad, heads, head_cols, hidden):
+    rows = 2 * BUCKET_SLOTS
+    out_pad = -(-head_cols // LANES) * LANES
+    dma = pltpu.SemaphoreType.DMA
+    vm = pltpu.VMEM
+    steps = 2 * nz - 1
+    shapes = dict(
+        tok=vm((rows, W), BF16),
+        cot=vm((2, HALF, W), BF16),
+        wqkv=vm((W, qkv_pad), BF16),
+        wo=vm((W, out_pad), BF16),
+        wup=vm((W, hidden), BF16),
+        wdown=vm((W, hidden), BF16),
+        q=vm((rows, head_cols), BF16),
+        k=vm((rows, head_cols), BF16),
+        v=vm((rows, head_cols), BF16),
+        ctx=vm((rows, head_cols), BF16),
+        dctx=vm((rows, head_cols), BF16),
+        dqkv=vm((rows, qkv_pad), BF16),
+        prob=vm((2 * heads, BUCKET_SLOTS, BUCKET_SLOTS), F32),
+        gsb=vm((heads, BUCKET_SLOTS, BUCKET_SLOTS), BF16),
+        pbb=vm((heads, BUCKET_SLOTS, BUCKET_SLOTS), BF16),
+        dqf=vm((BUCKET_SLOTS, head_cols), F32),
+        mbias=vm((2, BUCKET_SLOTS, BUCKET_SLOTS), BF16),
+        band=vm((heads, LANES, 2 * BUCKET_SLOTS), F32),
+        dband=vm((heads, LANES, 2 * BUCKET_SLOTS), F32),
+        gate=vm((rows, LANES), F32),
+        gu=vm((rows, LANES), F32),
+        gw=vm((rows, LANES), F32),
+        dgate=vm((rows, LANES), F32),
+        dlin=vm((rows, LANES), F32),
+        gmat=vm((W, LANES), F32),
+        vecs=vm((16, W), F32),
+        acc=vm((16, W), F32),
+        nb=vm((rows, W), BF16),
+        held=vm((2, HALF, W), F32),
+        xh1=vm((2, HALF, W), F32),
+        rstd1=vm((2, HALF, LANES), F32),
+        act=vm((rows, hidden), BF16),
+        gelup=vm((rows, hidden), F32),
+        gffn=vm((rows, W), BF16),
+        gub=vm((rows, hidden), BF16),
+        gattn=vm((rows, W), BF16),
+        stage=vm((2, HALF, W), BF16),
+        tstage=vm((2, HALF, W), BF16),
+        ownf=vm((HALF, W), F32),
+        cs=vm((2, HALF, W), BF16),
+        cr=vm((2, HALF, W), BF16),
+        ys=vm((2, HALF, W), BF16),
+        yr=vm((2, 2, HALF, W), BF16),
+        xrqkv=vm((nz, owned, qkv_pad), BF16),
+        xro=vm((nz, owned, out_pad), BF16),
+        xrup=vm((nz, owned, hidden), BF16),
+        xrdown=vm((nz, owned, hidden), BF16),
+        zsqkv=vm((nz - 1, owned, qkv_pad), BF16),
+        zso=vm((nz - 1, owned, out_pad), BF16),
+        zsup=vm((nz - 1, owned, hidden), BF16),
+        zsdown=vm((nz - 1, owned, hidden), BF16),
+        zrqkv=vm((nz - 1, owned, qkv_pad), BF16),
+        zro=vm((nz - 1, owned, out_pad), BF16),
+        zrup=vm((nz - 1, owned, hidden), BF16),
+        zrdown=vm((nz - 1, owned, hidden), BF16),
+        sm=vm((4, SMALL_ROWS, LANES), F32),
+        smr=vm((3, SMALL_ROWS, LANES), F32),
+        smz=vm((nz, SMALL_ROWS, LANES), F32),
+        sqt=vm((4, 8, LANES), F32),
+        sqd=vm((2 * nz, 8, LANES), F32),
+        s_in=dma((3,)),
+        s_gs=dma((4, steps)),
+        s_gr=dma((4, steps)),
+        s_cs=dma((4, 2)),
+        s_cr=dma((4, 2)),
+        s_ys=dma((4, 2)),
+        s_yr=dma((4, 2)),
+        s_as=dma((3, 2)),
+        s_ar=dma((3, 2)),
+        s_ol=dma((2, 2)),
+        s_os=dma((2, 2)),
+        s_or=dma((2, 2)),
+        s_xs=dma((4, nz)),
+        s_xr=dma((4, nz)),
+        s_zs=dma((4, nz)),
+        s_zr=dma((4, nz)),
+        s_ms=dma((3 + nz,)),
+        s_mr=dma((3 + nz,)),
+        s_ts=dma((4,)),
+        s_tr=dma((4,)),
+        s_ds=dma((2 * nz,)),
+        s_dr=dma((2 * nz,)),
+    )
+    return shapes
+
+
+def layer_kernel(names, dims, *refs):
+    n_dp, owned, qkv_pad, heads, head_cols, hidden = dims
+    nz = n_dp // 2
+    (tok_in, cot_in, lens, keep, relb, wa, wf, small) = refs[:8]
+    (bo_out, tg_out, sh_qkv, sh_o, sh_up, sh_down, small_out, norm_out) = refs[8:16]
+    m = SimpleNamespace(**dict(zip(names, refs[16:], strict=True)))
+    D = lax.axis_index("dp")
+    T = lax.axis_index("tensor")
+    z = lax.div(D, 2)
+    x = lax.rem(D, 2)
+    c = lax.rem(T, 2)
+    yy = lax.div(T, 2)
+    core_dev = (D, T + 1 - 2 * c)
+    y_dev = (D, lax.rem(T + 2, 4))
+    x_dev = (z * 2 + 1 - x, T)
+
+    def z_at(k):
+        return lax.rem(z + k, nz)
+
+    def z_dev(k):
+        return (z_at(k) * 2 + x, T)
+
+    def remote(src, dst, ss, rs, dev):
+        return pltpu.make_async_remote_copy(
+            src_ref=src, dst_ref=dst, send_sem=ss, recv_sem=rs, device_id=dev, device_id_type=MESH_ID
+        )
+
+    def loop(n, step):
+        def run(i, carry):
+            step(i)
+            return carry
+
+        lax.fori_loop(0, n, run, 0)
+
+    def block(owner):
+        return pl.ds(pl.multiple_of(owner * owned, owned), owned)
+
+    tok_copy = pltpu.make_async_copy(tok_in, m.tok, m.s_in.at[0])
+    tok_copy.start()
+    cot_copies = []
+    for b in range(2):
+        rows = pl.ds(pl.multiple_of(b * BUCKET_SLOTS + c * HALF, HALF), HALF)
+        cp = pltpu.make_async_copy(cot_in.at[rows], m.cot.at[b], m.s_in.at[1 + b])
+        cp.start()
+        cot_copies.append(cp)
+    barrier = pltpu.get_barrier_semaphore()
+    for k in range(1, 4):
+        pl.semaphore_signal(barrier, inc=1, device_id=(D, lax.rem(T + k, 4)), device_id_type=MESH_ID)
+    for k in range(1, n_dp):
+        pl.semaphore_signal(barrier, inc=1, device_id=(lax.rem(D + k, n_dp), T), device_id_type=MESH_ID)
+    mine = block(D)
+    qkv_own = [wa[0], wa[1], wa[2]]
+    if qkv_pad > 3 * head_cols:
+        qkv_own.append(jnp.zeros((owned, qkv_pad - 3 * head_cols), F32))
+    m.wqkv[mine, :] = jnp.concatenate(qkv_own, axis=1).astype(BF16)
+    out_pad = m.wo.shape[1]
+    o_own = [wa[3]]
+    if out_pad > head_cols:
+        o_own.append(jnp.zeros((owned, out_pad - head_cols), F32))
+    m.wo[mine, :] = jnp.concatenate(o_own, axis=1).astype(BF16)
+    m.wup[mine, :] = wf[0].astype(BF16)
+    m.wdown[mine, :] = wf[1].astype(BF16)
+    pl.semaphore_wait(barrier, 3 + n_dp - 1)
+
+    def gather_start(which, buf):
+        own = buf.at[mine]
+        sent = []
+        for k in range(1, nz):
+            sent.append(
+                remote(own, own, m.s_gs.at[which, k], m.s_gr.at[which, nz - k], z_dev(k))
+            )
+        sent.append(remote(own, own, m.s_gs.at[which, 0], m.s_gr.at[which, 0], x_dev))
+        for cp in sent:
+            cp.start()
+        gathers[which] = sent
+
+    def gather_pass(which, buf):
+        sent = gathers[which]
+        for j in range(1, nz):
+            part = buf.at[block(z_at(j) * 2 + x)]
+            remote(part, part, m.s_gs.at[which, j], m.s_gr.at[which, j], x_dev).wait_recv()
+            cp = remote(
+                part, part, m.s_gs.at[which, nz - 1 + j], m.s_gr.at[which, nz - 1 + j], x_dev
+            )
+            cp.start()
+            sent.append(cp)
+
+    def gather_end(which, buf):
+        for j in range(nz):
+            part = buf.at[block(z_at(j) * 2 + 1 - x)]
+            index = 0 if j == 0 else nz - 1 + j
+            remote(
+                part, part, m.s_gs.at[which, index], m.s_gr.at[which, index], x_dev
+            ).wait_recv()
+
+    gathers = {}
+    gather_start(0, m.wqkv)
+
+    def small_row(first, count):
+        return jnp.concatenate([small[first + i : first + i + 1, :] for i in range(count)], axis=1)
+
+    def pick(values, size):
+        total = jnp.zeros((1, size), F32)
+        for t in range(4):
+            total = total + jnp.where(T == t, values[:, t * size : (t + 1) * size], 0.0)
+        return total
+
+    vecs = m.vecs
+    vecs[...] = jnp.zeros_like(vecs)
+    m.acc[...] = jnp.zeros((16, W), F32)
+    for at, first in ((0, 0), (1, 6), (2, 12), (3, 18), (4, 36), (5, 42)):
+        vecs[at : at + 1, :] = small_row(first, W // LANES)
+    vecs[6:7, :] = pick(small_row(48, FF // LANES), hidden)
+    bq = pick(small_row(24, W // LANES), head_cols)
+    bv = pick(small_row(30, W // LANES), head_cols)
+    bias_qkv = jnp.concatenate(
+        [bq, jnp.zeros_like(bq), bv, jnp.zeros((1, qkv_pad - 3 * head_cols), F32)], axis=1
+    )
+    vecs[7:8, 0:qkv_pad] = bias_qkv
+
+    lane = iota((1, LANES), 1)
+    col = iota((W, LANES), 0)
+    col_lane = iota((W, LANES), 1)
+    gate_row = small[GATE_ROW : GATE_ROW + 1, :]
+    col_in_head = lax.rem(col, HD)
+    picked_u = jnp.sum(
+        jnp.where(col_lane == 2 * col_in_head, gate_row, 0.0), axis=1, keepdims=True
+    )
+    picked_w = jnp.sum(
+        jnp.where(col_lane == 2 * col_in_head + 1, gate_row, 0.0), axis=1, keepdims=True
+    )
+    in_group = lax.rem(col_lane, 8)
+    own_head = (col_lane < 16) & (in_group < heads) & (lax.div(col, HD) == T * heads + in_group)
+    m.gmat[...] = jnp.where(own_head, jnp.where(col_lane < 8, picked_u, picked_w), 0.0)
+    offset_row = small[OFFSET_ROW : OFFSET_ROW + 1, :]
+    offset_u = jnp.sum(jnp.where(lane == 0, offset_row, 0.0), axis=1, keepdims=True)
+    offset_w = jnp.sum(jnp.where(lane == 1, offset_row, 0.0), axis=1, keepdims=True)
+    scale = jnp.zeros((1, LANES), F32)
+    for h in range(heads):
+        one = jnp.sum(jnp.where(lane == 2 + T * heads + h, offset_row, 0.0), axis=1, keepdims=True)
+        scale = scale + jnp.where(lane == h, one, 0.0)
+    head_lane = lane < heads
+
+    offsets = jnp.concatenate([relb[i : i + 1, :] for i in range(2 * BUCKET_SLOTS // LANES)], axis=1)
+    table = small[TABLE_ROW : TABLE_ROW + 32, :]
+    long_row = 2 * BUCKET_SLOTS
+    sub8 = iota((8, long_row), 0)
+    for h in range(heads):
+        flat = offsets * H + (T * heads + h)
+        at_row = lax.div(flat, LANES)
+        at_lane = lax.rem(flat, LANES)
+        hot_row = jnp.where(iota((32, long_row), 0) == at_row, 1.0, 0.0)
+        spread = exact_tn(table, hot_row)
+        values = jnp.sum(
+            jnp.where(iota((LANES, long_row), 0) == at_lane, spread, 0.0), axis=0, keepdims=True
+        )
+        stack = jnp.broadcast_to(pltpu.roll(jnp.broadcast_to(values, (8, long_row)), 1, 1), (8, long_row))
+        for bit in (1, 2, 4):
+            stack = jnp.where(lax.rem(lax.div(sub8, bit), 2) == 1, pltpu.roll(stack, bit, 1), stack)
+        size = 8
+        m.band[h, 0:8, :] = stack
+        while size < LANES:
+            m.band[h, size : 2 * size, :] = pltpu.roll(m.band[h, 0:size, :], size, 1)
+            size *= 2
+    m.dband[...] = jnp.zeros(m.dband.shape, F32)
+
+    for b in range(2):
+        end = 0
+        ends = []
+        for i in range(CLIPS):
+            end = end + lens[b, i]
+            ends.append(end)
+        key_at = iota((1, BUCKET_SLOTS), 1)
+        key_segment = jnp.zeros((1, BUCKET_SLOTS), jnp.int32)
+        for end in ends:
+            key_segment = key_segment + jnp.where(key_at >= end, 1, 0)
+        kept = jnp.concatenate([keep[4 * b + i : 4 * b + i + 1, :] for i in range(4)], axis=1)
+        live = jnp.where((kept == 1) & (key_segment < CLIPS), key_segment, -1)
+
+        def mask_chunk(i, b=b, ends=ends, live=live):
+            query_at = iota((CHUNK, BUCKET_SLOTS), 0) + i * CHUNK
+            segment = jnp.zeros((CHUNK, BUCKET_SLOTS), jnp.int32)
+            for end in ends:
+                segment = segment + jnp.where(query_at >= end, 1, 0)
+            allowed = (segment == live) | (query_at == iota((CHUNK, BUCKET_SLOTS), 1))
+            m.mbias[b, pl.ds(pl.multiple_of(i * CHUNK, CHUNK), CHUNK), :] = jnp.where(
+                allowed, 0.0, MASK_VALUE
+            ).astype(BF16)
+
+        loop(BUCKET_SLOTS // CHUNK, mask_chunk)
+
+    tok_copy.wait()
+    gmat = m.gmat[...]
+    part_hi = gmat.astype(BF16)
+    rest = gmat - part_hi.astype(F32)
+    part_mid = rest.astype(BF16)
+    part_lo = (rest - part_mid.astype(F32)).astype(BF16)
+
+    def gate_chunk(i):
+        rows = pl.ds(pl.multiple_of(i * HALF, HALF), HALF)
+        tokens = m.tok[rows, :]
+        linear = mm(tokens, part_hi) + mm(tokens, part_mid) + mm(tokens, part_lo)
+        u = jax.nn.sigmoid(linear + offset_u)
+        w = jax.nn.sigmoid(pltpu.roll(linear, LANES - 8, 1) + offset_w)
+        m.gu[rows, :] = u
+        m.gw[rows, :] = w
+        m.gate[rows, :] = u * (w * scale - 1.0) + 2.0
+
+    loop(4, gate_chunk)
+
+    gather_pass(0, m.wqkv)
+    gather_end(0, m.wqkv)
+    gather_start(1, m.wo)
+    gather_start(2, m.wup)
+    gather_start(3, m.wdown)
+
+    def project(i):
+        rows = pl.ds(pl.multiple_of(i * HALF, HALF), HALF)
+        both = mm(m.tok[rows, :], m.wqkv[...]) + vecs[7:8, 0:qkv_pad]
+        query = both[:, 0:head_cols].astype(BF16)
+        m.q[rows, :] = (query.astype(F32) * 0.125).astype(BF16)
+        m.k[rows, :] = both[:, head_cols : 2 * head_cols].astype(BF16)
+        m.v[rows, :] = both[:, 2 * head_cols : 3 * head_cols].astype(BF16)
+
+    loop(4, project)
+
+    head_of = lax.div(iota((1, head_cols), 1), HD)
+    head_masks = [jnp.where(head_of == h, 1.0, 0.0) for h in range(heads)]
+    low_masks = [m.astype(BF16) for m in head_masks]
+
+    def attend(b):
+        keys = m.k[b * BUCKET_SLOTS : (b + 1) * BUCKET_SLOTS, :]
+        values = m.v[b * BUCKET_SLOTS : (b + 1) * BUCKET_SLOTS, :]
+
+        def chunk(i):
+            local = pl.ds(pl.multiple_of(i * CHUNK, CHUNK), CHUNK)
+            rows = pl.ds(pl.multiple_of(b * BUCKET_SLOTS + i * CHUNK, CHUNK), CHUNK)
+            window = pl.ds(pl.multiple_of(BUCKET_SLOTS - i * CHUNK, CHUNK), BUCKET_SLOTS)
+            query = m.q[rows, :]
+            gates = m.gate[rows, :]
+            context = jnp.zeros((CHUNK, head_cols), F32)
+            for h in range(heads):
+                scores = mm_nt(query * low_masks[h], keys)
+                scores = scores + gates[:, h : h + 1] * m.band[h, :, window]
+                scores = scores + m.mbias[b, local, :].astype(F32)
+                top = jnp.max(scores, axis=1, keepdims=True)
+                weight = jnp.exp(scores - top)
+                total = jnp.sum(weight, axis=1, keepdims=True)
+                probability = weight * (1.0 / total)
+                m.prob[b * heads + h, local, :] = probability
+                context = context + mm(probability.astype(BF16), values) * head_masks[h]
+            m.ctx[rows, :] = context.astype(BF16)
+
+        loop(BUCKET_SLOTS // CHUNK, chunk)
+
+    core_sent = {}
+    y_sent = {}
+
+    def exchange(phase, b, product):
+        other = b * BUCKET_SLOTS + (1 - c) * HALF
+        own = b * BUCKET_SLOTS + c * HALF
+        if (phase - 1, b) in core_sent:
+            core_sent[(phase - 1, b)].wait_send()
+            y_sent[(phase - 1, b)].wait_send()
+
+        def send_chunk(i):
+            at = pl.ds(pl.multiple_of(i * CHUNK, CHUNK), CHUNK)
+            rows = pl.ds(pl.multiple_of(other + i * CHUNK, CHUNK), CHUNK)
+            m.cs[b, at, :] = product(rows).astype(BF16)
+
+        loop(HALF // CHUNK, send_chunk)
+        cp = remote(
+            m.cs.at[b], m.cr.at[b], m.s_cs.at[phase, b], m.s_cr.at[phase, b], core_dev
+        )
+        cp.start()
+        core_sent[(phase, b)] = cp
+
+        def own_chunk(i):
+            at = pl.ds(pl.multiple_of(i * CHUNK, CHUNK), CHUNK)
+            rows = pl.ds(pl.multiple_of(own + i * CHUNK, CHUNK), CHUNK)
+            m.ownf[at, :] = product(rows)
+
+        loop(HALF // CHUNK, own_chunk)
+        cp.wait_recv()
+
+        def add_chunk(i):
+            at = pl.ds(pl.multiple_of(i * CHUNK, CHUNK), CHUNK)
+            m.ys[b, at, :] = (m.ownf[at, :] + m.cr[b, at, :].astype(F32)).astype(BF16)
+
+        loop(HALF // CHUNK, add_chunk)
+        cp = remote(
+            m.ys.at[b],
+            m.yr.at[phase % 2, b],
+            m.s_ys.at[phase, b],
+            m.s_yr.at[phase, b],
+            y_dev,
+        )
+        cp.start()
+        y_sent[(phase, b)] = cp
+
+    def arrived(phase, b, at):
+        return m.ys[b, at, :].astype(F32) + m.yr[phase % 2, b, at, :].astype(F32)
+
+    def own_rows(b, i):
+        return pl.ds(pl.multiple_of(b * BUCKET_SLOTS + c * HALF + i * CHUNK, CHUNK), CHUNK)
+
+    core_spread = {}
+
+    def spread_start(which, buf, b):
+        rows = pl.ds(pl.multiple_of(b * BUCKET_SLOTS + c * HALF, HALF), HALF)
+        part = buf.at[rows]
+        cp = remote(part, part, m.s_as.at[which, b], m.s_ar.at[which, b], core_dev)
+        cp.start()
+        core_spread[(which, b)] = cp
+
+    def spread_end(which, b):
+        core_spread[(which, b)].wait_recv()
+
+    def row_mean(values):
+        return jnp.mean(values, axis=1, keepdims=True)
+
+    def add_row(at, values):
+        m.acc[at : at + 1, 0 : values.shape[1]] += jnp.sum(values, axis=0, keepdims=True)
+
+    def norm_one(b):
+        y_sent[(0, b)].wait_recv()
+
+        def chunk(i):
+            at = pl.ds(pl.multiple_of(i * CHUNK, CHUNK), CHUNK)
+            rows = own_rows(b, i)
+            residual = DEEP_ALPHA * m.tok[rows, :].astype(F32) + (arrived(0, b, at) + vecs[4:5, :])
+            centred = residual - row_mean(residual)
+            rstd = lax.rsqrt(row_mean(centred * centred) + NORM_EPSILON)
+            hat = centred * rstd
+            normed = hat * vecs[0:1, :] + vecs[1:2, :]
+            m.xh1[b, at, :] = hat
+            m.rstd1[b, at, :] = jnp.broadcast_to(rstd, (CHUNK, LANES))
+            m.held[b, at, :] = normed
+            m.nb[rows, :] = normed.astype(BF16)
+
+        loop(HALF // CHUNK, chunk)
+        spread_start(0, m.nb, b)
+
+    def feed(b):
+        spread_end(0, b)
+
+        def chunk(i):
+            rows = pl.ds(pl.multiple_of(b * BUCKET_SLOTS + i * CHUNK, CHUNK), CHUNK)
+            up = mm(m.nb[rows, :], m.wup[...]) + vecs[6:7, :]
+            half_phi = 0.5 * (1.0 + lax.erf(up * INV_SQRT2))
+            m.act[rows, :] = (up * half_phi).astype(BF16)
+            m.gelup[rows, :] = half_phi + up * (jnp.exp(up * up * -0.5) * INV_SQRT_2PI)
+
+        loop(BUCKET_SLOTS // CHUNK, chunk)
+
+    out_copies = []
+
+    def result_rows(which, b, stage, out):
+        rows = pl.ds(pl.multiple_of(b * BUCKET_SLOTS + c * HALF, HALF), HALF)
+        part = stage.at[b]
+        here = pltpu.make_async_copy(part, out.at[rows], m.s_ol.at[which, b])
+        there = remote(part, out.at[rows], m.s_os.at[which, b], m.s_or.at[which, b], core_dev)
+        here.start()
+        there.start()
+        out_copies.append((here, there))
+
+    def norm_two(b):
+        y_sent[(1, b)].wait_recv()
+        cot_copies[b].wait()
+
+        def chunk(i):
+            at = pl.ds(pl.multiple_of(i * CHUNK, CHUNK), CHUNK)
+            rows = own_rows(b, i)
+            residual = DEEP_ALPHA * m.held[b, at, :] + (arrived(1, b, at) + vecs[5:6, :])
+            centred = residual - row_mean(residual)
+            rstd = lax.rsqrt(row_mean(centred * centred) + NORM_EPSILON)
+            hat = centred * rstd
+            m.stage[b, at, :] = (hat * vecs[2:3, :] + vecs[3:4, :]).astype(BF16)
+            upstream = m.cot[b, at, :].astype(F32)
+            add_row(2, upstream * hat)
+            add_row(3, upstream)
+            scaled = upstream * vecs[2:3, :]
+            grad = rstd * (scaled - row_mean(scaled) - hat * row_mean(scaled * hat))
+            m.held[b, at, :] = grad
+            low = grad.astype(BF16)
+            m.gffn[rows, :] = low
+            add_row(5, low.astype(F32))
+
+        loop(HALF // CHUNK, chunk)
+        spread_start(1, m.gffn, b)
+        result_rows(0, b, m.stage, bo_out)
+
+    def feed_back(b):
+        spread_end(1, b)
+
+        def chunk(i):
+            rows = pl.ds(pl.multiple_of(b * BUCKET_SLOTS + i * CHUNK, CHUNK), CHUNK)
+            grad = mm(m.gffn[rows, :], m.wdown[...]) * m.gelup[rows, :]
+            low = grad.astype(BF16)
+            m.gub[rows, :] = low
+            add_row(6, low.astype(F32))
+
+        loop(BUCKET_SLOTS // CHUNK, chunk)
+
+    def norm_one_back(b):
+        y_sent[(2, b)].wait_recv()
+
+        def chunk(i):
+            at = pl.ds(pl.multiple_of(i * CHUNK, CHUNK), CHUNK)
+            rows = own_rows(b, i)
+            upstream = arrived(2, b, at) + DEEP_ALPHA * m.held[b, at, :]
+            hat = m.xh1[b, at, :]
+            add_row(0, upstream * hat)
+            add_row(1, upstream)
+            scaled = upstream * vecs[0:1, :]
+            rstd = m.rstd1[b, at, 0:1]
+            grad = rstd * (scaled - row_mean(scaled) - hat * row_mean(scaled * hat))
+            m.held[b, at, :] = grad
+            low = grad.astype(BF16)
+            m.gattn[rows, :] = low
+            add_row(4, low.astype(F32))
+
+        loop(HALF // CHUNK, chunk)
+        spread_start(2, m.gattn, b)
+
+    def attend_back(b):
+        spread_end(2, b)
+        keys = m.k[b * BUCKET_SLOTS : (b + 1) * BUCKET_SLOTS, :]
+        values = m.v[b * BUCKET_SLOTS : (b + 1) * BUCKET_SLOTS, :]
+
+        def chunk(i):
+            local = pl.ds(pl.multiple_of(i * CHUNK, CHUNK), CHUNK)
+            rows = pl.ds(pl.multiple_of(b * BUCKET_SLOTS + i * CHUNK, CHUNK), CHUNK)
+            window = pl.ds(pl.multiple_of(BUCKET_SLOTS - i * CHUNK, CHUNK), BUCKET_SLOTS)
+            place = pl.ds(pl.multiple_of(3 * CHUNK - i * CHUNK, CHUNK), BUCKET_SLOTS)
+            grad_context = mm(m.gattn[rows, :], m.wo[:, 0:head_cols]).astype(BF16)
+            m.dctx[rows, :] = grad_context
+            gates = m.gate[rows, :]
+            grad_query = jnp.zeros((CHUNK, head_cols), F32)
+            grad_gates = jnp.zeros((CHUNK, LANES), F32)
+            for h in range(heads):
+                grad_probs = mm_nt(grad_context * low_masks[h], values)
+                probability = m.prob[b * heads + h, local, :]
+                m.pbb[h, local, :] = probability.astype(BF16)
+                inner = jnp.sum(grad_probs * probability, axis=1, keepdims=True)
+                low = (probability * (grad_probs - inner)).astype(BF16)
+                m.gsb[h, local, :] = low
+                grad_query = grad_query + mm(low, keys) * head_masks[h]
+                rounded = low.astype(F32)
+                one = jnp.sum(rounded * m.band[h, :, window], axis=1, keepdims=True)
+                grad_gates = grad_gates + jnp.where(lane == h, one, 0.0)
+                m.dband[h, :, place] += rounded * gates[:, h : h + 1]
+            m.dqf[local, :] = grad_query * 0.125
+            m.dgate[rows, :] = grad_gates
+
+        loop(BUCKET_SLOTS // CHUNK, chunk)
+        all_rows = slice(b * BUCKET_SLOTS, (b + 1) * BUCKET_SLOTS)
+        grad_key = jnp.zeros((BUCKET_SLOTS, head_cols), F32)
+        grad_value = jnp.zeros((BUCKET_SLOTS, head_cols), F32)
+        for h in range(heads):
+            grad_key = grad_key + mm_tn(m.gsb[h], m.q[all_rows, :]) * head_masks[h]
+            grad_value = grad_value + mm_tn(m.pbb[h], m.dctx[all_rows, :]) * head_masks[h]
+        pieces = [m.dqf[...], grad_key, grad_value]
+        if qkv_pad > 3 * head_cols:
+            pieces.append(jnp.zeros((BUCKET_SLOTS, qkv_pad - 3 * head_cols), F32))
+        low = jnp.concatenate(pieces, axis=1).astype(BF16)
+        m.dqkv[all_rows, :] = low
+        add_row(7, low.astype(F32))
+
+        def gate_back(i):
+            rows = pl.ds(pl.multiple_of(b * BUCKET_SLOTS + i * CHUNK, CHUNK), CHUNK)
+            grad = m.dgate[rows, :]
+            u = m.gu[rows, :]
+            w = m.gw[rows, :]
+            grad_u = grad * (w * scale - 1.0) * u * (1.0 - u)
+            grad_w = grad * u * scale * w * (1.0 - w)
+            grad_u = jnp.where(head_lane, grad_u, 0.0)
+            grad_w = jnp.where(head_lane, grad_w, 0.0)
+            m.dlin[rows, :] = grad_u + pltpu.roll(grad_w, 8, 1)
+            add_row(8, jnp.where(head_lane, grad * u * w, 0.0))
+
+        loop(BUCKET_SLOTS // CHUNK, gate_back)
+
+    def input_part(rows):
+        return mm_nt(m.dqkv[rows, :], m.wqkv[...]) + exact_nt(m.dlin[rows, :], m.gmat[...])
+
+    def token_rows(b):
+        y_sent[(3, b)].wait_recv()
+
+        def chunk(i):
+            at = pl.ds(pl.multiple_of(i * CHUNK, CHUNK), CHUNK)
+            total = arrived(3, b, at) + DEEP_ALPHA * m.held[b, at, :]
+            m.tstage[b, at, :] = total.astype(BF16)
+
+        loop(HALF // CHUNK, chunk)
+        result_rows(1, b, m.tstage, tg_out)
+
+    def weight_grad(which, buf, left, right, width):
+        for cp in gathers.pop(which):
+            cp.wait_send()
+
+        def chunk(i):
+            cols = pl.ds(pl.multiple_of(i * HALF, HALF), HALF)
+            part = mm_tn(left[:, cols], right[...])
+            if width < buf.shape[1]:
+                part = jnp.concatenate([part, jnp.zeros((HALF, buf.shape[1] - width), F32)], axis=1)
+            buf[cols, :] = part.astype(BF16)
+
+        loop(W // HALF, chunk)
+
+    reduces = []
+
+    def reduce_start(which, buf, land):
+        for zt in range(nz):
+            cp = remote(
+                buf.at[block(2 * zt + 1 - x)],
+                land.at[zt],
+                m.s_xs.at[which, zt],
+                m.s_xr.at[which, zt],
+                x_dev,
+            )
+            cp.start()
+            reduces.append(cp)
+
+    def reduce_pass(which, buf, land, out, arrive, share):
+        for k in list(range(1, nz)) + [0]:
+            zt = z_at(k)
+            here = land.at[zt]
+            remote(here, here, m.s_xs.at[which, zt], m.s_xr.at[which, zt], x_dev).wait_recv()
+            total = buf[block(2 * zt + x), :].astype(F32) + land[zt].astype(F32)
+            if k == 0:
+                share[...] = total
+            else:
+                out[k - 1] = total.astype(BF16)
+                cp = remote(
+                    out.at[k - 1],
+                    arrive.at[k - 1],
+                    m.s_zs.at[which, k],
+                    m.s_zr.at[which, k],
+                    z_dev(k),
+                )
+                cp.start()
+                reduces.append(cp)
+
+    def reduce_end(which, arrive, share):
+        total = share[...]
+        for k in range(1, nz):
+            here = arrive.at[k - 1]
+            remote(here, here, m.s_zs.at[which, k], m.s_zr.at[which, k], z_dev(k)).wait_recv()
+            total = total + arrive[k - 1].astype(F32)
+        share[...] = total
+        squares = total * total
+        folded = jnp.zeros((owned, LANES), F32)
+        for i in range(total.shape[1] // LANES):
+            folded = folded + squares[:, i * LANES : (i + 1) * LANES]
+        tile = jnp.zeros((8, LANES), F32)
+        for i in range(owned // 8):
+            tile = tile + folded[8 * i : 8 * i + 8, :]
+        return tile
+
+    attend(0)
+    gather_pass(1, m.wo)
+    gather_end(1, m.wo)
+    out_product = lambda rows: mm_nt(m.ctx[rows, :], m.wo[:, 0:head_cols])
+    exchange(0, 0, out_product)
+    attend(1)
+    gather_pass(2, m.wup)
+    exchange(0, 1, out_product)
+    gather_pass(3, m.wdown)
+    norm_one(0)
+    gather_end(2, m.wup)
+    feed(0)
+    gather_end(3, m.wdown)
+    down_product = lambda rows: mm_nt(m.act[rows, :], m.wdown[...])
+    exchange(1, 0, down_product)
+    norm_one(1)
+    feed(1)
+    exchange(1, 1, down_product)
+    up_product = lambda rows: mm_nt(m.gub[rows, :], m.wup[...])
+    norm_two(0)
+    feed_back(0)
+    exchange(2, 0, up_product)
+    norm_two(1)
+    feed_back(1)
+    exchange(2, 1, up_product)
+    weight_grad(3, m.wdown, m.gffn, m.act, hidden)
+    reduce_start(0, m.wdown, m.xrdown)
+    weight_grad(2, m.wup, m.nb, m.gub, hidden)
+    reduce_start(1, m.wup, m.xrup)
+    norm_one_back(0)
+    attend_back(0)
+    exchange(3, 0, input_part)
+    reduce_pass(0, m.wdown, m.xrdown, m.zsdown, m.zrdown, sh_down)
+    norm_one_back(1)
+    attend_back(1)
+    exchange(3, 1, input_part)
+    weight_grad(0, m.wqkv, m.tok, m.dqkv, qkv_pad)
+    reduce_start(3, m.wqkv, m.xrqkv)
+    reduce_pass(1, m.wup, m.xrup, m.zsup, m.zrup, sh_up)
+    weight_grad(1, m.wo, m.gattn, m.ctx, head_cols)
+    reduce_start(2, m.wo, m.xro)
+
+    sm = m.sm
+    acc = m.acc
+    lead = jnp.where(yy == 0, 1.0, 0.0)
+
+    def put(first, values):
+        for i in range(values.shape[1] // LANES):
+            sm[0, first + i : first + i + 1, :] = values[:, i * LANES : (i + 1) * LANES]
+
+    def spot(values):
+        return jnp.concatenate([jnp.where(T == t, values, 0.0) for t in range(4)], axis=1)
+
+    for at, first in ((0, 0), (1, 6), (2, 12), (3, 18), (4, 36), (5, 42)):
+        put(first, acc[at : at + 1, :] * lead)
+    put(24, spot(acc[7:8, 0:head_cols]))
+    put(30, spot(acc[7:8, 2 * head_cols : 3 * head_cols]))
+    put(48, spot(acc[6:7, 0:hidden]))
+    table_grad = jnp.zeros((32, LANES), F32)
+    for h in range(heads):
+        size = LANES // 2
+        left = m.dband[h]
+        while size >= 1:
+            left = left[0:size, :] + pltpu.roll(left[size : 2 * size, :], long_row - size, 1) if size >= 8 else left
+            if size < 8:
+                break
+            size //= 2
+        for bit in (1, 2, 4):
+            left = jnp.where(lax.rem(lax.div(sub8, bit), 2) == 1, pltpu.roll(left, long_row - bit, 1), left)
+        diagonal = jnp.sum(left, axis=0, keepdims=True)
+        diagonal = pltpu.roll(jnp.broadcast_to(diagonal, (8, long_row)), LANES - 1, 1)[0:1, :]
+        flat = offsets * H + (T * heads + h)
+        at_row = lax.div(flat, LANES)
+        at_lane = lax.rem(flat, LANES)
+        valid = iota((1, long_row), 1) < long_row - 1
+        hot_row = jnp.where((iota((32, long_row), 0) == at_row) & valid, 1.0, 0.0)
+        hot_lane = jnp.where(iota((LANES, long_row), 0) == at_lane, diagonal, 0.0)
+        table_grad = table_grad + exact_nt(hot_row, hot_lane)
+    sm[0, TABLE_ROW : TABLE_ROW + 30, :] = table_grad[0:30, :]
+
+    lin = m.dlin[...]
+    lin_hi = lin.astype(BF16)
+    lin_rest = lin - lin_hi.astype(F32)
+    lin_mid = lin_rest.astype(BF16)
+    lin_lo = (lin_rest - lin_mid.astype(F32)).astype(BF16)
+    lin_grad = mm_tn(lin_hi, m.tok[...]) + mm_tn(lin_mid, m.tok[...]) + mm_tn(lin_lo, m.tok[...])
+    group = iota((16, W), 0)
+    mine_here = (lax.rem(group, 8) < heads) & (
+        lax.div(iota((16, W), 1), HD) == T * heads + lax.rem(group, 8)
+    )
+    lin_grad = jnp.where(mine_here, lin_grad[0:16, :], 0.0)
+    hot = jnp.where(lax.rem(col, HD) == lax.div(col_lane, 2), 1.0, 0.0)
+    folded = exact_mm(lin_grad, hot)
+    by_lane = jnp.where(
+        lax.rem(lane, 2) == 0,
+        jnp.sum(folded[0:8, :], axis=0, keepdims=True),
+        jnp.sum(folded[8:16, :], axis=0, keepdims=True),
+    )
+    sm[0, GATE_ROW : GATE_ROW + 1, :] = by_lane
+    lin_total = jnp.sum(lin, axis=0, keepdims=True)
+    total_u = jnp.sum(jnp.where(lane < 8, lin_total, 0.0), axis=1, keepdims=True)
+    total_w = jnp.sum(jnp.where((lane >= 8) & (lane < 16), lin_total, 0.0), axis=1, keepdims=True)
+    last = jnp.where(lane == 0, total_u, 0.0) + jnp.where(lane == 1, total_w, 0.0)
+    scale_grad = acc[8:9, 0:LANES]
+    for h in range(heads):
+        one = jnp.sum(jnp.where(lane == h, scale_grad, 0.0), axis=1, keepdims=True)
+        last = last + jnp.where(lane == 2 + T * heads + h, one, 0.0)
+    sm[0, OFFSET_ROW : OFFSET_ROW + 1, :] = last
+
+    small_sent = []
+
+    def small_step(at, dev):
+        cp = remote(sm.at[at], m.smr.at[at], m.s_ms.at[at], m.s_mr.at[at], dev)
+        cp.start()
+        small_sent.append(cp)
+        return cp
+
+    token_rows(0)
+    small_copy = small_step(0, core_dev)
+    small_copy.wait_recv()
+    sm[1] = sm[0] + m.smr[0]
+    small_copy = small_step(1, y_dev)
+    reduce_pass(3, m.wqkv, m.xrqkv, m.zsqkv, m.zrqkv, sh_qkv)
+    small_copy.wait_recv()
+    sm[2] = sm[1] + m.smr[1]
+    small_copy = small_step(2, x_dev)
+    reduce_pass(2, m.wo, m.xro, m.zso, m.zro, sh_o)
+    token_rows(1)
+    small_copy.wait_recv()
+    sm[3] = sm[2] + m.smr[2]
+    for k in range(1, nz):
+        cp = remote(
+            sm.at[3], m.smz.at[z], m.s_ms.at[2 + k], m.s_mr.at[2 + k], z_dev(k)
+        )
+        cp.start()
+        small_sent.append(cp)
+    m.smz[z] = sm[3]
+    squares = reduce_end(0, m.zrdown, sh_down)
+    squares = squares + reduce_end(1, m.zrup, sh_up)
+    squares = squares + reduce_end(2, m.zro, sh_o)
+    squares = squares + reduce_end(3, m.zrqkv, sh_qkv)
+    sqt = m.sqt
+    sqt[T] = squares
+    tail_sent = []
+    for k in range(1, 4):
+        cp = remote(
+            sqt.at[T], sqt.at[T], m.s_ts.at[k], m.s_tr.at[k], (D, lax.rem(T + k, 4))
+        )
+        cp.start()
+        tail_sent.append(cp)
+    for k in range(1, nz):
+        here = m.smz.at[z_at(nz - k)]
+        remote(here, here, m.s_ms.at[2 + k], m.s_mr.at[2 + k], z_dev(k)).wait_recv()
+    small_total = m.smz[0]
+    for i in range(1, nz):
+        small_total = small_total + m.smz[i]
+    small_out[...] = small_total
+    small_square = small_total * small_total
+    small_tile = jnp.zeros((8, LANES), F32)
+    for i in range(SMALL_ROWS // 8):
+        small_tile = small_tile + small_square[8 * i : 8 * i + 8, :]
+    for k in range(1, 4):
+        here = sqt.at[lax.rem(T + 4 - k, 4)]
+        remote(here, here, m.s_ts.at[k], m.s_tr.at[k], core_dev).wait_recv()
+    sqd = m.sqd
+    sqd[D] = sqt[0] + sqt[1] + sqt[2] + sqt[3]
+    for k in range(1, n_dp):
+        cp = remote(
+            sqd.at[D], sqd.at[D], m.s_ds.at[k], m.s_dr.at[k], (lax.rem(D + k, n_dp), T)
+        )
+        cp.start()
+        tail_sent.append(cp)
+    for k in range(1, n_dp):
+        here = sqd.at[lax.rem(D + n_dp - k, n_dp)]
+        remote(here, here, m.s_ds.at[k], m.s_dr.at[k], core_dev).wait_recv()
+    everything = small_tile
+    for i in range(n_dp):
+        everything = everything + sqd[i]
+    sum_all = jnp.sum(jnp.sum(everything, axis=0, keepdims=True), axis=1, keepdims=True)
+    norm_out[...] = jnp.broadcast_to(jnp.sqrt(sum_all), (8, LANES))
+
+    for cp in reduces + small_sent + tail_sent:
+        cp.wait_send()
+    for cp in core_spread.values():
+        cp.wait_send()
+    for b in range(2):
+        core_sent[(3, b)].wait_send()
+        y_sent[(3, b)].wait_send()
+    for here, there in out_copies:
+        here.wait()
+        there.wait()
+
+
+def adam_kernel(
+    head_cols,
+    sh_qkv, sh_o, sh_up, sh_down, sh_small, norm,
+    aw, am, av, fw, fm, fv, sw, sm, sv,
+    norm_out,
+    o_am, o_av, o_aw, o_ac, o_fm, o_fv, o_fw, o_fc, o_sm, o_sv, o_sw,
+):
+    length = norm[0:1, 0:1]
+    factor = CLIP_LIMIT / jnp.maximum(length, CLIP_LIMIT)
+    for i in range(4):
+        if i < 3:
+            grad = sh_qkv[:, i * head_cols : (i + 1) * head_cols]
+        else:
+            grad = sh_o[:, 0:head_cols]
+        moment, square, master = adam_step(
+            aw[i], am[i], av[i], factor * grad, RATE_MATRIX, WEIGHT_DECAY
+        )
+        o_am[i] = moment
+        o_av[i] = square
+        o_aw[i] = master
+        o_ac[i] = master.astype(BF16)
+    for i, share in enumerate((sh_up, sh_down)):
+        moment, square, master = adam_step(
+            fw[i], fm[i], fv[i], factor * share[...], RATE_MATRIX, WEIGHT_DECAY
+        )
+        o_fm[i] = moment
+        o_fv[i] = square
+        o_fw[i] = master
+        o_fc[i] = master.astype(BF16)
+    moment, square, master = adam_step(sw[...], sm[...], sv[...], factor * sh_small[...], RATE_SMALL, 0.0)
+    o_sm[...] = moment
+    o_sv[...] = square
+    o_sw[...] = master
+    norm_out[...] = jnp.broadcast_to(length, (8, LANES))
+
+
+def tiles(vector):
+    return jnp.pad(vector, (0, SMALL_ROWS * LANES - vector.shape[0])).reshape(SMALL_ROWS, LANES)
+
+
+def fused_body(
+    n_dp,
+    tokens,
+    cotangent,
+    clip_lengths,
+    key_mask,
+    rel_buckets,
+    attention_weights,
+    attention_first,
+    attention_second,
+    feedforward_weights,
+    feedforward_first,
+    feedforward_second,
+    small_params,
+    small_first,
+    small_second,
+):
+    rows = tokens.shape[0]
+    owned, head_cols = attention_weights.shape[1:]
+    hidden = feedforward_weights.shape[2]
+    heads = head_cols // HD
+    qkv_pad = -(-3 * head_cols // LANES) * LANES
+    out_pad = -(-head_cols // LANES) * LANES
+    nz = n_dp // 2
+    small = tiles(small_params)
+    offsets = jnp.pad(rel_buckets, (0, 1)).reshape(2 * BUCKET_SLOTS // LANES, LANES)
+    keep = key_mask.reshape(rows // LANES, LANES)
+    scratch = layer_scratch(owned, nz, qkv_pad, heads, head_cols, hidden)
+    names = tuple(scratch)
+    vmem = pl.BlockSpec(memory_space=pltpu.VMEM)
+    smem = pl.BlockSpec(memory_space=pltpu.SMEM)
+    anywhere = pl.BlockSpec(memory_space=pl.ANY)
+    sds = jax.ShapeDtypeStruct
+    block_rows, token_rows, sh_qkv, sh_o, sh_up, sh_down, sh_small, norm = pl.pallas_call(
+        partial(layer_kernel, names, (n_dp, owned, qkv_pad, heads, head_cols, hidden)),
+        out_shape=(
+            sds((rows, W), BF16),
+            sds((rows, W), BF16),
+            sds((owned, qkv_pad), F32),
+            sds((owned, out_pad), F32),
+            sds((owned, hidden), F32),
+            sds((owned, hidden), F32),
+            sds((SMALL_ROWS, LANES), F32),
+            sds((8, LANES), F32),
+        ),
+        in_specs=[anywhere, anywhere, smem, vmem, vmem, vmem, vmem, vmem],
+        out_specs=(anywhere, anywhere, vmem, vmem, vmem, vmem, vmem, vmem),
+        scratch_shapes=list(scratch.values()),
+        compiler_params=pltpu.CompilerParams(
+            collective_id=1, has_side_effects=True, vmem_limit_bytes=60 * 1024 * 1024
+        ),
+        name="layer",
+    )(tokens, cotangent, clip_lengths, keep, offsets, attention_weights, feedforward_weights, small)
+    like = lambda a, dtype=F32: sds(a.shape, dtype)
+    results = pl.pallas_call(
+        partial(adam_kernel, head_cols),
+        out_shape=(
+            sds((8, LANES), F32),
+            like(attention_weights),
+            like(attention_weights),
+            like(attention_weights),
+            like(attention_weights, BF16),
+            like(feedforward_weights),
+            like(feedforward_weights),
+            like(feedforward_weights),
+            like(feedforward_weights, BF16),
+            sds((SMALL_ROWS, LANES), F32),
+            sds((SMALL_ROWS, LANES), F32),
+            sds((SMALL_ROWS, LANES), F32),
+        ),
+        in_specs=[vmem] * 15,
+        out_specs=(vmem,) * 12,
+        compiler_params=pltpu.CompilerParams(vmem_limit_bytes=32 * 1024 * 1024),
+        name="adam",
+    )(
+        sh_qkv,
+        sh_o,
+        sh_up,
+        sh_down,
+        sh_small,
+        norm,
+        attention_weights,
+        attention_first,
+        attention_second,
+        feedforward_weights,
+        feedforward_first,
+        feedforward_second,
+        small,
+        tiles(small_first),
+        tiles(small_second),
+    )
+    length = small_params.shape[0]
+    flat = lambda a: a.reshape(-1)[:length]
+    return (
+        results[0][0, 0],
+        *results[1:9],
+        flat(results[9]),
+        flat(results[10]),
+        flat(results[11]),
+        block_rows,
+        token_rows,
+    )
+
+
+def fused_fits(mesh, owned):
+    return mesh.shape["tensor"] == 4 and mesh.shape["dp"] % 2 == 0 and owned % 16 == 0
+
 def solution(mesh):
     in_specs = (
         P("dp", None),
@@ -404,4 +1445,8 @@
         P("dp", None),
         P("dp", None),
     )
+    n_dp = mesh.shape["dp"]
+    body = general_body
+    if fused_fits(mesh, MODEL_WIDTH // n_dp):
+        body = partial(fused_body, n_dp)
     return jax.shard_map(body, mesh=mesh, in_specs=in_specs, out_specs=out_specs, check_vma=False)

time: 784 us -> 189 us (0.24)
  waiting for transfers between devices: 478 us -> 0 us
  Pallas kernels: 0 us -> 176 us
  local copies, waits for them, and re-layouts: 117 us -> 12.5 us
  matrix products: 61.7 us -> 0 us
  other arithmetic: 59.4 us -> 0 us
  blocking collectives: 40.1 us -> 0 us
  between operations: 19.4 us -> 0.78 us
    psum x5 -> x0, waiting for transfers between devices: 428 us -> none  [the longest x1 168 us: body(): lax.psum((local_attention, local_forward), 'dp')]
    pallas_call x0 -> x2, Pallas kernels: none -> 176 us  [the longest x1 173 us: fused_body(): pl.pallas_call(partial(layer_kernel, names, (n_dp, owned, qkv_pad, heads,...]
    dot_general x29 -> x0, matrix products: 61.7 us -> none  [the longest x1 11.7 us: body(): jnp.dot(normed_bf, up_weight, preferred_element_type=jnp.float32)]
    all_gather x2 -> x0, waiting for transfers between devices: 49.6 us -> none  [the longest x1 49.6 us: body(): lax.all_gather(feedforward_weights.astype(jnp.bfloat16), 'dp', axis=1, ti...]
    psum x1 -> x0, blocking collectives: 40.1 us -> none  [body(): big_squares = lax.psum(share_squares, ('dp', 'tensor'))]
    reduce_sum x19 -> x0, other arithmetic: 35.3 us -> none  [the longest x2 8.78 us: layer_norm(): return centred * lax.rsqrt(variance + NORM_EPSILON) * norm_gain + norm_shift]
    reshape x12 -> x3, local copies, waits for them, and re-layouts: 34.8 us -> 3.56 us  [the longest x2 2.28 us: tiles(): jnp.pad(vector, (0, SMALL_ROWS * LANES - vector.shape[0]))]
    unnamed x193 -> x32, local copies, waits for them, and re-layouts: 34.1 us -> 8.39 us
  transfers between devices with their start and end apart: 7 -> 0, of which waited for: 6 -> 0; matrix products, arithmetic and copies ran while one was open for 17% -> 0% of each run, Pallas kernels for 0% -> 0%
where the time goes in v1:
time: 189 us
  Pallas kernels  176 us (93%)
  local copies, waits for them, and re-layouts  12.5 us (7%)
    pallas_call x1, Pallas kernels, fused_body(): pl.pallas_call(partial(layer_kernel, names, (n_dp, owned, qkv_pad, heads,...  173 us
    unnamed x32, local copies, waits for them, and re-layouts  8.39 us

profile of v1, /device:TPU:0, one launch (start us, length us, event | category | flops | bytes accessed | tf_op | source)
XLA Modules:
  0.0 189.0 jit_solution(18114898820613747859)
XLA Ops:
  0.6 1.3 pad_bitcast_fusion.3.refs_4_
  1.9 1.4 pad_bitcast_fusion.2.refs_7_.sw
  3.4 0.8 pad_bitcast_fusion
  4.2 0.0 copy-start
  4.2 0.0 copy-start.1
  4.2 0.0 copy-start.2
  4.2 0.0 copy-start.3
  4.2 0.0 copy-start.4
  4.3 0.0 copy-start.5
  4.3 0.0 copy-start.6
  4.3 172.7 %layer.1 = (bf16[1024,768]{1,0:T(8,128)(2,1)}, bf16[1024,768]{1,0:T(8,128)(2,1)}, f32[96,640]{1,0:T(8,128)}, f32[96,256]{1,0:T(8,128)}, f32[96,768]{1,0:T(8,128)...) custom-call(bf16[1024,768]{1,0:T(8,128)(2,1)} %refs_0_.1, bf16[1024,768]{1,0:T(8,128)(2,1)} %refs_1_.1, ...), custom_call_target="tpu_custom_call" | custom-call | tf_op jit(solution)/shard_map/layer/pallas_call | solution.py:1341
  177.0 0.0 copy-done
  177.0 0.0 copy-done.1
  177.0 0.0 copy-done.2
  177.0 0.0 copy-done.3
  177.0 0.0 copy-done.4
  177.0 0.0 copy-done.5
  177.0 0.0 copy-done.6
  177.1 0.0 copy-start.7
  177.1 1.0 copy-done.7
  178.0 0.0 copy-start.8
  178.0 1.0 copy-done.8
  179.0 0.9 copy-done.9
  179.9 0.9 copy-done.10
  180.8 0.8 copy-done.11
  181.6 0.7 copy-done.12
  182.3 3.0 %adam.1 = (f32[8,128]{1,0:T(8,128)S(1)}, f32[4,96,192]{2,1,0:T(8,128)}, f32[4,96,192]{2,1,0:T(8,128)}, f32[4,96,192]{2,1,0:T(8,128)}, bf16[4,96,192]{2,1,0:T(8,1...) custom-call(f32[96,640]{1,0:T(8,128)S(1)} %copy-done.9, ...), custom_call_target="tpu_custom_call" | custom-call | tf_op jit(solution)/shard_map/adam/pallas_call | solution.py:1362
  185.3 0.5 slice.12
  185.8 0.0 copy-done.14
  185.8 1.1 copy.30
  187.0 0.8 copy-done.13
  187.8 1.1 copy.31
  (6 shorter events, 0.0 us)
Async XLA Ops:
  4.2 172.8 %copy-start = (f32[2,96,768]{2,1,0:T(8,128)S(1)}, f32[2,96,768]{2,1,0:T(8,128)}, u32[]{:S(2)}) copy-start(f32[2,96,768]{2,1,0:T(8,128)} %fw.1) | copy-start | bytes 1769476
  4.2 172.8 %copy-start.1 = (f32[4,96,192]{2,1,0:T(8,128)S(1)}, f32[4,96,192]{2,1,0:T(8,128)}, u32[]{:S(2)}) copy-start(f32[4,96,192]{2,1,0:T(8,128)} %aw.1) | copy-start | bytes 884740
  4.2 172.8 %copy-start.2 = (f32[2,96,768]{2,1,0:T(8,128)S(1)}, f32[2,96,768]{2,1,0:T(8,128)}, u32[]{:S(2)}) copy-start(f32[2,96,768]{2,1,0:T(8,128)} %fm.1) | copy-start | bytes 1769476
  4.2 172.8 %copy-start.3 = (f32[2,96,768]{2,1,0:T(8,128)S(1)}, f32[2,96,768]{2,1,0:T(8,128)}, u32[]{:S(2)}) copy-start(f32[2,96,768]{2,1,0:T(8,128)} %fv.1) | copy-start | bytes 1769476
  4.2 172.8 %copy-start.4 = (f32[104,128]{1,0:T(8,128)S(1)}, f32[104,128]{1,0:T(8,128)}, u32[]{:S(2)}) copy-start(f32[104,128]{1,0:T(8,128)} %pad_bitcast_fusion.2.refs_7_.sw) | copy-start | bytes 159748
  4.3 172.8 %copy-start.5 = (f32[4,96,192]{2,1,0:T(8,128)S(1)}, f32[4,96,192]{2,1,0:T(8,128)}, u32[]{:S(2)}) copy-start(f32[4,96,192]{2,1,0:T(8,128)} %am.1) | copy-start | bytes 884740
  4.3 172.8 %copy-start.6 = (f32[4,96,192]{2,1,0:T(8,128)S(1)}, f32[4,96,192]{2,1,0:T(8,128)}, u32[]{:S(2)}) copy-start(f32[4,96,192]{2,1,0:T(8,128)} %av.1) | copy-start | bytes 884740
  177.1 1.0 copy-start.7
  178.0 1.0 copy-start.8
  179.0 0.9 copy-start.9
  179.9 0.9 copy-start.10
  180.8 0.8 copy-start.11
  181.6 0.7 copy-start.12
  182.3 3.5 %copy-start.14 = (bf16[1024,768]{1,0:T(8,128)(2,1)S(1)}, bf16[1024,768]{1,0:T(8,128)(2,1)}, u32[]{:S(2)}) copy-start(bf16[1024,768]{1,0:T(8,128)(2,1)} %get-tuple-element.82) | copy-start | bytes 4718596
  185.8 2.0 %copy-start.13 = (bf16[1024,768]{1,0:T(8,128)(2,1)S(1)}, bf16[1024,768]{1,0:T(8,128)(2,1)}, u32[]{:S(2)}) copy-start(bf16[1024,768]{1,0:T(8,128)(2,1)} %get-tuple-element.83) | copy-start | bytes 4718596

commit v2 on v1

--- a/solution.py
+++ b/solution.py
@@ -421,35 +421,39 @@
 
 def layer_scratch(owned, nz, qkv_pad, heads, head_cols, hidden):
     rows = 2 * BUCKET_SLOTS
-    out_pad = -(-head_cols // LANES) * LANES
     dma = pltpu.SemaphoreType.DMA
     vm = pltpu.VMEM
-    steps = 2 * nz - 1
     shapes = dict(
         tok=vm((rows, W), BF16),
         cot=vm((2, HALF, W), BF16),
         wqkv=vm((W, qkv_pad), BF16),
-        wo=vm((W, out_pad), BF16),
+        wo1=vm((W, LANES), BF16),
+        wo=vm((W, head_cols), BF16),
+        wot=vm((head_cols, W), BF16),
+        wqkvt=vm((qkv_pad + LANES, W), BF16),
+        wupt=vm((hidden, W), BF16),
+        wdownt=vm((hidden, W), BF16),
+        go=vm((W, LANES), BF16),
+        glin=vm((W, LANES), F32),
         wup=vm((W, hidden), BF16),
         wdown=vm((W, hidden), BF16),
         q=vm((rows, head_cols), BF16),
         k=vm((rows, head_cols), BF16),
         v=vm((rows, head_cols), BF16),
+        kt=vm((head_cols, rows), BF16),
+        vt=vm((head_cols, rows), BF16),
         ctx=vm((rows, head_cols), BF16),
         dctx=vm((rows, head_cols), BF16),
-        dqkv=vm((rows, qkv_pad), BF16),
+        dqkv=vm((rows, qkv_pad + LANES), BF16),
         prob=vm((2 * heads, BUCKET_SLOTS, BUCKET_SLOTS), F32),
         gsb=vm((heads, BUCKET_SLOTS, BUCKET_SLOTS), BF16),
-        pbb=vm((heads, BUCKET_SLOTS, BUCKET_SLOTS), BF16),
         dqf=vm((BUCKET_SLOTS, head_cols), F32),
         mbias=vm((2, BUCKET_SLOTS, BUCKET_SLOTS), BF16),
         band=vm((heads, LANES, 2 * BUCKET_SLOTS), F32),
         dband=vm((heads, LANES, 2 * BUCKET_SLOTS), F32),
         gate=vm((rows, LANES), F32),
         gu=vm((rows, LANES), F32),
-        gw=vm((rows, LANES), F32),
         dgate=vm((rows, LANES), F32),
-        dlin=vm((rows, LANES), F32),
         gmat=vm((W, LANES), F32),
         vecs=vm((16, W), F32),
         acc=vm((16, W), F32),
@@ -463,22 +467,21 @@
         gub=vm((rows, hidden), BF16),
         gattn=vm((rows, W), BF16),
         stage=vm((2, HALF, W), BF16),
-        tstage=vm((2, HALF, W), BF16),
         ownf=vm((HALF, W), F32),
         cs=vm((2, HALF, W), BF16),
         cr=vm((2, HALF, W), BF16),
         ys=vm((2, HALF, W), BF16),
         yr=vm((2, 2, HALF, W), BF16),
         xrqkv=vm((nz, owned, qkv_pad), BF16),
-        xro=vm((nz, owned, out_pad), BF16),
+        xro=vm((nz, owned, LANES), BF16),
         xrup=vm((nz, owned, hidden), BF16),
         xrdown=vm((nz, owned, hidden), BF16),
         zsqkv=vm((nz - 1, owned, qkv_pad), BF16),
-        zso=vm((nz - 1, owned, out_pad), BF16),
+        zso=vm((nz - 1, owned, LANES), BF16),
         zsup=vm((nz - 1, owned, hidden), BF16),
         zsdown=vm((nz - 1, owned, hidden), BF16),
         zrqkv=vm((nz - 1, owned, qkv_pad), BF16),
-        zro=vm((nz - 1, owned, out_pad), BF16),
+        zro=vm((nz - 1, owned, LANES), BF16),
         zrup=vm((nz - 1, owned, hidden), BF16),
         zrdown=vm((nz - 1, owned, hidden), BF16),
         sm=vm((4, SMALL_ROWS, LANES), F32),
@@ -487,14 +490,18 @@
         sqt=vm((4, 8, LANES), F32),
         sqd=vm((2 * nz, 8, LANES), F32),
         s_in=dma((3,)),
-        s_gs=dma((4, steps)),
-        s_gr=dma((4, steps)),
-        s_cs=dma((4, 2)),
-        s_cr=dma((4, 2)),
-        s_ys=dma((4, 2)),
-        s_yr=dma((4, 2)),
-        s_as=dma((3, 2)),
-        s_ar=dma((3, 2)),
+        s_gs=dma((6,)),
+        s_gr=dma((6,)),
+        s_ls=dma((6, 2, nz)),
+        s_lr=dma((6, 2, nz)),
+        s_lxs=dma((6, 2, nz)),
+        s_lxr=dma((6, 2, nz)),
+        s_cs=dma((4, 2, 2)),
+        s_cr=dma((4, 2, 2)),
+        s_ys=dma((4, 2, 2)),
+        s_yr=dma((4, 2, 2)),
+        s_as=dma((3, 2, 2)),
+        s_ar=dma((3, 2, 2)),
         s_ol=dma((2, 2)),
         s_os=dma((2, 2)),
         s_or=dma((2, 2)),
@@ -515,9 +522,9 @@
 def layer_kernel(names, dims, *refs):
     n_dp, owned, qkv_pad, heads, head_cols, hidden = dims
     nz = n_dp // 2
-    (tok_in, cot_in, lens, keep, relb, wa, wf, small) = refs[:8]
-    (bo_out, tg_out, sh_qkv, sh_o, sh_up, sh_down, small_out, norm_out) = refs[8:16]
-    m = SimpleNamespace(**dict(zip(names, refs[16:], strict=True)))
+    (tok_in, cot_in, lens, keep, wa, wf, small) = refs[:7]
+    (bo_out, tg_out, sh_qkv, sh_o, sh_up, sh_down, small_out, norm_out) = refs[7:15]
+    m = SimpleNamespace(**dict(zip(names, refs[15:], strict=True)))
     D = lax.axis_index("dp")
     T = lax.axis_index("tensor")
     z = lax.div(D, 2)
@@ -530,6 +537,8 @@
 
     def z_at(k):
         return lax.rem(z + k, nz)
+
+    z_order = sorted(range(1, nz), key=lambda k: min(k, nz - k))
 
     def z_dev(k):
         return (z_at(k) * 2 + x, T)
@@ -563,52 +572,113 @@
     for k in range(1, n_dp):
         pl.semaphore_signal(barrier, inc=1, device_id=(lax.rem(D + k, n_dp), T), device_id_type=MESH_ID)
     mine = block(D)
-    qkv_own = [wa[0], wa[1], wa[2]]
-    if qkv_pad > 3 * head_cols:
-        qkv_own.append(jnp.zeros((owned, qkv_pad - 3 * head_cols), F32))
-    m.wqkv[mine, :] = jnp.concatenate(qkv_own, axis=1).astype(BF16)
-    out_pad = m.wo.shape[1]
-    o_own = [wa[3]]
-    if out_pad > head_cols:
-        o_own.append(jnp.zeros((owned, out_pad - head_cols), F32))
-    m.wo[mine, :] = jnp.concatenate(o_own, axis=1).astype(BF16)
+    first_o = qkv_pad - 3 * head_cols
+    m.wqkv[mine, :] = jnp.concatenate([wa[0], wa[1], wa[2], wa[3, :, 0:first_o]], axis=1).astype(BF16)
+    m.wo1[mine, :] = wa[3, :, first_o:head_cols].astype(BF16)
     m.wup[mine, :] = wf[0].astype(BF16)
     m.wdown[mine, :] = wf[1].astype(BF16)
     pl.semaphore_wait(barrier, 3 + n_dp - 1)
 
-    def gather_start(which, buf):
-        own = buf.at[mine]
-        sent = []
-        for k in range(1, nz):
-            sent.append(
-                remote(own, own, m.s_gs.at[which, k], m.s_gr.at[which, nz - k], z_dev(k))
-            )
-        sent.append(remote(own, own, m.s_gs.at[which, 0], m.s_gr.at[which, 0], x_dev))
-        for cp in sent:
-            cp.start()
-        gathers[which] = sent
-
-    def gather_pass(which, buf):
-        sent = gathers[which]
-        for j in range(1, nz):
-            part = buf.at[block(z_at(j) * 2 + x)]
-            remote(part, part, m.s_gs.at[which, j], m.s_gr.at[which, j], x_dev).wait_recv()
-            cp = remote(
-                part, part, m.s_gs.at[which, nz - 1 + j], m.s_gr.at[which, nz - 1 + j], x_dev
-            )
-            cp.start()
-            sent.append(cp)
-
-    def gather_end(which, buf):
-        for j in range(nz):
-            part = buf.at[block(z_at(j) * 2 + 1 - x)]
-            index = 0 if j == 0 else nz - 1 + j
-            remote(
-                part, part, m.s_gs.at[which, index], m.s_gr.at[which, index], x_dev
-            ).wait_recv()
+    part_rows = owned // 2 if owned % 32 == 0 else owned
+    pieces = [(m.wqkv, 0, owned), (m.wo1, 0, owned)]
+    for buf in (m.wup, m.wdown):
+        pieces.append((buf, 0, part_rows))
+        pieces.append((buf, owned - part_rows, part_rows))
+
+    def piece(which, owner):
+        buf, first, count = pieces[which]
+        return buf.at[pl.ds(pl.multiple_of(owner * owned + first, 16), count)]
 
     gathers = {}
-    gather_start(0, m.wqkv)
+
+    def launch(record, where):
+        remote(*where()).start()
+        record.append(where)
+
+    def when(condition, action):
+        pl.when(condition)(action)
+
+    def from_z(way, step):
+        owner_z = z - step if way == 0 else z + step
+        return owner_z, (owner_z >= 0) if way == 0 else (owner_z < nz)
+
+    def send_when(which, condition, where):
+        when(condition(), lambda: remote(*where()).start())
+        gathers.setdefault(which, []).append((condition, where))
+
+    def line_send(which, way, step, hops):
+        origin = step - hops
+
+        def where():
+            part = piece(which, from_z(way, origin)[0] * 2 + x)
+            target = ((z + hops if way == 0 else z - hops) * 2 + x, T)
+            return part, part, m.s_ls.at[which, way, step], m.s_lr.at[which, way, step], target
+
+        def condition():
+            there = (z + hops < nz) if way == 0 else (z >= hops)
+            return there & from_z(way, origin)[1]
+
+        send_when(which, condition, where)
+
+    def line_start(which, hops):
+        for hop in range(1, hops + 1):
+            for way in range(2):
+                line_send(which, way, hop, hop)
+
+    def gather_x(which):
+        def where():
+            own = piece(which, D)
+            return own, own, m.s_gs.at[which], m.s_gr.at[which], x_dev
+
+        send_when(which, lambda: D >= 0, where)
+
+    def line_step(which, step, hops):
+        for way in range(2):
+
+            def landed(way=way):
+                part = piece(which, from_z(way, step)[0] * 2 + x)
+                sems = m.s_ls.at[which, way, step], m.s_lr.at[which, way, step]
+                remote(part, part, *sems, x_dev).wait_recv()
+
+            when(from_z(way, step)[1], landed)
+            if step >= hops and step + 1 < nz:
+                line_send(which, way, step + 1, 1)
+
+            def where(way=way):
+                part = piece(which, from_z(way, step)[0] * 2 + x)
+                return part, part, m.s_lxs.at[which, way, step], m.s_lxr.at[which, way, step], x_dev
+
+            send_when(which, lambda way=way: from_z(way, step)[1], where)
+
+    def line_end(which):
+        part = piece(which, z * 2 + 1 - x)
+        remote(part, part, m.s_gs.at[which], m.s_gr.at[which], x_dev).wait_recv()
+        for step in range(1, nz):
+            for way in range(2):
+
+                def landed(way=way):
+                    part = piece(which, from_z(way, step)[0] * 2 + 1 - x)
+                    sems = m.s_lxs.at[which, way, step], m.s_lxr.at[which, way, step]
+                    remote(part, part, *sems, x_dev).wait_recv()
+
+                when(from_z(way, step)[1], landed)
+
+    def sent_all(which):
+        for condition, where in gathers.pop(which):
+            when(condition(), lambda where=where: remote(*where()).wait_send())
+
+    def turn(source, target):
+        count = source.shape[1]
+        step = HALF if count % HALF == 0 else LANES
+
+        def chunk(i):
+            at = pl.ds(pl.multiple_of(i * step, step), step)
+            target[at, :] = source[:, at].T
+
+        loop(count // step, chunk)
+
+    line_start(0, 1)
+    gather_x(0)
 
     def small_row(first, count):
         return jnp.concatenate([small[first + i : first + i + 1, :] for i in range(count)], axis=1)
@@ -655,7 +725,9 @@
         scale = scale + jnp.where(lane == h, one, 0.0)
     head_lane = lane < heads
 
-    offsets = jnp.concatenate([relb[i : i + 1, :] for i in range(2 * BUCKET_SLOTS // LANES)], axis=1)
+    line_step(0, 1, 1)
+
+    offsets = small_row(3 * SMALL_ROWS, 2 * BUCKET_SLOTS // LANES).astype(jnp.int32)
     table = small[TABLE_ROW : TABLE_ROW + 32, :]
     long_row = 2 * BUCKET_SLOTS
     sub8 = iota((8, long_row), 0)
@@ -678,6 +750,8 @@
             size *= 2
     m.dband[...] = jnp.zeros(m.dband.shape, F32)
 
+    line_step(0, 2, 1)
+
     for b in range(2):
         end = 0
         ends = []
@@ -703,38 +777,49 @@
 
         loop(BUCKET_SLOTS // CHUNK, mask_chunk)
 
+    for step in range(3, nz):
+        line_step(0, step, 1)
+    line_start(1, 2)
+
     tok_copy.wait()
     gmat = m.gmat[...]
     part_hi = gmat.astype(BF16)
     rest = gmat - part_hi.astype(F32)
     part_mid = rest.astype(BF16)
     part_lo = (rest - part_mid.astype(F32)).astype(BF16)
+    gate_parts = (part_hi, part_hi, part_hi, part_mid, part_mid, part_lo)
+    stacked = jnp.zeros((W, LANES), F32)
+    for i, part in enumerate(gate_parts):
+        moved = part.astype(F32)
+        stacked = stacked + (pltpu.roll(moved, 16 * i, 1) if i else moved)
+    m.wqkvt[qkv_pad : qkv_pad + LANES, :] = stacked.astype(BF16).T
 
     def gate_chunk(i):
         rows = pl.ds(pl.multiple_of(i * HALF, HALF), HALF)
         tokens = m.tok[rows, :]
         linear = mm(tokens, part_hi) + mm(tokens, part_mid) + mm(tokens, part_lo)
-        u = jax.nn.sigmoid(linear + offset_u)
-        w = jax.nn.sigmoid(pltpu.roll(linear, LANES - 8, 1) + offset_w)
-        m.gu[rows, :] = u
-        m.gw[rows, :] = w
-        m.gate[rows, :] = u * (w * scale - 1.0) + 2.0
+        both = jax.nn.sigmoid(linear + jnp.where(lane < 8, offset_u, offset_w))
+        m.gu[rows, :] = both
+        m.gate[rows, :] = both * (pltpu.roll(both, LANES - 8, 1) * scale - 1.0) + 2.0
 
     loop(4, gate_chunk)
 
-    gather_pass(0, m.wqkv)
-    gather_end(0, m.wqkv)
-    gather_start(1, m.wo)
-    gather_start(2, m.wup)
-    gather_start(3, m.wdown)
+    line_end(0)
+    gather_x(1)
+    line_start(2, 2)
+    gather_x(2)
 
     def project(i):
         rows = pl.ds(pl.multiple_of(i * HALF, HALF), HALF)
         both = mm(m.tok[rows, :], m.wqkv[...]) + vecs[7:8, 0:qkv_pad]
         query = both[:, 0:head_cols].astype(BF16)
         m.q[rows, :] = (query.astype(F32) * 0.125).astype(BF16)
-        m.k[rows, :] = both[:, head_cols : 2 * head_cols].astype(BF16)
-        m.v[rows, :] = both[:, 2 * head_cols : 3 * head_cols].astype(BF16)
+        key = both[:, head_cols : 2 * head_cols].astype(BF16)
+        value = both[:, 2 * head_cols : 3 * head_cols].astype(BF16)
+        m.k[rows, :] = key
+        m.v[rows, :] = value
+        m.kt[:, rows] = key.T
+        m.vt[:, rows] = value.T
 
     loop(4, project)
 
@@ -742,8 +827,18 @@
     head_masks = [jnp.where(head_of == h, 1.0, 0.0) for h in range(heads)]
     low_masks = [m.astype(BF16) for m in head_masks]
 
-    def attend(b):
-        keys = m.k[b * BUCKET_SLOTS : (b + 1) * BUCKET_SLOTS, :]
+    def hooked(first, count, chunk, hooks):
+        def step_of(i):
+            step = i + first
+            chunk(step)
+            for at, action in hooks.items():
+                if first <= at < first + count:
+                    when(step == at, action)
+
+        loop(count, step_of)
+
+    def attend(b, hooks):
+        keys = m.kt[:, b * BUCKET_SLOTS : (b + 1) * BUCKET_SLOTS]
         values = m.v[b * BUCKET_SLOTS : (b + 1) * BUCKET_SLOTS, :]
 
         def chunk(i):
@@ -754,7 +849,7 @@
             gates = m.gate[rows, :]
             context = jnp.zeros((CHUNK, head_cols), F32)
             for h in range(heads):
-                scores = mm_nt(query * low_masks[h], keys)
+                scores = mm(query * low_masks[h], keys)
                 scores = scores + gates[:, h : h + 1] * m.band[h, :, window]
                 scores = scores + m.mbias[b, local, :].astype(F32)
                 top = jnp.max(scores, axis=1, keepdims=True)
@@ -765,7 +860,7 @@
                 context = context + mm(probability.astype(BF16), values) * head_masks[h]
             m.ctx[rows, :] = context.astype(BF16)
 
-        loop(BUCKET_SLOTS // CHUNK, chunk)
+        hooked(0, BUCKET_SLOTS // CHUNK, chunk, hooks)
 
     core_sent = {}
     y_sent = {}
@@ -773,44 +868,34 @@
     def exchange(phase, b, product):
         other = b * BUCKET_SLOTS + (1 - c) * HALF
         own = b * BUCKET_SLOTS + c * HALF
-        if (phase - 1, b) in core_sent:
-            core_sent[(phase - 1, b)].wait_send()
-            y_sent[(phase - 1, b)].wait_send()
-
-        def send_chunk(i):
-            at = pl.ds(pl.multiple_of(i * CHUNK, CHUNK), CHUNK)
+        for cp in core_sent.get((phase - 1, b), []) + y_sent.get((phase - 1, b), []):
+            cp.wait_send()
+        for i in range(2):
+            at = slice(i * CHUNK, (i + 1) * CHUNK)
             rows = pl.ds(pl.multiple_of(other + i * CHUNK, CHUNK), CHUNK)
             m.cs[b, at, :] = product(rows).astype(BF16)
-
-        loop(HALF // CHUNK, send_chunk)
-        cp = remote(
-            m.cs.at[b], m.cr.at[b], m.s_cs.at[phase, b], m.s_cr.at[phase, b], core_dev
-        )
-        cp.start()
-        core_sent[(phase, b)] = cp
-
-        def own_chunk(i):
-            at = pl.ds(pl.multiple_of(i * CHUNK, CHUNK), CHUNK)
+            cp = remote(
+                m.cs.at[b, at], m.cr.at[b, at], m.s_cs.at[phase, b, i], m.s_cr.at[phase, b, i], core_dev
+            )
+            cp.start()
+            core_sent.setdefault((phase, b), []).append(cp)
+        for i in range(2):
+            at = slice(i * CHUNK, (i + 1) * CHUNK)
             rows = pl.ds(pl.multiple_of(own + i * CHUNK, CHUNK), CHUNK)
             m.ownf[at, :] = product(rows)
-
-        loop(HALF // CHUNK, own_chunk)
-        cp.wait_recv()
-
-        def add_chunk(i):
-            at = pl.ds(pl.multiple_of(i * CHUNK, CHUNK), CHUNK)
+        for i in range(2):
+            at = slice(i * CHUNK, (i + 1) * CHUNK)
+            core_sent[(phase, b)][i].wait_recv()
             m.ys[b, at, :] = (m.ownf[at, :] + m.cr[b, at, :].astype(F32)).astype(BF16)
-
-        loop(HALF // CHUNK, add_chunk)
-        cp = remote(
-            m.ys.at[b],
-            m.yr.at[phase % 2, b],
-            m.s_ys.at[phase, b],
-            m.s_yr.at[phase, b],
-            y_dev,
-        )
-        cp.start()
-        y_sent[(phase, b)] = cp
+            cp = remote(
+                m.ys.at[b, at],
+                m.yr.at[phase % 2, b, at],
+                m.s_ys.at[phase, b, i],
+                m.s_yr.at[phase, b, i],
+                y_dev,
+            )
+            cp.start()
+            y_sent.setdefault((phase, b), []).append(cp)
 
     def arrived(phase, b, at):
         return m.ys[b, at, :].astype(F32) + m.yr[phase % 2, b, at, :].astype(F32)
@@ -820,15 +905,23 @@
 
     core_spread = {}
 
-    def spread_start(which, buf, b):
-        rows = pl.ds(pl.multiple_of(b * BUCKET_SLOTS + c * HALF, HALF), HALF)
-        part = buf.at[rows]
-        cp = remote(part, part, m.s_as.at[which, b], m.s_ar.at[which, b], core_dev)
+    def spread(which, buf, b, i):
+        part = buf.at[own_rows(b, i)]
+        cp = remote(part, part, m.s_as.at[which, b, i], m.s_ar.at[which, b, i], core_dev)
         cp.start()
-        core_spread[(which, b)] = cp
-
-    def spread_end(which, b):
-        core_spread[(which, b)].wait_recv()
+        core_spread.setdefault((which, b), []).append(cp)
+
+    spread_done = set()
+
+    def spread_end(which, b, i):
+        if (which, b, i) not in spread_done:
+            core_spread[(which, b)][i].wait_recv()
+            spread_done.add((which, b, i))
+
+    def as_it_lands(phase, b, chunk):
+        for i in range(2):
+            y_sent[(phase, b)][i].wait_recv()
+            chunk(i)
 
     def row_mean(values):
         return jnp.mean(values, axis=1, keepdims=True)
@@ -837,7 +930,6 @@
         m.acc[at : at + 1, 0 : values.shape[1]] += jnp.sum(values, axis=0, keepdims=True)
 
     def norm_one(b):
-        y_sent[(0, b)].wait_recv()
 
         def chunk(i):
             at = pl.ds(pl.multiple_of(i * CHUNK, CHUNK), CHUNK)
@@ -851,21 +943,28 @@
             m.rstd1[b, at, :] = jnp.broadcast_to(rstd, (CHUNK, LANES))
             m.held[b, at, :] = normed
             m.nb[rows, :] = normed.astype(BF16)
-
-        loop(HALF // CHUNK, chunk)
-        spread_start(0, m.nb, b)
+            spread(0, m.nb, b, i)
+
+        as_it_lands(0, b, chunk)
+
+    def own_first(which, b, chunk):
+        def rows_at(step):
+            i = lax.rem(step + 2 * c, 4)
+            return pl.ds(pl.multiple_of(b * BUCKET_SLOTS + i * CHUNK, CHUNK), CHUNK)
+
+        loop(2, lambda step: chunk(rows_at(step)))
+        for i in range(2):
+            spread_end(which, b, i)
+            chunk(rows_at(2 + i))
 
     def feed(b):
-        spread_end(0, b)
-
-        def chunk(i):
-            rows = pl.ds(pl.multiple_of(b * BUCKET_SLOTS + i * CHUNK, CHUNK), CHUNK)
+        def chunk(rows):
             up = mm(m.nb[rows, :], m.wup[...]) + vecs[6:7, :]
             half_phi = 0.5 * (1.0 + lax.erf(up * INV_SQRT2))
             m.act[rows, :] = (up * half_phi).astype(BF16)
             m.gelup[rows, :] = half_phi + up * (jnp.exp(up * up * -0.5) * INV_SQRT_2PI)
 
-        loop(BUCKET_SLOTS // CHUNK, chunk)
+        own_first(0, b, chunk)
 
     out_copies = []
 
@@ -879,7 +978,6 @@
         out_copies.append((here, there))
 
     def norm_two(b):
-        y_sent[(1, b)].wait_recv()
         cot_copies[b].wait()
 
         def chunk(i):
@@ -898,26 +996,22 @@
             m.held[b, at, :] = grad
             low = grad.astype(BF16)
             m.gffn[rows, :] = low
+            spread(1, m.gffn, b, i)
             add_row(5, low.astype(F32))
 
-        loop(HALF // CHUNK, chunk)
-        spread_start(1, m.gffn, b)
+        as_it_lands(1, b, chunk)
         result_rows(0, b, m.stage, bo_out)
 
     def feed_back(b):
-        spread_end(1, b)
-
-        def chunk(i):
-            rows = pl.ds(pl.multiple_of(b * BUCKET_SLOTS + i * CHUNK, CHUNK), CHUNK)
+        def chunk(rows):
             grad = mm(m.gffn[rows, :], m.wdown[...]) * m.gelup[rows, :]
             low = grad.astype(BF16)
             m.gub[rows, :] = low
             add_row(6, low.astype(F32))
 
-        loop(BUCKET_SLOTS // CHUNK, chunk)
+        own_first(1, b, chunk)
 
     def norm_one_back(b):
-        y_sent[(2, b)].wait_recv()
 
         def chunk(i):
             at = pl.ds(pl.multiple_of(i * CHUNK, CHUNK), CHUNK)
@@ -932,30 +1026,29 @@
             m.held[b, at, :] = grad
             low = grad.astype(BF16)
             m.gattn[rows, :] = low
+            spread(2, m.gattn, b, i)
             add_row(4, low.astype(F32))
 
-        loop(HALF // CHUNK, chunk)
-        spread_start(2, m.gattn, b)
-
-    def attend_back(b):
-        spread_end(2, b)
+        as_it_lands(2, b, chunk)
+
+    def attend_back(b, hooks):
         keys = m.k[b * BUCKET_SLOTS : (b + 1) * BUCKET_SLOTS, :]
-        values = m.v[b * BUCKET_SLOTS : (b + 1) * BUCKET_SLOTS, :]
-
-        def chunk(i):
+        values = m.vt[:, b * BUCKET_SLOTS : (b + 1) * BUCKET_SLOTS]
+
+        def chunk(step):
+            i = lax.rem(step + 2 * c, 4)
             local = pl.ds(pl.multiple_of(i * CHUNK, CHUNK), CHUNK)
             rows = pl.ds(pl.multiple_of(b * BUCKET_SLOTS + i * CHUNK, CHUNK), CHUNK)
             window = pl.ds(pl.multiple_of(BUCKET_SLOTS - i * CHUNK, CHUNK), BUCKET_SLOTS)
             place = pl.ds(pl.multiple_of(3 * CHUNK - i * CHUNK, CHUNK), BUCKET_SLOTS)
-            grad_context = mm(m.gattn[rows, :], m.wo[:, 0:head_cols]).astype(BF16)
+            grad_context = mm(m.gattn[rows, :], m.wo[...]).astype(BF16)
             m.dctx[rows, :] = grad_context
             gates = m.gate[rows, :]
             grad_query = jnp.zeros((CHUNK, head_cols), F32)
             grad_gates = jnp.zeros((CHUNK, LANES), F32)
             for h in range(heads):
-                grad_probs = mm_nt(grad_context * low_masks[h], values)
+                grad_probs = mm(grad_context * low_masks[h], values)
                 probability = m.prob[b * heads + h, local, :]
-                m.pbb[h, local, :] = probability.astype(BF16)
                 inner = jnp.sum(grad_probs * probability, axis=1, keepdims=True)
                 low = (probability * (grad_probs - inner)).astype(BF16)
                 m.gsb[h, local, :] = low
@@ -967,94 +1060,118 @@
             m.dqf[local, :] = grad_query * 0.125
             m.dgate[rows, :] = grad_gates
 
-        loop(BUCKET_SLOTS // CHUNK, chunk)
+        hooked(0, 2, chunk, hooks)
+        spread_end(2, b, 0)
+        spread_end(2, b, 1)
+        hooked(2, 2, chunk, hooks)
         all_rows = slice(b * BUCKET_SLOTS, (b + 1) * BUCKET_SLOTS)
         grad_key = jnp.zeros((BUCKET_SLOTS, head_cols), F32)
         grad_value = jnp.zeros((BUCKET_SLOTS, head_cols), F32)
         for h in range(heads):
             grad_key = grad_key + mm_tn(m.gsb[h], m.q[all_rows, :]) * head_masks[h]
-            grad_value = grad_value + mm_tn(m.pbb[h], m.dctx[all_rows, :]) * head_masks[h]
-        pieces = [m.dqf[...], grad_key, grad_value]
-        if qkv_pad > 3 * head_cols:
-            pieces.append(jnp.zeros((BUCKET_SLOTS, qkv_pad - 3 * head_cols), F32))
-        low = jnp.concatenate(pieces, axis=1).astype(BF16)
-        m.dqkv[all_rows, :] = low
+            probs = m.prob[b * heads + h].astype(BF16)
+            grad_value = grad_value + mm_tn(probs, m.dctx[all_rows, :]) * head_masks[h]
+        pad = jnp.zeros((BUCKET_SLOTS, qkv_pad - 3 * head_cols), F32)
+        low = jnp.concatenate([m.dqf[...], grad_key, grad_value, pad], axis=1).astype(BF16)
+        m.dqkv[all_rows, 0:qkv_pad] = low
         add_row(7, low.astype(F32))
 
         def gate_back(i):
             rows = pl.ds(pl.multiple_of(b * BUCKET_SLOTS + i * CHUNK, CHUNK), CHUNK)
             grad = m.dgate[rows, :]
             u = m.gu[rows, :]
-            w = m.gw[rows, :]
-            grad_u = grad * (w * scale - 1.0) * u * (1.0 - u)
-            grad_w = grad * u * scale * w * (1.0 - w)
-            grad_u = jnp.where(head_lane, grad_u, 0.0)
-            grad_w = jnp.where(head_lane, grad_w, 0.0)
-            m.dlin[rows, :] = grad_u + pltpu.roll(grad_w, 8, 1)
+            w = pltpu.roll(u, LANES - 8, 1)
+            grad_u = jnp.where(head_lane, grad * (w * scale - 1.0) * u * (1.0 - u), 0.0)
+            grad_w = jnp.where(head_lane, grad * u * scale * w * (1.0 - w), 0.0)
             add_row(8, jnp.where(head_lane, grad * u * w, 0.0))
+            linear = grad_u + pltpu.roll(grad_w, 8, 1)
+            add_row(9, linear)
+            hi = linear.astype(BF16).astype(F32)
+            mid = (linear - hi).astype(BF16).astype(F32)
+            lo = (linear - hi - mid).astype(BF16).astype(F32)
+            stacked = hi
+            for at, part in enumerate((mid, lo, hi, mid, hi)):
+                stacked = stacked + pltpu.roll(part, 16 * (at + 1), 1)
+            m.dqkv[rows, qkv_pad : qkv_pad + LANES] = stacked.astype(BF16)
 
         loop(BUCKET_SLOTS // CHUNK, gate_back)
 
     def input_part(rows):
-        return mm_nt(m.dqkv[rows, :], m.wqkv[...]) + exact_nt(m.dlin[rows, :], m.gmat[...])
+        return mm(m.dqkv[rows, :], m.wqkvt[...])
 
     def token_rows(b):
-        y_sent[(3, b)].wait_recv()
+        for cp in out_copies[b]:
+            cp.wait()
 
         def chunk(i):
             at = pl.ds(pl.multiple_of(i * CHUNK, CHUNK), CHUNK)
             total = arrived(3, b, at) + DEEP_ALPHA * m.held[b, at, :]
-            m.tstage[b, at, :] = total.astype(BF16)
-
-        loop(HALF // CHUNK, chunk)
-        result_rows(1, b, m.tstage, tg_out)
-
-    def weight_grad(which, buf, left, right, width):
-        for cp in gathers.pop(which):
-            cp.wait_send()
+            m.stage[b, at, :] = total.astype(BF16)
+
+        as_it_lands(3, b, chunk)
+        result_rows(1, b, m.stage, tg_out)
+
+    def weight_grad(sent, left, right, put_part, rows=slice(None)):
+        for which in sent:
+            sent_all(which)
 
         def chunk(i):
             cols = pl.ds(pl.multiple_of(i * HALF, HALF), HALF)
-            part = mm_tn(left[:, cols], right[...])
-            if width < buf.shape[1]:
-                part = jnp.concatenate([part, jnp.zeros((HALF, buf.shape[1] - width), F32)], axis=1)
+            put_part(cols, mm_tn(left[rows, cols], right[rows, :]))
+
+        loop(W // HALF, chunk)
+
+    def add_whole(buf):
+        def put_part(cols, part):
+            buf[cols, :] = (buf[cols, :].astype(F32) + part).astype(BF16)
+
+        return put_part
+
+    def put_whole(buf):
+        def put_part(cols, part):
             buf[cols, :] = part.astype(BF16)
 
-        loop(W // HALF, chunk)
+        return put_part
+
+    def put_qkv(cols, part):
+        m.wqkv[cols, 0 : 3 * head_cols] = part[:, 0 : 3 * head_cols].astype(BF16)
+        m.glin[cols, :] = part[:, qkv_pad : qkv_pad + LANES]
+
+    def put_o(cols, part):
+        m.wqkv[cols, 3 * head_cols : qkv_pad] = part[:, 0:first_o].astype(BF16)
+        m.go[cols, :] = part[:, first_o:head_cols].astype(BF16)
 
     reduces = []
 
+    pass_order = z_order + [0]
+
     def reduce_start(which, buf, land):
-        for zt in range(nz):
-            cp = remote(
-                buf.at[block(2 * zt + 1 - x)],
-                land.at[zt],
-                m.s_xs.at[which, zt],
-                m.s_xr.at[which, zt],
-                x_dev,
-            )
-            cp.start()
-            reduces.append(cp)
-
-    def reduce_pass(which, buf, land, out, arrive, share):
-        for k in list(range(1, nz)) + [0]:
-            zt = z_at(k)
-            here = land.at[zt]
-            remote(here, here, m.s_xs.at[which, zt], m.s_xr.at[which, zt], x_dev).wait_recv()
-            total = buf[block(2 * zt + x), :].astype(F32) + land[zt].astype(F32)
-            if k == 0:
-                share[...] = total
-            else:
-                out[k - 1] = total.astype(BF16)
-                cp = remote(
-                    out.at[k - 1],
-                    arrive.at[k - 1],
-                    m.s_zs.at[which, k],
-                    m.s_zr.at[which, k],
-                    z_dev(k),
-                )
-                cp.start()
-                reduces.append(cp)
+        for k in pass_order:
+
+            def where(k=k):
+                rows = block(2 * z_at(k) + 1 - x)
+                return buf.at[rows], land.at[k], m.s_xs.at[which, k], m.s_xr.at[which, k], x_dev
+
+            launch(reduces, where)
+
+    def reduce_block(k, which, buf, land, out, arrive, share):
+        here = land.at[k]
+        remote(here, here, m.s_xs.at[which, k], m.s_xr.at[which, k], x_dev).wait_recv()
+        total = buf[block(2 * z_at(k) + x), :].astype(F32) + land[k].astype(F32)
+        if k == 0:
+            share[...] = total
+        else:
+            out[k - 1] = total.astype(BF16)
+
+            def where():
+                start = out.at[k - 1]
+                return start, arrive.at[k - 1], m.s_zs.at[which, k], m.s_zr.at[which, k], z_dev(k)
+
+            launch(reduces, where)
+
+    def reduce_pass(*matrix):
+        for k in pass_order:
+            reduce_block(k, *matrix)
 
     def reduce_end(which, arrive, share):
         total = share[...]
@@ -1072,47 +1189,89 @@
             tile = tile + folded[8 * i : 8 * i + 8, :]
         return tile
 
-    attend(0)
-    gather_pass(1, m.wo)
-    gather_end(1, m.wo)
-    out_product = lambda rows: mm_nt(m.ctx[rows, :], m.wo[:, 0:head_cols])
+    def pass_on(which):
+        line_step(which, 1, 2)
+        line_step(which, 2, 2)
+
+    def pass_last(which):
+        for step in range(3, nz):
+            line_step(which, step, 2)
+
+    line_start(3, 2)
+    gather_x(3)
+
+    def first_pass():
+        pass_on(1)
+        line_start(4, 2)
+        gather_x(4)
+
+    def second_pass():
+        pass_last(1)
+        pass_on(2)
+        line_start(5, 2)
+        gather_x(5)
+
+    attend(0, {0: first_pass, 2: second_pass})
+    pass_last(2)
+    line_end(1)
+    turn(m.wqkv, m.wqkvt)
+    m.wo[...] = jnp.concatenate([m.wqkv[:, 3 * head_cols : qkv_pad], m.wo1[...]], axis=1)
+    m.wot[0:first_o, :] = m.wqkvt[3 * head_cols : qkv_pad, :]
+    m.wot[first_o:head_cols, :] = m.wo1[...].T
+    out_product = lambda rows: mm(m.ctx[rows, :], m.wot[...])
     exchange(0, 0, out_product)
-    attend(1)
-    gather_pass(2, m.wup)
+    attend(1, {0: lambda: pass_on(3), 1: lambda: pass_last(3), 2: lambda: pass_on(4), 3: lambda: pass_last(4)})
+    pass_on(5)
     exchange(0, 1, out_product)
-    gather_pass(3, m.wdown)
+    pass_last(5)
     norm_one(0)
-    gather_end(2, m.wup)
+    line_end(2)
+    line_end(3)
     feed(0)
-    gather_end(3, m.wdown)
-    down_product = lambda rows: mm_nt(m.act[rows, :], m.wdown[...])
+    line_end(4)
+    line_end(5)
+    turn(m.wdown, m.wdownt)
+    down_product = lambda rows: mm(m.act[rows, :], m.wdownt[...])
     exchange(1, 0, down_product)
     norm_one(1)
     feed(1)
     exchange(1, 1, down_product)
-    up_product = lambda rows: mm_nt(m.gub[rows, :], m.wup[...])
+    turn(m.wup, m.wupt)
+    up_product = lambda rows: mm(m.gub[rows, :], m.wupt[...])
     norm_two(0)
     feed_back(0)
     exchange(2, 0, up_product)
+    first_rows, last_rows = slice(0, BUCKET_SLOTS), slice(BUCKET_SLOTS, 2 * BUCKET_SLOTS)
+    weight_grad((), m.gffn, m.act, put_whole(m.wdownt), first_rows)
+    weight_grad((2, 3), m.nb, m.gub, put_whole(m.wup), first_rows)
     norm_two(1)
     feed_back(1)
+    weight_grad((), m.gffn, m.act, add_whole(m.wdownt), last_rows)
+    reduce_start(0, m.wdownt, m.xrdown)
     exchange(2, 1, up_product)
-    weight_grad(3, m.wdown, m.gffn, m.act, hidden)
-    reduce_start(0, m.wdown, m.xrdown)
-    weight_grad(2, m.wup, m.nb, m.gub, hidden)
+    weight_grad((), m.nb, m.gub, add_whole(m.wup), last_rows)
     reduce_start(1, m.wup, m.xrup)
+    down = (0, m.wdownt, m.xrdown, m.zsdown, m.zrdown, sh_down)
+    up = (1, m.wup, m.xrup, m.zsup, m.zrup, sh_up)
+    out = (2, m.go, m.xro, m.zso, m.zro, sh_o)
+    qkv = (3, m.wqkv, m.xrqkv, m.zsqkv, m.zrqkv, sh_qkv)
     norm_one_back(0)
-    attend_back(0)
+    blocks = lambda ks, matrix: lambda: [reduce_block(k, *matrix) for k in ks] and None
+    early = [pass_order[0:1], pass_order[1:2], pass_order[2:-1]]
+    attend_back(0, {1 + i: blocks(ks, down) for i, ks in enumerate(early)})
     exchange(3, 0, input_part)
-    reduce_pass(0, m.wdown, m.xrdown, m.zsdown, m.zrdown, sh_down)
+    reduce_block(0, *down)
     norm_one_back(1)
-    attend_back(1)
+    spread_end(2, 1, 0)
+    spread_end(2, 1, 1)
+    weight_grad((0, 1), m.gattn, m.ctx, put_o)
+    reduce_start(2, m.go, m.xro)
+    attend_back(1, {i: blocks(ks, up) for i, ks in zip((0, 2, 3), early)})
+    weight_grad((), m.tok, m.dqkv, put_qkv)
+    reduce_start(3, m.wqkv, m.xrqkv)
+    reduce_block(0, *up)
+    reduce_pass(*out)
     exchange(3, 1, input_part)
-    weight_grad(0, m.wqkv, m.tok, m.dqkv, qkv_pad)
-    reduce_start(3, m.wqkv, m.xrqkv)
-    reduce_pass(1, m.wup, m.xrup, m.zsup, m.zrup, sh_up)
-    weight_grad(1, m.wo, m.gattn, m.ctx, head_cols)
-    reduce_start(2, m.wo, m.xro)
 
     sm = m.sm
     acc = m.acc
@@ -1152,26 +1311,15 @@
         table_grad = table_grad + exact_nt(hot_row, hot_lane)
     sm[0, TABLE_ROW : TABLE_ROW + 30, :] = table_grad[0:30, :]
 
-    lin = m.dlin[...]
-    lin_hi = lin.astype(BF16)
-    lin_rest = lin - lin_hi.astype(F32)
-    lin_mid = lin_rest.astype(BF16)
-    lin_lo = (lin_rest - lin_mid.astype(F32)).astype(BF16)
-    lin_grad = mm_tn(lin_hi, m.tok[...]) + mm_tn(lin_mid, m.tok[...]) + mm_tn(lin_lo, m.tok[...])
-    group = iota((16, W), 0)
-    mine_here = (lax.rem(group, 8) < heads) & (
-        lax.div(iota((16, W), 1), HD) == T * heads + lax.rem(group, 8)
-    )
-    lin_grad = jnp.where(mine_here, lin_grad[0:16, :], 0.0)
-    hot = jnp.where(lax.rem(col, HD) == lax.div(col_lane, 2), 1.0, 0.0)
-    folded = exact_mm(lin_grad, hot)
-    by_lane = jnp.where(
-        lax.rem(lane, 2) == 0,
-        jnp.sum(folded[0:8, :], axis=0, keepdims=True),
-        jnp.sum(folded[8:16, :], axis=0, keepdims=True),
-    )
-    sm[0, GATE_ROW : GATE_ROW + 1, :] = by_lane
-    lin_total = jnp.sum(lin, axis=0, keepdims=True)
+    lin_grad = m.glin[...]
+    lin_grad = lin_grad + pltpu.roll(lin_grad, LANES - 16, 1) + pltpu.roll(lin_grad, LANES - 32, 1)
+    lin_grad = jnp.where(own_head, lin_grad, 0.0)
+    grad_u = jnp.sum(jnp.where(col_lane < 8, lin_grad, 0.0), axis=1, keepdims=True)
+    grad_w = jnp.sum(jnp.where(col_lane >= 8, lin_grad, 0.0), axis=1, keepdims=True)
+    by_lane = jnp.where(col_lane == 2 * col_in_head, grad_u, 0.0)
+    by_lane = by_lane + jnp.where(col_lane == 2 * col_in_head + 1, grad_w, 0.0)
+    sm[0, GATE_ROW : GATE_ROW + 1, :] = jnp.sum(by_lane, axis=0, keepdims=True)
+    lin_total = acc[9:10, 0:LANES]
     total_u = jnp.sum(jnp.where(lane < 8, lin_total, 0.0), axis=1, keepdims=True)
     total_w = jnp.sum(jnp.where((lane >= 8) & (lane < 16), lin_total, 0.0), axis=1, keepdims=True)
     last = jnp.where(lane == 0, total_u, 0.0) + jnp.where(lane == 1, total_w, 0.0)
@@ -1189,17 +1337,19 @@
         small_sent.append(cp)
         return cp
 
-    token_rows(0)
     small_copy = small_step(0, core_dev)
+    for k in pass_order[0:1]:
+        reduce_block(k, *qkv)
     small_copy.wait_recv()
     sm[1] = sm[0] + m.smr[0]
     small_copy = small_step(1, y_dev)
-    reduce_pass(3, m.wqkv, m.xrqkv, m.zsqkv, m.zrqkv, sh_qkv)
+    for k in pass_order[1:-1]:
+        reduce_block(k, *qkv)
+    token_rows(0)
     small_copy.wait_recv()
     sm[2] = sm[1] + m.smr[1]
     small_copy = small_step(2, x_dev)
-    reduce_pass(2, m.wo, m.xro, m.zso, m.zro, sh_o)
-    token_rows(1)
+    reduce_block(0, *qkv)
     small_copy.wait_recv()
     sm[3] = sm[2] + m.smr[2]
     for k in range(1, nz):
@@ -1209,6 +1359,7 @@
         cp.start()
         small_sent.append(cp)
     m.smz[z] = sm[3]
+    token_rows(1)
     squares = reduce_end(0, m.zrdown, sh_down)
     squares = squares + reduce_end(1, m.zrup, sh_up)
     squares = squares + reduce_end(2, m.zro, sh_o)
@@ -1228,7 +1379,9 @@
     small_total = m.smz[0]
     for i in range(1, nz):
         small_total = small_total + m.smz[i]
-    small_out[...] = small_total
+    for i in range(3):
+        small_out[i] = small[i * SMALL_ROWS : (i + 1) * SMALL_ROWS, :]
+    small_out[3] = small_total
     small_square = small_total * small_total
     small_tile = jnp.zeros((8, LANES), F32)
     for i in range(SMALL_ROWS // 8):
@@ -1253,32 +1406,65 @@
     sum_all = jnp.sum(jnp.sum(everything, axis=0, keepdims=True), axis=1, keepdims=True)
     norm_out[...] = jnp.broadcast_to(jnp.sqrt(sum_all), (8, LANES))
 
-    for cp in reduces + small_sent + tail_sent:
+    for which in list(gathers):
+        sent_all(which)
+    for where in reduces:
+        remote(*where()).wait_send()
+    for cp in small_sent + tail_sent:
         cp.wait_send()
-    for cp in core_spread.values():
-        cp.wait_send()
+    for sent in core_spread.values():
+        for cp in sent:
+            cp.wait_send()
     for b in range(2):
-        core_sent[(3, b)].wait_send()
-        y_sent[(3, b)].wait_send()
-    for here, there in out_copies:
+        for cp in core_sent[(3, b)] + y_sent[(3, b)]:
+            cp.wait_send()
+    for here, there in out_copies[2:]:
         here.wait()
         there.wait()
 
 
-def adam_kernel(
-    head_cols,
-    sh_qkv, sh_o, sh_up, sh_down, sh_small, norm,
-    aw, am, av, fw, fm, fv, sw, sm, sv,
-    norm_out,
-    o_am, o_av, o_aw, o_ac, o_fm, o_fv, o_fw, o_fc, o_sm, o_sv, o_sw,
-):
+def adam_kernel(head_cols, *refs):
+    ins, rest = refs[:14], refs[14:]
+    block_in, token_in = ins[12:14]
+    outs, rest = rest[:14], rest[14:]
+    norm_out, block_out, token_out = outs[0], outs[12], outs[13]
+    held, made = rest[:12], rest[12:24]
+    block_held, token_held, s_in, s_out = rest[24:]
+    loads = [pltpu.make_async_copy(ins[i], held[i], s_in.at[i]) for i in range(12)]
+    for cp in loads:
+        cp.start()
+    passing = [
+        pltpu.make_async_copy(block_in, block_held, s_in.at[12]),
+        pltpu.make_async_copy(token_in, token_held, s_in.at[13]),
+    ]
+    passed = [
+        pltpu.make_async_copy(block_held, block_out, s_out.at[12]),
+        pltpu.make_async_copy(token_held, token_out, s_out.at[13]),
+    ]
+    for cp in passing:
+        cp.start()
+    stores = []
+
+    def store(i):
+        cp = pltpu.make_async_copy(made[i], outs[i], s_out.at[i])
+        cp.start()
+        stores.append(cp)
+
+    sh_qkv, sh_o, sh_up, sh_down, sh_small, norm, aw, am, av, fw, fm, fv = held
+    (o_norm, o_am, o_av, o_aw, o_ac, o_fm, o_fv, o_fw, o_fc, o_sm, o_sv, o_sw) = made
+    for i in (0, 1, 2, 3, 5):
+        loads[i].wait()
     length = norm[0:1, 0:1]
     factor = CLIP_LIMIT / jnp.maximum(length, CLIP_LIMIT)
+    o_norm[...] = jnp.broadcast_to(length, (8, LANES))
+    store(0)
+    for i in (6, 7, 8):
+        loads[i].wait()
     for i in range(4):
         if i < 3:
             grad = sh_qkv[:, i * head_cols : (i + 1) * head_cols]
         else:
-            grad = sh_o[:, 0:head_cols]
+            grad = jnp.concatenate([sh_qkv[:, 3 * head_cols :], sh_o[...]], axis=1)
         moment, square, master = adam_step(
             aw[i], am[i], av[i], factor * grad, RATE_MATRIX, WEIGHT_DECAY
         )
@@ -1286,6 +1472,13 @@
         o_av[i] = square
         o_aw[i] = master
         o_ac[i] = master.astype(BF16)
+    for i in (1, 2, 3, 4):
+        store(i)
+    for first, second in zip(passing, passed, strict=True):
+        first.wait()
+        second.start()
+    for i in (9, 10, 11):
+        loads[i].wait()
     for i, share in enumerate((sh_up, sh_down)):
         moment, square, master = adam_step(
             fw[i], fm[i], fv[i], factor * share[...], RATE_MATRIX, WEIGHT_DECAY
@@ -1294,15 +1487,23 @@
         o_fv[i] = square
         o_fw[i] = master
         o_fc[i] = master.astype(BF16)
-    moment, square, master = adam_step(sw[...], sm[...], sv[...], factor * sh_small[...], RATE_SMALL, 0.0)
+    for i in (5, 6, 7, 8):
+        store(i)
+    loads[4].wait()
+    moment, square, master = adam_step(
+        sh_small[0], sh_small[1], sh_small[2], factor * sh_small[3], RATE_SMALL, 0.0
+    )
     o_sm[...] = moment
     o_sv[...] = square
     o_sw[...] = master
-    norm_out[...] = jnp.broadcast_to(length, (8, LANES))
+    for i in (9, 10, 11):
+        store(i)
+    for cp in stores + passed:
+        cp.wait()
 
 
 def tiles(vector):
-    return jnp.pad(vector, (0, SMALL_ROWS * LANES - vector.shape[0])).reshape(SMALL_ROWS, LANES)
+    return jnp.pad(vector, (0, SMALL_ROWS * LANES - vector.shape[0]))
 
 
 def fused_body(
@@ -1327,10 +1528,15 @@
     hidden = feedforward_weights.shape[2]
     heads = head_cols // HD
     qkv_pad = -(-3 * head_cols // LANES) * LANES
-    out_pad = -(-head_cols // LANES) * LANES
     nz = n_dp // 2
-    small = tiles(small_params)
-    offsets = jnp.pad(rel_buckets, (0, 1)).reshape(2 * BUCKET_SLOTS // LANES, LANES)
+    packed = jnp.concatenate(
+        [
+            tiles(small_params),
+            tiles(small_first),
+            tiles(small_second),
+            jnp.pad(rel_buckets.astype(F32), (0, 1)),
+        ]
+    ).reshape(-1, LANES)
     keep = key_mask.reshape(rows // LANES, LANES)
     scratch = layer_scratch(owned, nz, qkv_pad, heads, head_cols, hidden)
     names = tuple(scratch)
@@ -1344,42 +1550,37 @@
             sds((rows, W), BF16),
             sds((rows, W), BF16),
             sds((owned, qkv_pad), F32),
-            sds((owned, out_pad), F32),
+            sds((owned, LANES), F32),
             sds((owned, hidden), F32),
             sds((owned, hidden), F32),
-            sds((SMALL_ROWS, LANES), F32),
+            sds((4, SMALL_ROWS, LANES), F32),
             sds((8, LANES), F32),
         ),
-        in_specs=[anywhere, anywhere, smem, vmem, vmem, vmem, vmem, vmem],
+        in_specs=[anywhere, anywhere, smem, vmem, vmem, vmem, vmem],
         out_specs=(anywhere, anywhere, vmem, vmem, vmem, vmem, vmem, vmem),
         scratch_shapes=list(scratch.values()),
         compiler_params=pltpu.CompilerParams(
-            collective_id=1, has_side_effects=True, vmem_limit_bytes=60 * 1024 * 1024
+            collective_id=1, has_side_effects=True, vmem_limit_bytes=62 * 1024 * 1024
         ),
         name="layer",
-    )(tokens, cotangent, clip_lengths, keep, offsets, attention_weights, feedforward_weights, small)
+    )(tokens, cotangent, clip_lengths, keep, attention_weights, feedforward_weights, packed)
     like = lambda a, dtype=F32: sds(a.shape, dtype)
-    results = pl.pallas_call(
-        partial(adam_kernel, head_cols),
-        out_shape=(
-            sds((8, LANES), F32),
-            like(attention_weights),
-            like(attention_weights),
-            like(attention_weights),
-            like(attention_weights, BF16),
-            like(feedforward_weights),
-            like(feedforward_weights),
-            like(feedforward_weights),
-            like(feedforward_weights, BF16),
-            sds((SMALL_ROWS, LANES), F32),
-            sds((SMALL_ROWS, LANES), F32),
-            sds((SMALL_ROWS, LANES), F32),
-        ),
-        in_specs=[vmem] * 15,
-        out_specs=(vmem,) * 12,
-        compiler_params=pltpu.CompilerParams(vmem_limit_bytes=32 * 1024 * 1024),
-        name="adam",
-    )(
+    small_like = sds((SMALL_ROWS, LANES), F32)
+    made = (
+        sds((8, LANES), F32),
+        like(attention_weights),
+        like(attention_weights),
+        like(attention_weights),
+        like(attention_weights, BF16),
+        like(feedforward_weights),
+        like(feedforward_weights),
+        like(feedforward_weights),
+        like(feedforward_weights, BF16),
+        small_like,
+        small_like,
+        small_like,
+    )
+    operands = (
         sh_qkv,
         sh_o,
         sh_up,
@@ -1392,10 +1593,22 @@
         feedforward_weights,
         feedforward_first,
         feedforward_second,
-        small,
-        tiles(small_first),
-        tiles(small_second),
-    )
+        block_rows,
+        token_rows,
+    )
+    in_vmem = lambda a: pltpu.VMEM(a.shape, a.dtype)
+    results = pl.pallas_call(
+        partial(adam_kernel, head_cols),
+        out_shape=(*made, like(tokens, BF16), like(tokens, BF16)),
+        in_specs=[anywhere] * len(operands),
+        out_specs=(anywhere,) * (len(made) + 2),
+        scratch_shapes=[in_vmem(a) for a in operands[:12]]
+        + [in_vmem(a) for a in made]
+        + [in_vmem(tokens), in_vmem(tokens)]
+        + [pltpu.SemaphoreType.DMA((14,)), pltpu.SemaphoreType.DMA((14,))],
+        compiler_params=pltpu.CompilerParams(vmem_limit_bytes=62 * 1024 * 1024),
+        name="adam",
+    )(*operands)
     length = small_params.shape[0]
     flat = lambda a: a.reshape(-1)[:length]
     return (
@@ -1404,8 +1617,7 @@
         flat(results[9]),
         flat(results[10]),
         flat(results[11]),
-        block_rows,
-        token_rows,
+        *results[12:],
     )
 
 

time: 189 us -> 148 us (0.78)
  Pallas kernels: 176 us -> 144 us
  local copies, waits for them, and re-layouts: 12.5 us -> 1.18 us
  other arithmetic: 0 us -> 2.23 us
    pallas_call x1, Pallas kernels: 173 us -> 138 us  [fused_body(): pl.pallas_call(partial(layer_kernel, names, (n_dp, owned, qkv_pad, heads,...]
    unnamed x32 -> x0, local copies, waits for them, and re-layouts: 8.39 us -> none
    reshape x3 -> x0, local copies, waits for them, and re-layouts: 3.56 us -> none  [the longest x2 2.28 us: tiles(): jnp.pad(vector, (0, SMALL_ROWS * LANES - vector.shape[0]))]
    pallas_call x1, Pallas kernels: 3.03 us -> 5.69 us  [fused_body(): pl.pallas_call(partial(adam_kernel, head_cols), out_shape=(*made, like(to...]
where the time goes in v2:
time: 148 us
  Pallas kernels  144 us (97%)
  other arithmetic  2.23 us (2%)
    pallas_call x1, Pallas kernels, fused_body(): pl.pallas_call(partial(layer_kernel, names, (n_dp, owned, qkv_pad, heads,...  138 us
    pallas_call x1, Pallas kernels, fused_body(): pl.pallas_call(partial(adam_kernel, head_cols), out_shape=(*made, like(to...  5.69 us

profile of v2, /device:TPU:0, one launch (start us, length us, event | category | flops | bytes accessed | tf_op | source)
XLA Modules:
  0.0 148.1 jit_solution(4749012252937462674)
XLA Ops:
  0.6 0.7 convert_element_type.9
  1.3 1.5 %fusion.refs_6_ = f32[320,128]{1,0:T(8,128)} fusion(f32[1023]{0:T(1024)S(1)} %convert_element_type.9, f32[13198]{0:T(1024)} %param.27, f32[13198]{0:T(1024)} %param.26, f32[13198]{0:T(1024)} %param.25), kind=kLoop, calls=%fused_computation.5 | loop fusion | flops 614400 | bytes 326308 | tf_op jit(solution)/shard_map/reshape | solution.py:1539
  2.9 138.3 %layer.1 = (bf16[1024,768]{1,0:T(8,128)(2,1)}, bf16[1024,768]{1,0:T(8,128)(2,1)}, f32[96,640]{1,0:T(8,128)}, f32[96,128]{1,0:T(8,128)}, f32[96,768]{1,0:T(8,128)...) custom-call(bf16[1024,768]{1,0:T(8,128)(2,1)} %refs_0_.1, bf16[1024,768]{1,0:T(8,128)(2,1)} %refs_1_.1, ...), custom_call_target="tpu_custom_call" | custom-call | tf_op jit(solution)/shard_map/layer/pallas_call | solution.py:1547
  141.2 5.7 %adam.1 = (f32[8,128]{1,0:T(8,128)}, f32[4,96,192]{2,1,0:T(8,128)}, f32[4,96,192]{2,1,0:T(8,128)}, f32[4,96,192]{2,1,0:T(8,128)}, bf16[4,96,192]{2,1,0:T(8,128)(...) custom-call(f32[96,640]{1,0:T(8,128)} %get-tuple-element.36.refs_0_,, ...), custom_call_target="tpu_custom_call" | custom-call | tf_op jit(solution)/shard_map/adam/pallas_call | solution.py:1600
  146.9 1.2 slice.12

commit v3 on v2

--- a/solution.py
+++ b/solution.py
@@ -379,6 +379,8 @@
 MESH_ID = pl.DeviceIdType.MESH
 LANES = 128
 SMALL_ROWS = 104
+QUARTER = 32
+SUM_ROWS = 4 * QUARTER
 TABLE_ROW = 72
 GATE_ROW = 102
 OFFSET_ROW = 103
@@ -424,6 +426,15 @@
     dma = pltpu.SemaphoreType.DMA
     vm = pltpu.VMEM
     shapes = dict(
+        wa=vm((4, owned, head_cols), F32),
+        wf=vm((2, owned, hidden), F32),
+        keep=vm((rows // LANES, LANES), jnp.int32),
+        small=vm((3 * SMALL_ROWS + 2 * BUCKET_SLOTS // LANES, LANES), F32),
+        shqkv=vm((owned, qkv_pad), F32),
+        sho=vm((owned, LANES), F32),
+        shup=vm((owned, hidden), F32),
+        shdown=vm((owned, hidden), F32),
+        smallout=vm((4, SMALL_ROWS, LANES), F32),
         tok=vm((rows, W), BF16),
         cot=vm((2, HALF, W), BF16),
         wqkv=vm((W, qkv_pad), BF16),
@@ -441,19 +452,19 @@
         k=vm((rows, head_cols), BF16),
         v=vm((rows, head_cols), BF16),
         kt=vm((head_cols, rows), BF16),
+        qt=vm((head_cols, rows), BF16),
+        dctxt=vm((head_cols, BUCKET_SLOTS), BF16),
         vt=vm((head_cols, rows), BF16),
         ctx=vm((rows, head_cols), BF16),
-        dctx=vm((rows, head_cols), BF16),
         dqkv=vm((rows, qkv_pad + LANES), BF16),
         prob=vm((2 * heads, BUCKET_SLOTS, BUCKET_SLOTS), F32),
-        gsb=vm((heads, BUCKET_SLOTS, BUCKET_SLOTS), BF16),
+        gsb=vm((heads * BUCKET_SLOTS, BUCKET_SLOTS), BF16),
         dqf=vm((BUCKET_SLOTS, head_cols), F32),
         mbias=vm((2, BUCKET_SLOTS, BUCKET_SLOTS), BF16),
         band=vm((heads, LANES, 2 * BUCKET_SLOTS), F32),
         dband=vm((heads, LANES, 2 * BUCKET_SLOTS), F32),
         gate=vm((rows, LANES), F32),
         gu=vm((rows, LANES), F32),
-        dgate=vm((rows, LANES), F32),
         gmat=vm((W, LANES), F32),
         vecs=vm((16, W), F32),
         acc=vm((16, W), F32),
@@ -484,18 +495,24 @@
         zro=vm((nz - 1, owned, LANES), BF16),
         zrup=vm((nz - 1, owned, hidden), BF16),
         zrdown=vm((nz - 1, owned, hidden), BF16),
-        sm=vm((4, SMALL_ROWS, LANES), F32),
-        smr=vm((3, SMALL_ROWS, LANES), F32),
-        smz=vm((nz, SMALL_ROWS, LANES), F32),
+        sm=vm((SUM_ROWS, LANES), F32),
+        smc=vm((2, QUARTER, LANES), F32),
+        smh=vm((2, QUARTER, LANES), F32),
+        smy=vm((QUARTER, LANES), F32),
+        smv=vm((QUARTER, LANES), F32),
+        smx=vm((QUARTER, LANES), F32),
+        smz=vm((nz, QUARTER, LANES), F32),
+        sma=vm((SUM_ROWS, LANES), F32),
         sqt=vm((4, 8, LANES), F32),
         sqd=vm((2 * nz, 8, LANES), F32),
-        s_in=dma((3,)),
+        s_in=dma((7,)),
+        s_out=dma((5,)),
         s_gs=dma((6,)),
         s_gr=dma((6,)),
-        s_ls=dma((6, 2, nz)),
-        s_lr=dma((6, 2, nz)),
-        s_lxs=dma((6, 2, nz)),
-        s_lxr=dma((6, 2, nz)),
+        s_ls=dma((7, 2, nz)),
+        s_lr=dma((7, 2, nz)),
+        s_lxs=dma((7, 2, nz)),
+        s_lxr=dma((7, 2, nz)),
         s_cs=dma((4, 2, 2)),
         s_cr=dma((4, 2, 2)),
         s_ys=dma((4, 2, 2)),
@@ -509,8 +526,8 @@
         s_xr=dma((4, nz)),
         s_zs=dma((4, nz)),
         s_zr=dma((4, nz)),
-        s_ms=dma((3 + nz,)),
-        s_mr=dma((3 + nz,)),
+        s_ms=dma((6 + nz,)),
+        s_mr=dma((6 + nz,)),
         s_ts=dma((4,)),
         s_tr=dma((4,)),
         s_ds=dma((2 * nz,)),
@@ -522,8 +539,8 @@
 def layer_kernel(names, dims, *refs):
     n_dp, owned, qkv_pad, heads, head_cols, hidden = dims
     nz = n_dp // 2
-    (tok_in, cot_in, lens, keep, wa, wf, small) = refs[:7]
-    (bo_out, tg_out, sh_qkv, sh_o, sh_up, sh_down, small_out, norm_out) = refs[7:15]
+    (tok_in, cot_in, lens, keep_in, wa_in, wf_in, small_in) = refs[:7]
+    (bo_out, tg_out, out_qkv, out_o, out_up, out_down, out_small, norm_out) = refs[7:15]
     m = SimpleNamespace(**dict(zip(names, refs[15:], strict=True)))
     D = lax.axis_index("dp")
     T = lax.axis_index("tensor")
@@ -536,9 +553,12 @@
     x_dev = (z * 2 + 1 - x, T)
 
     def z_at(k):
-        return lax.rem(z + k, nz)
-
-    z_order = sorted(range(1, nz), key=lambda k: min(k, nz - k))
+        total, bit = 0, 1
+        while bit < nz:
+            here = lax.rem(lax.div(z, bit), 2)
+            total = total + bit * (1 - here if k & bit else here)
+            bit *= 2
+        return total
 
     def z_dev(k):
         return (z_at(k) * 2 + x, T)
@@ -558,6 +578,13 @@
     def block(owner):
         return pl.ds(pl.multiple_of(owner * owned, owned), owned)
 
+    wa, wf, keep, small = m.wa, m.wf, m.keep, m.small
+    sh_qkv, sh_o, sh_up, sh_down, small_out = m.shqkv, m.sho, m.shup, m.shdown, m.smallout
+    first_loads = []
+    for i, (source, target) in enumerate(((wa_in, wa), (wf_in, wf), (small_in, small), (keep_in, keep))):
+        cp = pltpu.make_async_copy(source, target, m.s_in.at[3 + i])
+        cp.start()
+        first_loads.append(cp)
     tok_copy = pltpu.make_async_copy(tok_in, m.tok, m.s_in.at[0])
     tok_copy.start()
     cot_copies = []
@@ -571,6 +598,8 @@
         pl.semaphore_signal(barrier, inc=1, device_id=(D, lax.rem(T + k, 4)), device_id_type=MESH_ID)
     for k in range(1, n_dp):
         pl.semaphore_signal(barrier, inc=1, device_id=(lax.rem(D + k, n_dp), T), device_id_type=MESH_ID)
+    for cp in first_loads:
+        cp.wait()
     mine = block(D)
     first_o = qkv_pad - 3 * head_cols
     m.wqkv[mine, :] = jnp.concatenate([wa[0], wa[1], wa[2], wa[3, :, 0:first_o]], axis=1).astype(BF16)
@@ -585,9 +614,14 @@
         pieces.append((buf, 0, part_rows))
         pieces.append((buf, owned - part_rows, part_rows))
 
-    def piece(which, owner):
+    pieces.append(pieces[-1])
+    across = len(pieces) - 1
+    straight = (across - 1, across)
+
+    def piece(which, owner_z, other_column=False):
         buf, first, count = pieces[which]
-        return buf.at[pl.ds(pl.multiple_of(owner * owned + first, 16), count)]
+        column = 1 - x if other_column != (which == across) else x
+        return buf.at[pl.ds(pl.multiple_of((owner_z * 2 + column) * owned + first, 16), count)]
 
     gathers = {}
 
@@ -610,7 +644,7 @@
         origin = step - hops
 
         def where():
-            part = piece(which, from_z(way, origin)[0] * 2 + x)
+            part = piece(which, from_z(way, origin)[0])
             target = ((z + hops if way == 0 else z - hops) * 2 + x, T)
             return part, part, m.s_ls.at[which, way, step], m.s_lr.at[which, way, step], target
 
@@ -627,7 +661,7 @@
 
     def gather_x(which):
         def where():
-            own = piece(which, D)
+            own = piece(which, z)
             return own, own, m.s_gs.at[which], m.s_gr.at[which], x_dev
 
         send_when(which, lambda: D >= 0, where)
@@ -636,28 +670,33 @@
         for way in range(2):
 
             def landed(way=way):
-                part = piece(which, from_z(way, step)[0] * 2 + x)
+                part = piece(which, from_z(way, step)[0])
                 sems = m.s_ls.at[which, way, step], m.s_lr.at[which, way, step]
                 remote(part, part, *sems, x_dev).wait_recv()
 
             when(from_z(way, step)[1], landed)
             if step >= hops and step + 1 < nz:
                 line_send(which, way, step + 1, 1)
+            if which in straight:
+                continue
 
             def where(way=way):
-                part = piece(which, from_z(way, step)[0] * 2 + x)
+                part = piece(which, from_z(way, step)[0])
                 return part, part, m.s_lxs.at[which, way, step], m.s_lxr.at[which, way, step], x_dev
 
             send_when(which, lambda way=way: from_z(way, step)[1], where)
 
+    def partner_landed(which):
+        part = piece(which, z, True)
+        remote(part, part, m.s_gs.at[which], m.s_gr.at[which], x_dev).wait_recv()
+
     def line_end(which):
-        part = piece(which, z * 2 + 1 - x)
-        remote(part, part, m.s_gs.at[which], m.s_gr.at[which], x_dev).wait_recv()
+        partner_landed(which)
         for step in range(1, nz):
             for way in range(2):
 
                 def landed(way=way):
-                    part = piece(which, from_z(way, step)[0] * 2 + 1 - x)
+                    part = piece(which, from_z(way, step)[0], True)
                     sems = m.s_lxs.at[which, way, step], m.s_lxr.at[which, way, step]
                     remote(part, part, *sems, x_dev).wait_recv()
 
@@ -669,6 +708,9 @@
 
     def turn(source, target):
         count = source.shape[1]
+        if count % LANES:
+            target[...] = source[...].T
+            return
         step = HALF if count % HALF == 0 else LANES
 
         def chunk(i):
@@ -679,6 +721,7 @@
 
     line_start(0, 1)
     gather_x(0)
+    gather_x(across - 1)
 
     def small_row(first, count):
         return jnp.concatenate([small[first + i : first + i + 1, :] for i in range(count)], axis=1)
@@ -804,16 +847,17 @@
 
     loop(4, gate_chunk)
 
+    line_start(2, 2)
     line_end(0)
     gather_x(1)
-    line_start(2, 2)
     gather_x(2)
 
     def project(i):
         rows = pl.ds(pl.multiple_of(i * HALF, HALF), HALF)
         both = mm(m.tok[rows, :], m.wqkv[...]) + vecs[7:8, 0:qkv_pad]
-        query = both[:, 0:head_cols].astype(BF16)
-        m.q[rows, :] = (query.astype(F32) * 0.125).astype(BF16)
+        query = (both[:, 0:head_cols].astype(BF16).astype(F32) * 0.125).astype(BF16)
+        m.q[rows, :] = query
+        m.qt[:, rows] = query.T
         key = both[:, head_cols : 2 * head_cols].astype(BF16)
         value = both[:, 2 * head_cols : 3 * head_cols].astype(BF16)
         m.k[rows, :] = key
@@ -837,6 +881,12 @@
 
         loop(count, step_of)
 
+    def by_head(stacked):
+        total = stacked[0:CHUNK, :] * head_masks[0]
+        for h in range(1, heads):
+            total = total + stacked[h * CHUNK : (h + 1) * CHUNK, :] * head_masks[h]
+        return total
+
     def attend(b, hooks):
         keys = m.kt[:, b * BUCKET_SLOTS : (b + 1) * BUCKET_SLOTS]
         values = m.v[b * BUCKET_SLOTS : (b + 1) * BUCKET_SLOTS, :]
@@ -847,9 +897,10 @@
             window = pl.ds(pl.multiple_of(BUCKET_SLOTS - i * CHUNK, CHUNK), BUCKET_SLOTS)
             query = m.q[rows, :]
             gates = m.gate[rows, :]
-            context = jnp.zeros((CHUNK, head_cols), F32)
+            all_scores = mm(jnp.concatenate([query * mask for mask in low_masks], axis=0), keys)
+            all_probs = []
             for h in range(heads):
-                scores = mm(query * low_masks[h], keys)
+                scores = all_scores[h * CHUNK : (h + 1) * CHUNK, :]
                 scores = scores + gates[:, h : h + 1] * m.band[h, :, window]
                 scores = scores + m.mbias[b, local, :].astype(F32)
                 top = jnp.max(scores, axis=1, keepdims=True)
@@ -857,8 +908,8 @@
                 total = jnp.sum(weight, axis=1, keepdims=True)
                 probability = weight * (1.0 / total)
                 m.prob[b * heads + h, local, :] = probability
-                context = context + mm(probability.astype(BF16), values) * head_masks[h]
-            m.ctx[rows, :] = context.astype(BF16)
+                all_probs.append(probability.astype(BF16))
+            m.ctx[rows, :] = by_head(mm(jnp.concatenate(all_probs, axis=0), values)).astype(BF16)
 
         hooked(0, BUCKET_SLOTS // CHUNK, chunk, hooks)
 
@@ -1031,6 +1082,22 @@
 
         as_it_lands(2, b, chunk)
 
+    def gate_back(rows, grad):
+        u = m.gu[rows, :]
+        w = pltpu.roll(u, LANES - 8, 1)
+        grad_u = jnp.where(head_lane, grad * (w * scale - 1.0) * u * (1.0 - u), 0.0)
+        grad_w = jnp.where(head_lane, grad * u * scale * w * (1.0 - w), 0.0)
+        add_row(8, jnp.where(head_lane, grad * u * w, 0.0))
+        linear = grad_u + pltpu.roll(grad_w, 8, 1)
+        add_row(9, linear)
+        hi = linear.astype(BF16).astype(F32)
+        mid = (linear - hi).astype(BF16).astype(F32)
+        lo = (linear - hi - mid).astype(BF16).astype(F32)
+        stacked = hi
+        for at, part in enumerate((mid, lo, hi, mid, hi)):
+            stacked = stacked + pltpu.roll(part, 16 * (at + 1), 1)
+        m.dqkv[rows, qkv_pad : qkv_pad + LANES] = stacked.astype(BF16)
+
     def attend_back(b, hooks):
         keys = m.k[b * BUCKET_SLOTS : (b + 1) * BUCKET_SLOTS, :]
         values = m.vt[:, b * BUCKET_SLOTS : (b + 1) * BUCKET_SLOTS]
@@ -1042,60 +1109,41 @@
             window = pl.ds(pl.multiple_of(BUCKET_SLOTS - i * CHUNK, CHUNK), BUCKET_SLOTS)
             place = pl.ds(pl.multiple_of(3 * CHUNK - i * CHUNK, CHUNK), BUCKET_SLOTS)
             grad_context = mm(m.gattn[rows, :], m.wo[...]).astype(BF16)
-            m.dctx[rows, :] = grad_context
+            m.dctxt[:, local] = grad_context.T
             gates = m.gate[rows, :]
-            grad_query = jnp.zeros((CHUNK, head_cols), F32)
+            all_grads = mm(jnp.concatenate([grad_context * mask for mask in low_masks], axis=0), values)
+            all_low = []
             grad_gates = jnp.zeros((CHUNK, LANES), F32)
             for h in range(heads):
-                grad_probs = mm(grad_context * low_masks[h], values)
+                grad_probs = all_grads[h * CHUNK : (h + 1) * CHUNK, :]
                 probability = m.prob[b * heads + h, local, :]
                 inner = jnp.sum(grad_probs * probability, axis=1, keepdims=True)
                 low = (probability * (grad_probs - inner)).astype(BF16)
-                m.gsb[h, local, :] = low
-                grad_query = grad_query + mm(low, keys) * head_masks[h]
+                m.gsb[pl.ds(pl.multiple_of(h * BUCKET_SLOTS + i * CHUNK, CHUNK), CHUNK), :] = low
+                all_low.append(low)
                 rounded = low.astype(F32)
                 one = jnp.sum(rounded * m.band[h, :, window], axis=1, keepdims=True)
                 grad_gates = grad_gates + jnp.where(lane == h, one, 0.0)
                 m.dband[h, :, place] += rounded * gates[:, h : h + 1]
-            m.dqf[local, :] = grad_query * 0.125
-            m.dgate[rows, :] = grad_gates
+            m.dqf[local, :] = by_head(mm(jnp.concatenate(all_low, axis=0), keys)) * 0.125
+            gate_back(rows, grad_gates)
 
         hooked(0, 2, chunk, hooks)
         spread_end(2, b, 0)
         spread_end(2, b, 1)
         hooked(2, 2, chunk, hooks)
         all_rows = slice(b * BUCKET_SLOTS, (b + 1) * BUCKET_SLOTS)
-        grad_key = jnp.zeros((BUCKET_SLOTS, head_cols), F32)
-        grad_value = jnp.zeros((BUCKET_SLOTS, head_cols), F32)
-        for h in range(heads):
-            grad_key = grad_key + mm_tn(m.gsb[h], m.q[all_rows, :]) * head_masks[h]
-            probs = m.prob[b * heads + h].astype(BF16)
-            grad_value = grad_value + mm_tn(probs, m.dctx[all_rows, :]) * head_masks[h]
+        own_rows_of = lax.div(iota((head_cols, 1), 0), HD)
+        row_masks = [jnp.where(own_rows_of == h, 1.0, 0.0).astype(BF16) for h in range(heads)]
+        spread_out = lambda turned: jnp.concatenate([turned * mask for mask in row_masks], axis=1)
+        grad_key = mm(spread_out(m.qt[:, all_rows]), m.gsb[...]).T
+        probs = m.prob[b * heads : (b + 1) * heads].reshape(heads * BUCKET_SLOTS, BUCKET_SLOTS)
+        grad_value = mm(spread_out(m.dctxt[...]), probs.astype(BF16)).T
         pad = jnp.zeros((BUCKET_SLOTS, qkv_pad - 3 * head_cols), F32)
         low = jnp.concatenate([m.dqf[...], grad_key, grad_value, pad], axis=1).astype(BF16)
         m.dqkv[all_rows, 0:qkv_pad] = low
         add_row(7, low.astype(F32))
 
-        def gate_back(i):
-            rows = pl.ds(pl.multiple_of(b * BUCKET_SLOTS + i * CHUNK, CHUNK), CHUNK)
-            grad = m.dgate[rows, :]
-            u = m.gu[rows, :]
-            w = pltpu.roll(u, LANES - 8, 1)
-            grad_u = jnp.where(head_lane, grad * (w * scale - 1.0) * u * (1.0 - u), 0.0)
-            grad_w = jnp.where(head_lane, grad * u * scale * w * (1.0 - w), 0.0)
-            add_row(8, jnp.where(head_lane, grad * u * w, 0.0))
-            linear = grad_u + pltpu.roll(grad_w, 8, 1)
-            add_row(9, linear)
-            hi = linear.astype(BF16).astype(F32)
-            mid = (linear - hi).astype(BF16).astype(F32)
-            lo = (linear - hi - mid).astype(BF16).astype(F32)
-            stacked = hi
-            for at, part in enumerate((mid, lo, hi, mid, hi)):
-                stacked = stacked + pltpu.roll(part, 16 * (at + 1), 1)
-            m.dqkv[rows, qkv_pad : qkv_pad + LANES] = stacked.astype(BF16)
-
-        loop(BUCKET_SLOTS // CHUNK, gate_back)
-
     def input_part(rows):
         return mm(m.dqkv[rows, :], m.wqkvt[...])
 
@@ -1143,10 +1191,29 @@
 
     reduces = []
 
-    pass_order = z_order + [0]
-
-    def reduce_start(which, buf, land):
-        for k in pass_order:
+    def low_bit(k):
+        return k & -k if k else nz
+
+    bits = [1 << i for i in range(nz.bit_length() - 1)]
+    slots = {}
+    for k in range(nz):
+        for bit in bits:
+            if bit < low_bit(k):
+                slots[(k, bit)] = len(slots)
+    pass_order = sorted(range(nz), key=lambda k: (low_bit(k), -k))
+
+    def add_landed(total, k, which, arrive):
+        for bit in bits:
+            if bit < low_bit(k):
+                slot = slots[(k, bit)]
+                here = arrive.at[slot]
+                sems = m.s_zs.at[which, slot], m.s_zr.at[which, slot]
+                remote(here, here, *sems, z_dev(bit)).wait_recv()
+                total = total + arrive[slot].astype(F32)
+        return total
+
+    def reduce_start(which, buf, land, ks=None):
+        for k in ks or pass_order:
 
             def where(k=k):
                 rows = block(2 * z_at(k) + 1 - x)
@@ -1161,11 +1228,13 @@
         if k == 0:
             share[...] = total
         else:
-            out[k - 1] = total.astype(BF16)
+            out[k - 1] = add_landed(total, k, which, arrive).astype(BF16)
 
             def where():
-                start = out.at[k - 1]
-                return start, arrive.at[k - 1], m.s_zs.at[which, k], m.s_zr.at[which, k], z_dev(k)
+                bit = low_bit(k)
+                slot = slots[(k - bit, bit)]
+                sems = m.s_zs.at[which, slot], m.s_zr.at[which, slot]
+                return out.at[k - 1], arrive.at[slot], *sems, z_dev(bit)
 
             launch(reduces, where)
 
@@ -1174,11 +1243,7 @@
             reduce_block(k, *matrix)
 
     def reduce_end(which, arrive, share):
-        total = share[...]
-        for k in range(1, nz):
-            here = arrive.at[k - 1]
-            remote(here, here, m.s_zs.at[which, k], m.s_zr.at[which, k], z_dev(k)).wait_recv()
-            total = total + arrive[k - 1].astype(F32)
+        total = add_landed(share[...], 0, which, arrive)
         share[...] = total
         squares = total * total
         folded = jnp.zeros((owned, LANES), F32)
@@ -1208,28 +1273,30 @@
     def second_pass():
         pass_last(1)
         pass_on(2)
+        partner_landed(5)
         line_start(5, 2)
-        gather_x(5)
+        line_start(6, 2)
 
     attend(0, {0: first_pass, 2: second_pass})
-    pass_last(2)
     line_end(1)
-    turn(m.wqkv, m.wqkvt)
     m.wo[...] = jnp.concatenate([m.wqkv[:, 3 * head_cols : qkv_pad], m.wo1[...]], axis=1)
-    m.wot[0:first_o, :] = m.wqkvt[3 * head_cols : qkv_pad, :]
-    m.wot[first_o:head_cols, :] = m.wo1[...].T
+    turn(m.wo, m.wot)
     out_product = lambda rows: mm(m.ctx[rows, :], m.wot[...])
     exchange(0, 0, out_product)
-    attend(1, {0: lambda: pass_on(3), 1: lambda: pass_last(3), 2: lambda: pass_on(4), 3: lambda: pass_last(4)})
+    pass_last(2)
+    attend(1, {1: lambda: pass_on(3), 3: lambda: pass_last(3)})
+    exchange(0, 1, out_product)
+    pass_on(4)
     pass_on(5)
-    exchange(0, 1, out_product)
-    pass_last(5)
     norm_one(0)
+    pass_last(4)
+    pass_on(6)
     line_end(2)
     line_end(3)
     feed(0)
+    pass_last(5)
+    pass_last(6)
     line_end(4)
-    line_end(5)
     turn(m.wdown, m.wdownt)
     down_product = lambda rows: mm(m.act[rows, :], m.wdownt[...])
     exchange(1, 0, down_product)
@@ -1237,6 +1304,7 @@
     feed(1)
     exchange(1, 1, down_product)
     turn(m.wup, m.wupt)
+    turn(m.wqkv, m.wqkvt)
     up_product = lambda rows: mm(m.gub[rows, :], m.wupt[...])
     norm_two(0)
     feed_back(0)
@@ -1245,9 +1313,11 @@
     weight_grad((), m.gffn, m.act, put_whole(m.wdownt), first_rows)
     weight_grad((2, 3), m.nb, m.gub, put_whole(m.wup), first_rows)
     norm_two(1)
-    feed_back(1)
+    spread_end(1, 1, 0)
+    spread_end(1, 1, 1)
     weight_grad((), m.gffn, m.act, add_whole(m.wdownt), last_rows)
     reduce_start(0, m.wdownt, m.xrdown)
+    feed_back(1)
     exchange(2, 1, up_product)
     weight_grad((), m.nb, m.gub, add_whole(m.wup), last_rows)
     reduce_start(1, m.wup, m.xrup)
@@ -1258,28 +1328,31 @@
     norm_one_back(0)
     blocks = lambda ks, matrix: lambda: [reduce_block(k, *matrix) for k in ks] and None
     early = [pass_order[0:1], pass_order[1:2], pass_order[2:-1]]
-    attend_back(0, {1 + i: blocks(ks, down) for i, ks in enumerate(early)})
+    attend_back(0, {2 + i: blocks(ks, down) for i, ks in enumerate(early[:2])})
     exchange(3, 0, input_part)
-    reduce_block(0, *down)
+    blocks(early[2], down)()
     norm_one_back(1)
     spread_end(2, 1, 0)
     spread_end(2, 1, 1)
     weight_grad((0, 1), m.gattn, m.ctx, put_o)
-    reduce_start(2, m.go, m.xro)
-    attend_back(1, {i: blocks(ks, up) for i, ks in zip((0, 2, 3), early)})
+    reduce_block(0, *down)
+    downward = list(range(nz - 1, -1, -1))
+    reduce_start(2, m.go, m.xro, downward)
+    attend_back(1, {i: blocks(ks, up) for i, ks in enumerate(early[:2])})
     weight_grad((), m.tok, m.dqkv, put_qkv)
-    reduce_start(3, m.wqkv, m.xrqkv)
-    reduce_block(0, *up)
-    reduce_pass(*out)
-    exchange(3, 1, input_part)
+    first_part, last_part = downward[: nz // 2], downward[nz // 2 :]
+    reduce_start(3, m.wqkv, m.xrqkv, first_part)
+    blocks(early[2] + [0], up)()
+    reduce_block(downward[0], *out)
 
     sm = m.sm
+    sm[...] = jnp.zeros((SUM_ROWS, LANES), F32)
     acc = m.acc
     lead = jnp.where(yy == 0, 1.0, 0.0)
 
     def put(first, values):
         for i in range(values.shape[1] // LANES):
-            sm[0, first + i : first + i + 1, :] = values[:, i * LANES : (i + 1) * LANES]
+            sm[first + i : first + i + 1, :] = values[:, i * LANES : (i + 1) * LANES]
 
     def spot(values):
         return jnp.concatenate([jnp.where(T == t, values, 0.0) for t in range(4)], axis=1)
@@ -1289,27 +1362,34 @@
     put(24, spot(acc[7:8, 0:head_cols]))
     put(30, spot(acc[7:8, 2 * head_cols : 3 * head_cols]))
     put(48, spot(acc[6:7, 0:hidden]))
-    table_grad = jnp.zeros((32, LANES), F32)
+    parts = []
     for h in range(heads):
         size = LANES // 2
         left = m.dband[h]
-        while size >= 1:
-            left = left[0:size, :] + pltpu.roll(left[size : 2 * size, :], long_row - size, 1) if size >= 8 else left
-            if size < 8:
-                break
+        while size >= 8:
+            left = left[0:size, :] + pltpu.roll(left[size : 2 * size, :], long_row - size, 1)
             size //= 2
         for bit in (1, 2, 4):
             left = jnp.where(lax.rem(lax.div(sub8, bit), 2) == 1, pltpu.roll(left, long_row - bit, 1), left)
+        left = pltpu.roll(left, LANES - 1, 1)
         diagonal = jnp.sum(left, axis=0, keepdims=True)
-        diagonal = pltpu.roll(jnp.broadcast_to(diagonal, (8, long_row)), LANES - 1, 1)[0:1, :]
-        flat = offsets * H + (T * heads + h)
-        at_row = lax.div(flat, LANES)
-        at_lane = lax.rem(flat, LANES)
-        valid = iota((1, long_row), 1) < long_row - 1
-        hot_row = jnp.where((iota((32, long_row), 0) == at_row) & valid, 1.0, 0.0)
-        hot_lane = jnp.where(iota((LANES, long_row), 0) == at_lane, diagonal, 0.0)
+        hi = diagonal.astype(BF16).astype(F32)
+        mid = (diagonal - hi).astype(BF16).astype(F32)
+        parts += [hi, mid, diagonal - hi - mid]
+    parts = jnp.concatenate(parts + [jnp.zeros((16 - len(parts), long_row), F32)], axis=0).astype(BF16)
+    bucket_rows = -(-NB // LANES) * LANES
+    valid = iota((1, long_row), 1) < long_row - 1
+    hot_bucket = jnp.where((iota((bucket_rows, long_row), 0) == offsets) & valid, 1.0, 0.0).astype(BF16)
+    by_bucket = mm_nt(parts, hot_bucket)
+    bucket = iota((1, bucket_rows), 1)
+    table_grad = jnp.zeros((32, LANES), F32)
+    for h in range(heads):
+        sums = by_bucket[3 * h : 3 * h + 1] + by_bucket[3 * h + 1 : 3 * h + 2] + by_bucket[3 * h + 2 : 3 * h + 3]
+        flat = bucket * H + (T * heads + h)
+        hot_row = jnp.where((iota((32, bucket_rows), 0) == lax.div(flat, LANES)) & (bucket < NB), 1.0, 0.0)
+        hot_lane = jnp.where(iota((LANES, bucket_rows), 0) == lax.rem(flat, LANES), sums, 0.0)
         table_grad = table_grad + exact_nt(hot_row, hot_lane)
-    sm[0, TABLE_ROW : TABLE_ROW + 30, :] = table_grad[0:30, :]
+    sm[TABLE_ROW : TABLE_ROW + 30, :] = table_grad[0:30, :]
 
     lin_grad = m.glin[...]
     lin_grad = lin_grad + pltpu.roll(lin_grad, LANES - 16, 1) + pltpu.roll(lin_grad, LANES - 32, 1)
@@ -1318,7 +1398,7 @@
     grad_w = jnp.sum(jnp.where(col_lane >= 8, lin_grad, 0.0), axis=1, keepdims=True)
     by_lane = jnp.where(col_lane == 2 * col_in_head, grad_u, 0.0)
     by_lane = by_lane + jnp.where(col_lane == 2 * col_in_head + 1, grad_w, 0.0)
-    sm[0, GATE_ROW : GATE_ROW + 1, :] = jnp.sum(by_lane, axis=0, keepdims=True)
+    sm[GATE_ROW : GATE_ROW + 1, :] = jnp.sum(by_lane, axis=0, keepdims=True)
     lin_total = acc[9:10, 0:LANES]
     total_u = jnp.sum(jnp.where(lane < 8, lin_total, 0.0), axis=1, keepdims=True)
     total_w = jnp.sum(jnp.where((lane >= 8) & (lane < 16), lin_total, 0.0), axis=1, keepdims=True)
@@ -1327,43 +1407,63 @@
     for h in range(heads):
         one = jnp.sum(jnp.where(lane == h, scale_grad, 0.0), axis=1, keepdims=True)
         last = last + jnp.where(lane == 2 + T * heads + h, one, 0.0)
-    sm[0, OFFSET_ROW : OFFSET_ROW + 1, :] = last
+    sm[OFFSET_ROW : OFFSET_ROW + 1, :] = last
 
     small_sent = []
 
-    def small_step(at, dev):
-        cp = remote(sm.at[at], m.smr.at[at], m.s_ms.at[at], m.s_mr.at[at], dev)
+    def small_send(at, source, target, dev):
+        cp = remote(source, target, m.s_ms.at[at], m.s_mr.at[at], dev)
         cp.start()
         small_sent.append(cp)
         return cp
 
-    small_copy = small_step(0, core_dev)
-    for k in pass_order[0:1]:
+    def quarter(index):
+        return pl.ds(pl.multiple_of(index * QUARTER, QUARTER), QUARTER)
+
+    to_core = [small_send(i, sm.at[quarter(2 * i + 1 - c)], m.smc.at[i], core_dev) for i in range(2)]
+    for i in range(2):
+        to_core[i].wait_recv()
+        m.smh[i] = sm[quarter(2 * i + c), :] + m.smc[i]
+    to_y = small_send(2, m.smh.at[1 - yy], m.smy, y_dev)
+    for k in downward[1:]:
+        reduce_block(k, *out)
+    reduce_block(first_part[0], *qkv)
+    to_y.wait_recv()
+    m.smv[...] = m.smh[yy] + m.smy[...]
+    to_x = small_send(3, m.smv, m.smx, x_dev)
+    reduce_start(3, m.wqkv, m.xrqkv, last_part)
+    exchange(3, 1, input_part)
+    to_x.wait_recv()
+    m.smz[z] = m.smv[...] + m.smx[...]
+    for k in range(1, nz):
+        small_send(3 + k, m.smz.at[z], m.smz.at[z], z_dev(k))
+    for k in first_part[1:]:
         reduce_block(k, *qkv)
-    small_copy.wait_recv()
-    sm[1] = sm[0] + m.smr[0]
-    small_copy = small_step(1, y_dev)
-    for k in pass_order[1:-1]:
+    for k in last_part[:-1]:
         reduce_block(k, *qkv)
     token_rows(0)
-    small_copy.wait_recv()
-    sm[2] = sm[1] + m.smr[1]
-    small_copy = small_step(2, x_dev)
     reduce_block(0, *qkv)
-    small_copy.wait_recv()
-    sm[3] = sm[2] + m.smr[2]
-    for k in range(1, nz):
-        cp = remote(
-            sm.at[3], m.smz.at[z], m.s_ms.at[2 + k], m.s_mr.at[2 + k], z_dev(k)
-        )
-        cp.start()
-        small_sent.append(cp)
-    m.smz[z] = sm[3]
-    token_rows(1)
     squares = reduce_end(0, m.zrdown, sh_down)
     squares = squares + reduce_end(1, m.zrup, sh_up)
     squares = squares + reduce_end(2, m.zro, sh_o)
+    for k in range(1, nz):
+        here = m.smz.at[z_at(k)]
+        remote(here, here, m.s_ms.at[3 + k], m.s_mr.at[3 + k], z_dev(k)).wait_recv()
+    own_quarter = m.smz[0]
+    for i in range(1, nz):
+        own_quarter = own_quarter + m.smz[i]
+    m.sma[quarter(T), :] = own_quarter
+    for k in range(1, 4):
+        mine_small = m.sma.at[quarter(T)]
+        small_send(2 + nz + k, mine_small, mine_small, (D, lax.rem(T + k, 4)))
     squares = squares + reduce_end(3, m.zrqkv, sh_qkv)
+    last_copies = []
+    for i, (source, target) in enumerate(
+        ((sh_down, out_down), (sh_up, out_up), (sh_o, out_o), (sh_qkv, out_qkv))
+    ):
+        cp = pltpu.make_async_copy(source, target, m.s_out.at[i])
+        cp.start()
+        last_copies.append(cp)
     sqt = m.sqt
     sqt[T] = squares
     tail_sent = []
@@ -1373,15 +1473,17 @@
         )
         cp.start()
         tail_sent.append(cp)
-    for k in range(1, nz):
-        here = m.smz.at[z_at(nz - k)]
-        remote(here, here, m.s_ms.at[2 + k], m.s_mr.at[2 + k], z_dev(k)).wait_recv()
-    small_total = m.smz[0]
-    for i in range(1, nz):
-        small_total = small_total + m.smz[i]
+    token_rows(1)
+    for k in range(1, 4):
+        here = m.sma.at[quarter(lax.rem(T + 4 - k, 4))]
+        remote(here, here, m.s_ms.at[2 + nz + k], m.s_mr.at[2 + nz + k], core_dev).wait_recv()
+    small_total = m.sma[0:SMALL_ROWS, :]
     for i in range(3):
         small_out[i] = small[i * SMALL_ROWS : (i + 1) * SMALL_ROWS, :]
     small_out[3] = small_total
+    cp = pltpu.make_async_copy(small_out, out_small, m.s_out.at[4])
+    cp.start()
+    last_copies.append(cp)
     small_square = small_total * small_total
     small_tile = jnp.zeros((8, LANES), F32)
     for i in range(SMALL_ROWS // 8):
@@ -1418,6 +1520,8 @@
     for b in range(2):
         for cp in core_sent[(3, b)] + y_sent[(3, b)]:
             cp.wait_send()
+    for cp in last_copies:
+        cp.wait()
     for here, there in out_copies[2:]:
         here.wait()
         there.wait()
@@ -1456,7 +1560,7 @@
         loads[i].wait()
     length = norm[0:1, 0:1]
     factor = CLIP_LIMIT / jnp.maximum(length, CLIP_LIMIT)
-    o_norm[...] = jnp.broadcast_to(length, (8, LANES))
+    o_norm[...] = length
     store(0)
     for i in (6, 7, 8):
         loads[i].wait()
@@ -1556,8 +1660,8 @@
             sds((4, SMALL_ROWS, LANES), F32),
             sds((8, LANES), F32),
         ),
-        in_specs=[anywhere, anywhere, smem, vmem, vmem, vmem, vmem],
-        out_specs=(anywhere, anywhere, vmem, vmem, vmem, vmem, vmem, vmem),
+        in_specs=[anywhere, anywhere, smem] + [anywhere] * 4,
+        out_specs=(anywhere,) * 7 + (vmem,),
         scratch_shapes=list(scratch.values()),
         compiler_params=pltpu.CompilerParams(
             collective_id=1, has_side_effects=True, vmem_limit_bytes=62 * 1024 * 1024
@@ -1567,7 +1671,7 @@
     like = lambda a, dtype=F32: sds(a.shape, dtype)
     small_like = sds((SMALL_ROWS, LANES), F32)
     made = (
-        sds((8, LANES), F32),
+        sds((1, 1), F32),
         like(attention_weights),
         like(attention_weights),
         like(attention_weights),
@@ -1612,7 +1716,7 @@
     length = small_params.shape[0]
     flat = lambda a: a.reshape(-1)[:length]
     return (
-        results[0][0, 0],
+        results[0].reshape(()),
         *results[1:9],
         flat(results[9]),
         flat(results[10]),
@@ -1622,7 +1726,9 @@
 
 
 def fused_fits(mesh, owned):
-    return mesh.shape["tensor"] == 4 and mesh.shape["dp"] % 2 == 0 and owned % 16 == 0
+    columns = mesh.shape["dp"] // 2
+    whole = mesh.shape["dp"] % 2 == 0 and columns & (columns - 1) == 0
+    return mesh.shape["tensor"] == 4 and whole and owned % 16 == 0
 
 def solution(mesh):
     in_specs = (

time: 148 us -> 138 us (0.932)
  Pallas kernels: 144 us -> 134 us
    pallas_call x1, Pallas kernels: 138 us -> 129 us  [fused_body(): pl.pallas_call(partial(layer_kernel, names, (n_dp, owned, qkv_pad, heads,...]
where the time goes in v3:
time: 138 us
  Pallas kernels  134 us (97%)
  other arithmetic  2.23 us (2%)
    pallas_call x1, Pallas kernels, fused_body(): pl.pallas_call(partial(layer_kernel, names, (n_dp, owned, qkv_pad, heads,...  129 us
    pallas_call x1, Pallas kernels, fused_body(): pl.pallas_call(partial(adam_kernel, head_cols), out_shape=(*made, like(to...  5.68 us

profile of v3, /device:TPU:0, one launch (start us, length us, event | category | flops | bytes accessed | tf_op | source)
XLA Modules:
  0.0 137.5 jit_solution(13281469262335271172)
XLA Ops:
  0.6 0.7 convert_element_type.9
  1.3 1.5 %fusion.refs_6_ = f32[320,128]{1,0:T(8,128)} fusion(f32[1023]{0:T(1024)S(1)} %convert_element_type.9, f32[13198]{0:T(1024)} %param.27, f32[13198]{0:T(1024)} %param.26, f32[13198]{0:T(1024)} %param.25), kind=kLoop, calls=%fused_computation.5 | loop fusion | flops 614400 | bytes 326308 | tf_op jit(solution)/shard_map/reshape | solution.py:1643
  2.9 128.8 %layer.1 = (bf16[1024,768]{1,0:T(8,128)(2,1)}, bf16[1024,768]{1,0:T(8,128)(2,1)}, f32[96,640]{1,0:T(8,128)}, f32[96,128]{1,0:T(8,128)}, f32[96,768]{1,0:T(8,128)...) custom-call(bf16[1024,768]{1,0:T(8,128)(2,1)} %refs_0_.1, bf16[1024,768]{1,0:T(8,128)(2,1)} %refs_1_.1, ...), custom_call_target="tpu_custom_call" | custom-call | tf_op jit(solution)/shard_map/layer/pallas_call | solution.py:1651
  131.6 5.7 %adam.1 = (f32[1,1]{1,0:T(1,128)}, f32[4,96,192]{2,1,0:T(8,128)}, f32[4,96,192]{2,1,0:T(8,128)}, f32[4,96,192]{2,1,0:T(8,128)}, bf16[4,96,192]{2,1,0:T(8,128)(2,...) custom-call(f32[96,640]{1,0:T(8,128)} %get-tuple-element.36.refs_0_,, ...), custom_call_target="tpu_custom_call" | custom-call | tf_op jit(solution)/shard_map/adam/pallas_call | solution.py:1704

commit v4 on v3

--- a/solution.py
+++ b/solution.py
@@ -486,15 +486,18 @@
         xrqkv=vm((nz, owned, qkv_pad), BF16),
         xro=vm((nz, owned, LANES), BF16),
         xrup=vm((nz, owned, hidden), BF16),
-        xrdown=vm((nz, owned, hidden), BF16),
+        xrdown=vm((nz, owned, hidden // 2), BF16),
+        xrdownb=vm((nz, owned, hidden // 2), BF16),
         zsqkv=vm((nz - 1, owned, qkv_pad), BF16),
         zso=vm((nz - 1, owned, LANES), BF16),
         zsup=vm((nz - 1, owned, hidden), BF16),
-        zsdown=vm((nz - 1, owned, hidden), BF16),
+        zsdown=vm((nz - 1, owned, hidden // 2), BF16),
+        zsdownb=vm((nz - 1, owned, hidden // 2), BF16),
         zrqkv=vm((nz - 1, owned, qkv_pad), BF16),
         zro=vm((nz - 1, owned, LANES), BF16),
         zrup=vm((nz - 1, owned, hidden), BF16),
-        zrdown=vm((nz - 1, owned, hidden), BF16),
+        zrdown=vm((nz - 1, owned, hidden // 2), BF16),
+        zrdownb=vm((nz - 1, owned, hidden // 2), BF16),
         sm=vm((SUM_ROWS, LANES), F32),
         smc=vm((2, QUARTER, LANES), F32),
         smh=vm((2, QUARTER, LANES), F32),
@@ -522,10 +525,10 @@
         s_ol=dma((2, 2)),
         s_os=dma((2, 2)),
         s_or=dma((2, 2)),
-        s_xs=dma((4, nz)),
-        s_xr=dma((4, nz)),
-        s_zs=dma((4, nz)),
-        s_zr=dma((4, nz)),
+        s_xs=dma((5, nz)),
+        s_xr=dma((5, nz)),
+        s_zs=dma((5, nz)),
+        s_zr=dma((5, nz)),
         s_ms=dma((6 + nz,)),
         s_mr=dma((6 + nz,)),
         s_ts=dma((4,)),
@@ -850,6 +853,8 @@
     line_start(2, 2)
     line_end(0)
     gather_x(1)
+    line_step(1, 1, 2)
+    line_step(1, 2, 2)
     gather_x(2)
 
     def project(i):
@@ -1242,9 +1247,67 @@
         for k in pass_order:
             reduce_block(k, *matrix)
 
-    def reduce_end(which, arrive, share):
-        total = add_landed(share[...], 0, which, arrive)
-        share[...] = total
+    kept = [k for k in range(nz) if k % 2 == 0]
+    x_slots = {k: i for i, k in enumerate(kept)}
+    far_slots = {}
+    for k in kept:
+        for bit in bits[1:]:
+            if bit < low_bit(k):
+                far_slots[(k, bit)] = len(x_slots) + len(far_slots)
+
+    def owner_rows(k, side):
+        return block(2 * z_at(k) + (1 - x if side else x))
+
+    def near_start(which, buf, land):
+        for k in reversed(kept):
+            for side in (1, 0):
+
+                def where(k=k, side=side):
+                    at = k + side
+                    sems = m.s_xs.at[which, at], m.s_xr.at[which, at]
+                    return buf.at[owner_rows(k + 1, side)], land.at[at], *sems, z_dev(1)
+
+                launch(reduces, where)
+
+    def near_total(k, side, which, buf, land):
+        at = k + side
+        here = land.at[at]
+        remote(here, here, m.s_xs.at[which, at], m.s_xr.at[which, at], z_dev(1)).wait_recv()
+        return buf[owner_rows(k, side), :].astype(F32) + land[at].astype(F32)
+
+    def landed_slot(slot, which, arrive):
+        here = arrive.at[slot]
+        remote(here, here, m.s_zs.at[which, slot], m.s_zr.at[which, slot], x_dev).wait_recv()
+        return arrive[slot].astype(F32)
+
+    def near_across(k, which, buf, land, out, arrive, share):
+        slot = x_slots[k]
+        out[slot] = near_total(k, 1, which, buf, land).astype(BF16)
+
+        def where():
+            return out.at[slot], arrive.at[slot], m.s_zs.at[which, slot], m.s_zr.at[which, slot], x_dev
+
+        launch(reduces, where)
+
+    def near_far(k, which, buf, land, out, arrive, share):
+        total = near_total(k, 0, which, buf, land) + landed_slot(x_slots[k], which, arrive)
+        for bit in bits[1:]:
+            if bit < low_bit(k):
+                total = total + landed_slot(far_slots[(k, bit)], which, arrive)
+        if k == 0:
+            share[...] = total
+            return
+        bit = low_bit(k)
+        slot = far_slots[(k - bit, bit)]
+        out[slot] = total.astype(BF16)
+
+        def where():
+            sems = m.s_zs.at[which, slot], m.s_zr.at[which, slot]
+            return out.at[slot], arrive.at[slot], *sems, z_dev(bit)
+
+        launch(reduces, where)
+
+    def squares_of(total):
         squares = total * total
         folded = jnp.zeros((owned, LANES), F32)
         for i in range(total.shape[1] // LANES):
@@ -1254,6 +1317,11 @@
             tile = tile + folded[8 * i : 8 * i + 8, :]
         return tile
 
+    def reduce_end(which, arrive, share):
+        total = add_landed(share[...], 0, which, arrive)
+        share[...] = total
+        return squares_of(total)
+
     def pass_on(which):
         line_step(which, 1, 2)
         line_step(which, 2, 2)
@@ -1265,13 +1333,13 @@
     line_start(3, 2)
     gather_x(3)
 
+    pass_last(1)
+
     def first_pass():
-        pass_on(1)
         line_start(4, 2)
         gather_x(4)
 
     def second_pass():
-        pass_last(1)
         pass_on(2)
         partner_landed(5)
         line_start(5, 2)
@@ -1316,33 +1384,52 @@
     spread_end(1, 1, 0)
     spread_end(1, 1, 1)
     weight_grad((), m.gffn, m.act, add_whole(m.wdownt), last_rows)
-    reduce_start(0, m.wdownt, m.xrdown)
+    half = hidden // 2
+    left, right = m.wdownt.at[:, 0:half], m.wdownt.at[:, half:hidden]
+    down = (0, left, m.xrdown, m.zsdown, m.zrdown, sh_down.at[:, 0:half])
+    down_near = (4, right, m.xrdownb, m.zsdownb, m.zrdownb, sh_down.at[:, half:hidden])
+    near_start(4, right, m.xrdownb)
+    reduce_start(0, left, m.xrdown)
     feed_back(1)
     exchange(2, 1, up_product)
     weight_grad((), m.nb, m.gub, add_whole(m.wup), last_rows)
     reduce_start(1, m.wup, m.xrup)
-    down = (0, m.wdownt, m.xrdown, m.zsdown, m.zrdown, sh_down)
     up = (1, m.wup, m.xrup, m.zsup, m.zrup, sh_up)
     out = (2, m.go, m.xro, m.zso, m.zro, sh_o)
     qkv = (3, m.wqkv, m.xrqkv, m.zsqkv, m.zrqkv, sh_qkv)
     norm_one_back(0)
     blocks = lambda ks, matrix: lambda: [reduce_block(k, *matrix) for k in ks] and None
     early = [pass_order[0:1], pass_order[1:2], pass_order[2:-1]]
-    attend_back(0, {2 + i: blocks(ks, down) for i, ks in enumerate(early[:2])})
+    attend_back(
+        0,
+        {
+            0: lambda: near_across(2, *down_near),
+            1: lambda: near_across(0, *down_near),
+            2: blocks(early[0], down),
+            3: blocks(early[1], down),
+        },
+    )
     exchange(3, 0, input_part)
-    blocks(early[2], down)()
+    blocks(early[0], up)()
     norm_one_back(1)
     spread_end(2, 1, 0)
     spread_end(2, 1, 1)
     weight_grad((0, 1), m.gattn, m.ctx, put_o)
-    reduce_block(0, *down)
+    blocks(early[1], up)()
     downward = list(range(nz - 1, -1, -1))
     reduce_start(2, m.go, m.xro, downward)
-    attend_back(1, {i: blocks(ks, up) for i, ks in enumerate(early[:2])})
+    attend_back(
+        1,
+        {
+            0: blocks(early[2] + [0], down),
+            1: blocks(early[2], up),
+            2: blocks([0], up),
+            3: lambda: near_far(2, *down_near),
+        },
+    )
     weight_grad((), m.tok, m.dqkv, put_qkv)
-    first_part, last_part = downward[: nz // 2], downward[nz // 2 :]
+    first_part, last_part = downward[:-1], downward[-1:]
     reduce_start(3, m.wqkv, m.xrqkv, first_part)
-    blocks(early[2] + [0], up)()
     reduce_block(downward[0], *out)
 
     sm = m.sm
@@ -1425,25 +1512,26 @@
         to_core[i].wait_recv()
         m.smh[i] = sm[quarter(2 * i + c), :] + m.smc[i]
     to_y = small_send(2, m.smh.at[1 - yy], m.smy, y_dev)
-    for k in downward[1:]:
-        reduce_block(k, *out)
     reduce_block(first_part[0], *qkv)
+    exchange(3, 1, input_part)
+    reduce_block(downward[1], *out)
     to_y.wait_recv()
     m.smv[...] = m.smh[yy] + m.smy[...]
     to_x = small_send(3, m.smv, m.smx, x_dev)
     reduce_start(3, m.wqkv, m.xrqkv, last_part)
-    exchange(3, 1, input_part)
+    for k in downward[2:]:
+        reduce_block(k, *out)
     to_x.wait_recv()
     m.smz[z] = m.smv[...] + m.smx[...]
     for k in range(1, nz):
         small_send(3 + k, m.smz.at[z], m.smz.at[z], z_dev(k))
     for k in first_part[1:]:
         reduce_block(k, *qkv)
-    for k in last_part[:-1]:
-        reduce_block(k, *qkv)
     token_rows(0)
     reduce_block(0, *qkv)
-    squares = reduce_end(0, m.zrdown, sh_down)
+    squares = reduce_end(0, m.zrdown, sh_down.at[:, 0:half])
+    near_far(0, *down_near)
+    squares = squares + squares_of(sh_down[:, half:hidden])
     squares = squares + reduce_end(1, m.zrup, sh_up)
     squares = squares + reduce_end(2, m.zro, sh_o)
     for k in range(1, nz):
@@ -1535,8 +1623,6 @@
     held, made = rest[:12], rest[12:24]
     block_held, token_held, s_in, s_out = rest[24:]
     loads = [pltpu.make_async_copy(ins[i], held[i], s_in.at[i]) for i in range(12)]
-    for cp in loads:
-        cp.start()
     passing = [
         pltpu.make_async_copy(block_in, block_held, s_in.at[12]),
         pltpu.make_async_copy(token_in, token_held, s_in.at[13]),
@@ -1545,7 +1631,7 @@
         pltpu.make_async_copy(block_held, block_out, s_out.at[12]),
         pltpu.make_async_copy(token_held, token_out, s_out.at[13]),
     ]
-    for cp in passing:
+    for cp in loads + passing:
         cp.start()
     stores = []
 
@@ -1606,10 +1692,6 @@
         cp.wait()
 
 
-def tiles(vector):
-    return jnp.pad(vector, (0, SMALL_ROWS * LANES - vector.shape[0]))
-
-
 def fused_body(
     n_dp,
     tokens,
@@ -1633,14 +1715,14 @@
     heads = head_cols // HD
     qkv_pad = -(-3 * head_cols // LANES) * LANES
     nz = n_dp // 2
-    packed = jnp.concatenate(
-        [
-            tiles(small_params),
-            tiles(small_first),
-            tiles(small_second),
-            jnp.pad(rel_buckets.astype(F32), (0, 1)),
-        ]
-    ).reshape(-1, LANES)
+    small_size = SMALL_ROWS * LANES
+    total_size = 3 * small_size + 2 * BUCKET_SLOTS
+    packed = jnp.zeros((total_size,), F32)
+    pieces = (small_params, small_first, small_second, rel_buckets.astype(F32))
+    for i, values in enumerate(pieces):
+        after = total_size - i * small_size - values.shape[0]
+        packed = packed + jnp.pad(values, (i * small_size, after))
+    packed = packed.reshape(-1, LANES)
     keep = key_mask.reshape(rows // LANES, LANES)
     scratch = layer_scratch(owned, nz, qkv_pad, heads, head_cols, hidden)
     names = tuple(scratch)

time: 138 us -> 135 us (0.978)
  Pallas kernels: 134 us -> 132 us
    pallas_call x1, Pallas kernels: 129 us -> 126 us  [fused_body(): pl.pallas_call(partial(layer_kernel, names, (n_dp, owned, qkv_pad, heads,...]
where the time goes in v4:
time: 135 us
  Pallas kernels  132 us (98%)
  other arithmetic  2.23 us (2%)
    pallas_call x1, Pallas kernels, fused_body(): pl.pallas_call(partial(layer_kernel, names, (n_dp, owned, qkv_pad, heads,...  126 us
    pallas_call x1, Pallas kernels, fused_body(): pl.pallas_call(partial(adam_kernel, head_cols), out_shape=(*made, like(to...  5.68 us

profile of v4, /device:TPU:0, one launch (start us, length us, event | category | flops | bytes accessed | tf_op | source)
XLA Modules:
  0.0 135.0 jit_solution(7464058440465428670)
XLA Ops:
  0.6 0.7 convert_element_type.11
  1.3 1.5 %add_bitcast_fusion.refs_6_ = f32[320,128]{1,0:T(8,128)} fusion(f32[1023]{0:T(1024)S(1)} %convert_element_type.11, f32[13198]{0:T(1024)} %param.27, f32[13198]{0:T(1024)} %param.26, f32[13198]{0:T(1024)} %param.25), kind=kLoop, calls=%fused_computation | loop fusion | flops 122880 | bytes 326308 | tf_op jit(solution)/shard_map/reshape | solution.py:1725
  2.9 126.2 %layer.1 = (bf16[1024,768]{1,0:T(8,128)(2,1)}, bf16[1024,768]{1,0:T(8,128)(2,1)}, f32[96,640]{1,0:T(8,128)}, f32[96,128]{1,0:T(8,128)}, f32[96,768]{1,0:T(8,128)...) custom-call(bf16[1024,768]{1,0:T(8,128)(2,1)} %refs_0_.1, bf16[1024,768]{1,0:T(8,128)(2,1)} %refs_1_.1, ...), custom_call_target="tpu_custom_call" | custom-call | tf_op jit(solution)/shard_map/layer/pallas_call | solution.py:1733
  129.1 5.7 %adam.1 = (f32[1,1]{1,0:T(1,128)}, f32[4,96,192]{2,1,0:T(8,128)}, f32[4,96,192]{2,1,0:T(8,128)}, f32[4,96,192]{2,1,0:T(8,128)}, bf16[4,96,192]{2,1,0:T(8,128)(2,...) custom-call(f32[96,640]{1,0:T(8,128)} %get-tuple-element.36.refs_0_,, ...), custom_call_target="tpu_custom_call" | custom-call | tf_op jit(solution)/shard_map/adam/pallas_call | solution.py:1786

commit v5 on v4

--- a/solution.py
+++ b/solution.py
@@ -510,12 +510,12 @@
         sqd=vm((2 * nz, 8, LANES), F32),
         s_in=dma((7,)),
         s_out=dma((5,)),
-        s_gs=dma((6,)),
-        s_gr=dma((6,)),
-        s_ls=dma((7, 2, nz)),
-        s_lr=dma((7, 2, nz)),
-        s_lxs=dma((7, 2, nz)),
-        s_lxr=dma((7, 2, nz)),
+        s_gs=dma((8,)),
+        s_gr=dma((8,)),
+        s_ls=dma((8, 2, nz)),
+        s_lr=dma((8, 2, nz)),
+        s_lxs=dma((8, 2, nz)),
+        s_lxr=dma((8, 2, nz)),
         s_cs=dma((4, 2, 2)),
         s_cr=dma((4, 2, 2)),
         s_ys=dma((4, 2, 2)),
@@ -612,10 +612,8 @@
     pl.semaphore_wait(barrier, 3 + n_dp - 1)
 
     part_rows = owned // 2 if owned % 32 == 0 else owned
-    pieces = [(m.wqkv, 0, owned), (m.wo1, 0, owned)]
-    for buf in (m.wup, m.wdown):
-        pieces.append((buf, 0, part_rows))
-        pieces.append((buf, owned - part_rows, part_rows))
+    halves = lambda buf: [(buf, 0, part_rows), (buf, owned - part_rows, part_rows)]
+    pieces = halves(m.wqkv) + [(m.wo1, 0, owned)] + halves(m.wup) + halves(m.wdown)
 
     pieces.append(pieces[-1])
     across = len(pieces) - 1
@@ -722,8 +720,10 @@
 
         loop(count // step, chunk)
 
-    line_start(0, 1)
-    gather_x(0)
+    for which in (0, 1):
+        line_start(which, 1)
+    for which in (0, 1):
+        gather_x(which)
     gather_x(across - 1)
 
     def small_row(first, count):
@@ -772,6 +772,7 @@
     head_lane = lane < heads
 
     line_step(0, 1, 1)
+    line_step(1, 1, 1)
 
     offsets = small_row(3 * SMALL_ROWS, 2 * BUCKET_SLOTS // LANES).astype(jnp.int32)
     table = small[TABLE_ROW : TABLE_ROW + 32, :]
@@ -797,6 +798,7 @@
     m.dband[...] = jnp.zeros(m.dband.shape, F32)
 
     line_step(0, 2, 1)
+    line_step(1, 2, 1)
 
     for b in range(2):
         end = 0
@@ -825,7 +827,8 @@
 
     for step in range(3, nz):
         line_step(0, step, 1)
-    line_start(1, 2)
+        line_step(1, step, 1)
+    line_start(2, 2)
 
     tok_copy.wait()
     gmat = m.gmat[...]
@@ -850,12 +853,13 @@
 
     loop(4, gate_chunk)
 
-    line_start(2, 2)
+    line_start(3, 2)
     line_end(0)
-    gather_x(1)
-    line_step(1, 1, 2)
-    line_step(1, 2, 2)
+    line_end(1)
     gather_x(2)
+    line_step(2, 1, 2)
+    line_step(2, 2, 2)
+    gather_x(3)
 
     def project(i):
         rows = pl.ds(pl.multiple_of(i * HALF, HALF), HALF)
@@ -922,6 +926,10 @@
     y_sent = {}
 
     def exchange(phase, b, product):
+        exchange_first(phase, b, product)
+        exchange_last(phase, b)
+
+    def exchange_first(phase, b, product):
         other = b * BUCKET_SLOTS + (1 - c) * HALF
         own = b * BUCKET_SLOTS + c * HALF
         for cp in core_sent.get((phase - 1, b), []) + y_sent.get((phase - 1, b), []):
@@ -939,6 +947,8 @@
             at = slice(i * CHUNK, (i + 1) * CHUNK)
             rows = pl.ds(pl.multiple_of(own + i * CHUNK, CHUNK), CHUNK)
             m.ownf[at, :] = product(rows)
+
+    def exchange_last(phase, b):
         for i in range(2):
             at = slice(i * CHUNK, (i + 1) * CHUNK)
             core_sent[(phase, b)][i].wait_recv()
@@ -1330,41 +1340,41 @@
         for step in range(3, nz):
             line_step(which, step, 2)
 
-    line_start(3, 2)
-    gather_x(3)
-
-    pass_last(1)
+    line_start(4, 2)
+    gather_x(4)
+
+    pass_last(2)
 
     def first_pass():
-        line_start(4, 2)
-        gather_x(4)
+        line_start(5, 2)
+        gather_x(5)
 
     def second_pass():
-        pass_on(2)
-        partner_landed(5)
-        line_start(5, 2)
+        pass_on(3)
+        partner_landed(6)
         line_start(6, 2)
+        line_start(7, 2)
 
     attend(0, {0: first_pass, 2: second_pass})
-    line_end(1)
+    line_end(2)
     m.wo[...] = jnp.concatenate([m.wqkv[:, 3 * head_cols : qkv_pad], m.wo1[...]], axis=1)
     turn(m.wo, m.wot)
     out_product = lambda rows: mm(m.ctx[rows, :], m.wot[...])
     exchange(0, 0, out_product)
-    pass_last(2)
-    attend(1, {1: lambda: pass_on(3), 3: lambda: pass_last(3)})
+    pass_last(3)
+    attend(1, {1: lambda: pass_on(4), 3: lambda: pass_last(4)})
     exchange(0, 1, out_product)
-    pass_on(4)
     pass_on(5)
+    pass_on(6)
     norm_one(0)
-    pass_last(4)
-    pass_on(6)
-    line_end(2)
+    pass_last(5)
+    pass_on(7)
     line_end(3)
+    line_end(4)
     feed(0)
-    pass_last(5)
     pass_last(6)
-    line_end(4)
+    pass_last(7)
+    line_end(5)
     turn(m.wdown, m.wdownt)
     down_product = lambda rows: mm(m.act[rows, :], m.wdownt[...])
     exchange(1, 0, down_product)
@@ -1379,7 +1389,7 @@
     exchange(2, 0, up_product)
     first_rows, last_rows = slice(0, BUCKET_SLOTS), slice(BUCKET_SLOTS, 2 * BUCKET_SLOTS)
     weight_grad((), m.gffn, m.act, put_whole(m.wdownt), first_rows)
-    weight_grad((2, 3), m.nb, m.gub, put_whole(m.wup), first_rows)
+    weight_grad((3, 4), m.nb, m.gub, put_whole(m.wup), first_rows)
     norm_two(1)
     spread_end(1, 1, 0)
     spread_end(1, 1, 1)
@@ -1393,28 +1403,36 @@
     feed_back(1)
     exchange(2, 1, up_product)
     weight_grad((), m.nb, m.gub, add_whole(m.wup), last_rows)
-    reduce_start(1, m.wup, m.xrup)
+    near_across(2, *down_near)
+    odd, even = pass_order[: nz // 2], pass_order[nz // 2 :]
+    reduce_start(1, m.wup, m.xrup, odd)
     up = (1, m.wup, m.xrup, m.zsup, m.zrup, sh_up)
     out = (2, m.go, m.xro, m.zso, m.zro, sh_o)
     qkv = (3, m.wqkv, m.xrqkv, m.zsqkv, m.zrqkv, sh_qkv)
     norm_one_back(0)
     blocks = lambda ks, matrix: lambda: [reduce_block(k, *matrix) for k in ks] and None
     early = [pass_order[0:1], pass_order[1:2], pass_order[2:-1]]
+
+    def second_across():
+        near_across(0, *down_near)
+        reduce_start(1, m.wup, m.xrup, even)
+
     attend_back(
         0,
         {
-            0: lambda: near_across(2, *down_near),
-            1: lambda: near_across(0, *down_near),
-            2: blocks(early[0], down),
-            3: blocks(early[1], down),
+            0: second_across,
+            1: blocks(early[0], down),
+            2: blocks(early[1], down),
+            3: lambda: near_far(2, *down_near),
         },
     )
-    exchange(3, 0, input_part)
+    exchange_first(3, 0, input_part)
     blocks(early[0], up)()
     norm_one_back(1)
+    exchange_last(3, 0)
     spread_end(2, 1, 0)
     spread_end(2, 1, 1)
-    weight_grad((0, 1), m.gattn, m.ctx, put_o)
+    weight_grad((0, 1, 2), m.gattn, m.ctx, put_o)
     blocks(early[1], up)()
     downward = list(range(nz - 1, -1, -1))
     reduce_start(2, m.go, m.xro, downward)
@@ -1422,14 +1440,13 @@
         1,
         {
             0: blocks(early[2] + [0], down),
-            1: blocks(early[2], up),
-            2: blocks([0], up),
-            3: lambda: near_far(2, *down_near),
+            3: blocks(early[2], up),
         },
     )
     weight_grad((), m.tok, m.dqkv, put_qkv)
     first_part, last_part = downward[:-1], downward[-1:]
     reduce_start(3, m.wqkv, m.xrqkv, first_part)
+    reduce_block(0, *up)
     reduce_block(downward[0], *out)
 
     sm = m.sm
@@ -1521,11 +1538,12 @@
     reduce_start(3, m.wqkv, m.xrqkv, last_part)
     for k in downward[2:]:
         reduce_block(k, *out)
+    reduce_block(first_part[1], *qkv)
     to_x.wait_recv()
     m.smz[z] = m.smv[...] + m.smx[...]
     for k in range(1, nz):
         small_send(3 + k, m.smz.at[z], m.smz.at[z], z_dev(k))
-    for k in first_part[1:]:
+    for k in first_part[2:]:
         reduce_block(k, *qkv)
     token_rows(0)
     reduce_block(0, *qkv)

time: 135 us -> 133 us (0.985)
  Pallas kernels: 132 us -> 129 us
    pallas_call x1, Pallas kernels: 126 us -> 124 us  [fused_body(): pl.pallas_call(partial(layer_kernel, names, (n_dp, owned, qkv_pad, heads,...]
where the time goes in v5:
time: 133 us; the launch traced here: 132 us
  Pallas kernels  129 us (97%)
  other arithmetic  2.23 us (2%)
    pallas_call x1, Pallas kernels, fused_body(): pl.pallas_call(partial(layer_kernel, names, (n_dp, owned, qkv_pad, heads,...  124 us
    pallas_call x1, Pallas kernels, fused_body(): pl.pallas_call(partial(adam_kernel, head_cols), out_shape=(*made, like(to...  5.68 us

profile of v5, /device:TPU:0, one launch (start us, length us, event | category | flops | bytes accessed | tf_op | source)
XLA Modules:
  0.0 132.4 jit_solution(17931994915021544095)
XLA Ops:
  0.6 0.7 convert_element_type.11
  1.3 1.5 %add_bitcast_fusion.refs_6_ = f32[320,128]{1,0:T(8,128)} fusion(f32[1023]{0:T(1024)S(1)} %convert_element_type.11, f32[13198]{0:T(1024)} %param.27, f32[13198]{0:T(1024)} %param.26, f32[13198]{0:T(1024)} %param.25), kind=kLoop, calls=%fused_computation | loop fusion | flops 122880 | bytes 326308 | tf_op jit(solution)/shard_map/reshape | solution.py:1743
  2.9 123.6 %layer.1 = (bf16[1024,768]{1,0:T(8,128)(2,1)}, bf16[1024,768]{1,0:T(8,128)(2,1)}, f32[96,640]{1,0:T(8,128)}, f32[96,128]{1,0:T(8,128)}, f32[96,768]{1,0:T(8,128)...) custom-call(bf16[1024,768]{1,0:T(8,128)(2,1)} %refs_0_.1, bf16[1024,768]{1,0:T(8,128)(2,1)} %refs_1_.1, ...), custom_call_target="tpu_custom_call" | custom-call | tf_op jit(solution)/shard_map/layer/pallas_call | solution.py:1751
  126.5 5.7 %adam.1 = (f32[1,1]{1,0:T(1,128)}, f32[4,96,192]{2,1,0:T(8,128)}, f32[4,96,192]{2,1,0:T(8,128)}, f32[4,96,192]{2,1,0:T(8,128)}, bf16[4,96,192]{2,1,0:T(8,128)(2,...) custom-call(f32[96,640]{1,0:T(8,128)} %get-tuple-element.36.refs_0_,, ...), custom_call_target="tpu_custom_call" | custom-call | tf_op jit(solution)/shard_map/adam/pallas_call | solution.py:1804

commit v6 on v5

--- a/solution.py
+++ b/solution.py
@@ -1005,11 +1005,11 @@
             rstd = lax.rsqrt(row_mean(centred * centred) + NORM_EPSILON)
             hat = centred * rstd
             normed = hat * vecs[0:1, :] + vecs[1:2, :]
+            m.nb[rows, :] = normed.astype(BF16)
+            spread(0, m.nb, b, i)
             m.xh1[b, at, :] = hat
             m.rstd1[b, at, :] = jnp.broadcast_to(rstd, (CHUNK, LANES))
             m.held[b, at, :] = normed
-            m.nb[rows, :] = normed.astype(BF16)
-            spread(0, m.nb, b, i)
 
         as_it_lands(0, b, chunk)
 
@@ -1018,10 +1018,13 @@
             i = lax.rem(step + 2 * c, 4)
             return pl.ds(pl.multiple_of(b * BUCKET_SLOTS + i * CHUNK, CHUNK), CHUNK)
 
+        def rest():
+            for i in range(2):
+                spread_end(which, b, i)
+                chunk(rows_at(2 + i))
+
         loop(2, lambda step: chunk(rows_at(step)))
-        for i in range(2):
-            spread_end(which, b, i)
-            chunk(rows_at(2 + i))
+        return rest
 
     def feed(b):
         def chunk(rows):
@@ -1030,7 +1033,7 @@
             m.act[rows, :] = (up * half_phi).astype(BF16)
             m.gelup[rows, :] = half_phi + up * (jnp.exp(up * up * -0.5) * INV_SQRT_2PI)
 
-        own_first(0, b, chunk)
+        own_first(0, b, chunk)()
 
     out_copies = []
 
@@ -1053,16 +1056,16 @@
             centred = residual - row_mean(residual)
             rstd = lax.rsqrt(row_mean(centred * centred) + NORM_EPSILON)
             hat = centred * rstd
-            m.stage[b, at, :] = (hat * vecs[2:3, :] + vecs[3:4, :]).astype(BF16)
             upstream = m.cot[b, at, :].astype(F32)
-            add_row(2, upstream * hat)
-            add_row(3, upstream)
             scaled = upstream * vecs[2:3, :]
             grad = rstd * (scaled - row_mean(scaled) - hat * row_mean(scaled * hat))
-            m.held[b, at, :] = grad
             low = grad.astype(BF16)
             m.gffn[rows, :] = low
             spread(1, m.gffn, b, i)
+            m.held[b, at, :] = grad
+            m.stage[b, at, :] = (hat * vecs[2:3, :] + vecs[3:4, :]).astype(BF16)
+            add_row(2, upstream * hat)
+            add_row(3, upstream)
             add_row(5, low.astype(F32))
 
         as_it_lands(1, b, chunk)
@@ -1075,7 +1078,7 @@
             m.gub[rows, :] = low
             add_row(6, low.astype(F32))
 
-        own_first(1, b, chunk)
+        return own_first(1, b, chunk)
 
     def norm_one_back(b):
 
@@ -1084,15 +1087,15 @@
             rows = own_rows(b, i)
             upstream = arrived(2, b, at) + DEEP_ALPHA * m.held[b, at, :]
             hat = m.xh1[b, at, :]
-            add_row(0, upstream * hat)
-            add_row(1, upstream)
             scaled = upstream * vecs[0:1, :]
             rstd = m.rstd1[b, at, 0:1]
             grad = rstd * (scaled - row_mean(scaled) - hat * row_mean(scaled * hat))
-            m.held[b, at, :] = grad
             low = grad.astype(BF16)
             m.gattn[rows, :] = low
             spread(2, m.gattn, b, i)
+            m.held[b, at, :] = grad
+            add_row(0, upstream * hat)
+            add_row(1, upstream)
             add_row(4, low.astype(F32))
 
         as_it_lands(2, b, chunk)
@@ -1385,12 +1388,13 @@
     turn(m.wqkv, m.wqkvt)
     up_product = lambda rows: mm(m.gub[rows, :], m.wupt[...])
     norm_two(0)
-    feed_back(0)
+    feed_back(0)()
     exchange(2, 0, up_product)
     first_rows, last_rows = slice(0, BUCKET_SLOTS), slice(BUCKET_SLOTS, 2 * BUCKET_SLOTS)
     weight_grad((), m.gffn, m.act, put_whole(m.wdownt), first_rows)
     weight_grad((3, 4), m.nb, m.gub, put_whole(m.wup), first_rows)
     norm_two(1)
+    feed_rest = feed_back(1)
     spread_end(1, 1, 0)
     spread_end(1, 1, 1)
     weight_grad((), m.gffn, m.act, add_whole(m.wdownt), last_rows)
@@ -1400,16 +1404,16 @@
     down_near = (4, right, m.xrdownb, m.zsdownb, m.zrdownb, sh_down.at[:, half:hidden])
     near_start(4, right, m.xrdownb)
     reduce_start(0, left, m.xrdown)
-    feed_back(1)
+    feed_rest()
     exchange(2, 1, up_product)
     weight_grad((), m.nb, m.gub, add_whole(m.wup), last_rows)
-    near_across(2, *down_near)
     odd, even = pass_order[: nz // 2], pass_order[nz // 2 :]
-    reduce_start(1, m.wup, m.xrup, odd)
     up = (1, m.wup, m.xrup, m.zsup, m.zrup, sh_up)
     out = (2, m.go, m.xro, m.zso, m.zro, sh_o)
     qkv = (3, m.wqkv, m.xrqkv, m.zsqkv, m.zrqkv, sh_qkv)
     norm_one_back(0)
+    near_across(2, *down_near)
+    reduce_start(1, m.wup, m.xrup, odd)
     blocks = lambda ks, matrix: lambda: [reduce_block(k, *matrix) for k in ks] and None
     early = [pass_order[0:1], pass_order[1:2], pass_order[2:-1]]
 
@@ -1420,13 +1424,13 @@
     attend_back(
         0,
         {
-            0: second_across,
-            1: blocks(early[0], down),
-            2: blocks(early[1], down),
-            3: lambda: near_far(2, *down_near),
+            1: second_across,
+            2: blocks(early[0], down),
+            3: blocks(early[1], down),
         },
     )
     exchange_first(3, 0, input_part)
+    near_far(2, *down_near)
     blocks(early[0], up)()
     norm_one_back(1)
     exchange_last(3, 0)
@@ -1530,8 +1534,9 @@
         m.smh[i] = sm[quarter(2 * i + c), :] + m.smc[i]
     to_y = small_send(2, m.smh.at[1 - yy], m.smy, y_dev)
     reduce_block(first_part[0], *qkv)
-    exchange(3, 1, input_part)
+    exchange_first(3, 1, input_part)
     reduce_block(downward[1], *out)
+    exchange_last(3, 1)
     to_y.wait_recv()
     m.smv[...] = m.smh[yy] + m.smy[...]
     to_x = small_send(3, m.smv, m.smx, x_dev)

time: 133 us -> 132 us (level)
  no operation moved by 1% of the time
where the time goes in v6:
time: 132 us
  Pallas kernels  129 us (98%)
  other arithmetic  2.23 us (2%)
    pallas_call x1, Pallas kernels, fused_body(): pl.pallas_call(partial(layer_kernel, names, (n_dp, owned, qkv_pad, heads,...  123 us
    pallas_call x1, Pallas kernels, fused_body(): pl.pallas_call(partial(adam_kernel, head_cols), out_shape=(*made, like(to...  5.68 us

profile of v6, /device:TPU:0, one launch (start us, length us, event | category | flops | bytes accessed | tf_op | source)
XLA Modules:
  0.0 132.1 jit_solution(6779394900856655935)
XLA Ops:
  0.6 0.7 convert_element_type.11
  1.3 1.5 %add_bitcast_fusion.refs_6_ = f32[320,128]{1,0:T(8,128)} fusion(f32[1023]{0:T(1024)S(1)} %convert_element_type.11, f32[13198]{0:T(1024)} %param.27, f32[13198]{0:T(1024)} %param.26, f32[13198]{0:T(1024)} %param.25), kind=kLoop, calls=%fused_computation | loop fusion | flops 122880 | bytes 326308 | tf_op jit(solution)/shard_map/reshape | solution.py:1748
  2.9 123.4 %layer.1 = (bf16[1024,768]{1,0:T(8,128)(2,1)}, bf16[1024,768]{1,0:T(8,128)(2,1)}, f32[96,640]{1,0:T(8,128)}, f32[96,128]{1,0:T(8,128)}, f32[96,768]{1,0:T(8,128)...) custom-call(bf16[1024,768]{1,0:T(8,128)(2,1)} %refs_0_.1, bf16[1024,768]{1,0:T(8,128)(2,1)} %refs_1_.1, ...), custom_call_target="tpu_custom_call" | custom-call | tf_op jit(solution)/shard_map/layer/pallas_call | solution.py:1756
  126.2 5.7 %adam.1 = (f32[1,1]{1,0:T(1,128)}, f32[4,96,192]{2,1,0:T(8,128)}, f32[4,96,192]{2,1,0:T(8,128)}, f32[4,96,192]{2,1,0:T(8,128)}, bf16[4,96,192]{2,1,0:T(8,128)(2,...) custom-call(f32[96,640]{1,0:T(8,128)} %get-tuple-element.36.refs_0_,, ...), custom_call_target="tpu_custom_call" | custom-call | tf_op jit(solution)/shard_map/adam/pallas_call | solution.py:1809

commit v7 on v6

--- a/solution.py
+++ b/solution.py
@@ -518,8 +518,8 @@
         s_lxr=dma((8, 2, nz)),
         s_cs=dma((4, 2, 2)),
         s_cr=dma((4, 2, 2)),
-        s_ys=dma((4, 2, 2)),
-        s_yr=dma((4, 2, 2)),
+        s_ys=dma((4, 2, 4)),
+        s_yr=dma((4, 2, 4)),
         s_as=dma((3, 2, 2)),
         s_ar=dma((3, 2, 2)),
         s_ol=dma((2, 2)),
@@ -949,9 +949,11 @@
             m.ownf[at, :] = product(rows)
 
     def exchange_last(phase, b):
-        for i in range(2):
-            at = slice(i * CHUNK, (i + 1) * CHUNK)
-            core_sent[(phase, b)][i].wait_recv()
+        half = CHUNK // 2
+        for i in range(4):
+            at = slice(i * half, (i + 1) * half)
+            if i % 2 == 0:
+                core_sent[(phase, b)][i // 2].wait_recv()
             m.ys[b, at, :] = (m.ownf[at, :] + m.cr[b, at, :].astype(F32)).astype(BF16)
             cp = remote(
                 m.ys.at[b, at],
@@ -986,7 +988,8 @@
 
     def as_it_lands(phase, b, chunk):
         for i in range(2):
-            y_sent[(phase, b)][i].wait_recv()
+            for cp in y_sent[(phase, b)][2 * i : 2 * i + 2]:
+                cp.wait_recv()
             chunk(i)
 
     def row_mean(values):

time: 132 us -> 133 us (level)
  no operation moved by 1% of the time
where the time goes in v7:
time: 133 us; the launch traced here: 132 us
  Pallas kernels  129 us (97%)
  other arithmetic  2.23 us (2%)
    pallas_call x1, Pallas kernels, fused_body(): pl.pallas_call(partial(layer_kernel, names, (n_dp, owned, qkv_pad, heads,...  124 us
    pallas_call x1, Pallas kernels, fused_body(): pl.pallas_call(partial(adam_kernel, head_cols), out_shape=(*made, like(to...  5.68 us

profile of v7, /device:TPU:0, one launch (start us, length us, event | category | flops | bytes accessed | tf_op | source)
XLA Modules:
  0.0 132.4 jit_solution(5846200391606309063)
XLA Ops:
  0.6 0.7 convert_element_type.11
  1.3 1.5 %add_bitcast_fusion.refs_6_ = f32[320,128]{1,0:T(8,128)} fusion(f32[1023]{0:T(1024)S(1)} %convert_element_type.11, f32[13198]{0:T(1024)} %param.27, f32[13198]{0:T(1024)} %param.26, f32[13198]{0:T(1024)} %param.25), kind=kLoop, calls=%fused_computation | loop fusion | flops 122880 | bytes 326308 | tf_op jit(solution)/shard_map/reshape | solution.py:1751
  2.9 123.6 %layer.1 = (bf16[1024,768]{1,0:T(8,128)(2,1)}, bf16[1024,768]{1,0:T(8,128)(2,1)}, f32[96,640]{1,0:T(8,128)}, f32[96,128]{1,0:T(8,128)}, f32[96,768]{1,0:T(8,128)...) custom-call(bf16[1024,768]{1,0:T(8,128)(2,1)} %refs_0_.1, bf16[1024,768]{1,0:T(8,128)(2,1)} %refs_1_.1, ...), custom_call_target="tpu_custom_call" | custom-call | tf_op jit(solution)/shard_map/layer/pallas_call | solution.py:1759
  126.5 5.7 %adam.1 = (f32[1,1]{1,0:T(1,128)}, f32[4,96,192]{2,1,0:T(8,128)}, f32[4,96,192]{2,1,0:T(8,128)}, f32[4,96,192]{2,1,0:T(8,128)}, bf16[4,96,192]{2,1,0:T(8,128)(2,...) custom-call(f32[96,640]{1,0:T(8,128)} %get-tuple-element.36.refs_0_,, ...), custom_call_target="tpu_custom_call" | custom-call | tf_op jit(solution)/shard_map/adam/pallas_call | solution.py:1812
